TPU v7x, 256 devices: a whole 4x4x8 slice. The times are simulated.
256 devices in a mesh: replica: 8 (over x, y_hi), fsdp: 32 (over y_lo, z, core).
Axes of the slice: x: 4, y: 4 (y_hi: 2, y_lo: 2; y = y_hi * 2 + y_lo), z: 8, core: 2. Of those that a mesh axis runs over, the one named last changes fastest.
Arguments:
- inner: bfloat16 [8, 256, 28672], P('replica', 'fsdp'), may hold values from -6 to 6
- outer: float32 [256, 28672], P('fsdp'), may hold values from -6 to 6
- momentum: float32 [256, 28672], P('fsdp', 'replica'), may hold values from -4 to 4
Outputs:
- outer_new: float32 [256, 28672], P('fsdp')
- momentum_new: float32 [256, 28672], P('fsdp', 'replica')
- gathered: bfloat16 [8, 256, 28672], P('replica')
All inputs are finite; a program needn't handle non-finite values.
Results may differ from a plain program's by a relative error of at most 0.0004.
Values may be sent and summed in bfloat16 or wider, within the bound.
No kernel may reach another device: no remote copies, remote signals or barrier semaphores. Data moves between devices by JAX's collectives and lax.ppermute only.
A program may use at most 128 MiB of HBM per device.

v0:
```python
import jax
import jax.numpy as jnp
from jax import lax
from jax.sharding import PartitionSpec as P


def body(inner, outer, momentum):
    local = inner[0].astype(jnp.float32)
    terms = outer - local
    count = lax.axis_size("replica")
    width = momentum.shape[1]
    offset = lax.axis_index("replica") * width
    total = lax.psum(terms, "replica")
    average = total / count
    moment_all = lax.all_gather(momentum, "replica", axis=1, tiled=True)
    moment_next = 0.9 * moment_all + average
    outer_new = outer - 0.7 * (average + 0.9 * moment_next)
    momentum_new = lax.dynamic_slice_in_dim(moment_next, offset, width, 1)
    blended = (0.5 * local + 0.5 * outer_new).astype(jnp.bfloat16)
    gathered = lax.all_gather(blended, "fsdp", axis=0, tiled=True)
    return (outer_new, momentum_new, gathered[None])


def solution(mesh):
    placed = (P("replica", "fsdp", None), P("fsdp", None), P("fsdp", "replica"))
    return jax.shard_map(
        body,
        mesh=mesh,
        in_specs=placed,
        out_specs=(P("fsdp", None), P("fsdp", "replica"), P("replica", None, None)),
        check_vma=False,
    )
```

profile of v0, /device:TPU:1, one launch (start us, length us, event | category | flops | bytes accessed | tf_op | source)
XLA Modules:
  0.0 223.0 jit_solution(8468531507418328228)
XLA Ops:
  7.2 0.0 all-reduce.2.cloned.1.call-start
  7.2 2.3 %convert_subtract_fusion = f32[8,28672]{1,0:T(8,128)} fusion(f32[8,28672]{1,0:T(8,128)} %param.4, bf16[1,8,28672]{2,1,0:T(8,128)(2,1)} %param.3), kind=kLoop, calls=%fused_computation.1 | loop fusion | flops 458752 | bytes 2293760 | tf_op jit(solution)/shard_map/sub | solution.py:9
  9.5 0.0 all-reduce.2.cloned.1.call-update
  9.5 0.0 all-gather.2.cloned.1.call-start
  9.6 36.9 %all_gather.6 = f32[8,28672]{1,0:T(8,128)S(1)} all-gather(f32[8,3584]{1,0:T(8,128)} %param.5), channel_id=1, replica_groups=mesh['replica'=8,'fsdp'=32] {'replica'}, dimensions={1}, use_global_device_ids=true | all-gather | bytes 1032192 | tf_op jit(solution)/shard_map/all_gather | solution.py:15
  46.5 60.6 %all-reduce.2.cloned.1.call-done = f32[8,28672]{1,0:T(8,128)} async-done(((f32[8,28672]{1,0:T(8,128)}), f32[8,28672]{1,0:T(8,128)}) %all-reduce.2.cloned.1.call-update) | async-done | bytes 917520 | tf_op jit(solution)/shard_map/psum | solution.py:13
  107.2 3.0 %fusion.1 = (bf16[8,28672]{1,0:T(8,128)(2,1)}, f32[8,28672]{1,0:T(8,128)}, f32[8,28672]{1,0:T(8,128)S(1)}) fusion(bf16[1,8,28672]{2,1,0:T(8,128)(2,1)} %param.3, f32[8,28672]{1,0:T(8,128)} %param.4, f32[8,28672]{1,0:T(8,128)S(1)} %all_gather.6, f32[8,28672]{1,0:T(8,128)} %all-reduce.2.cloned.1.call-done), kind=kLoop, calls=%fused_computation.3 | loop fusion | flops 2523136 | bytes 5505024 | tf_op jit(solution)/shard_map/convert_element_type | solution.py:19
  110.1 0.0 all-gather.2.cloned.1.call-update
  110.2 0.7 constant_dynamic-slice_fusion
  110.8 92.0 %all-gather.2.cloned.1.call-done = bf16[256,28672]{1,0:T(8,128)(2,1)} async-done(((bf16[8,28672]{1,0:T(8,128)(2,1)}), bf16[256,28672]{1,0:T(8,128)(2,1)}) %all-gather.2.cloned.1.call-update) | async-done | bytes 14680080 | tf_op jit(solution)/shard_map/all_gather | solution.py:20
  202.8 13.4 %copy.8 = bf16[1,256,28672]{2,1,0:T(8,128)(2,1)} copy(bf16[1,256,28672]{2,1,0:T(8,128)(2,1)} %bitcast.5) | data formatting | bytes 29360128
Async XLA Ops:
  7.2 100.0 %all-reduce.2.cloned.1.call-start = ((), (), s32[]{:S(2)}) async-start(), calls=%async_computation | async-start | bytes 1835008 | tf_op jit(solution)/shard_map/psum | solution.py:13
  9.5 193.3 %all-gather.2.cloned.1.call-start = ((), (), s32[]{:S(2)}) async-start(), calls=%async_computation.1 | async-start | bytes 15138816 | tf_op jit(solution)/shard_map/all_gather | solution.py:20
Sparse Core Ops, SparseCore 0:
  11.2 95.8 all-reduce.1
  110.3 92.5 all-gather.1
where the time goes:
time: 223 us
  waiting for transfers between devices  153 us (69%)
  blocking collectives  36.9 us (17%)
  local copies, waits for them, and re-layouts  14 us (6%)
  between operations  14 us (6%)
  other arithmetic  5.27 us (2%)
    all_gather x1, waiting for transfers between devices, body(): gathered = lax.all_gather(blended, 'fsdp', axis=0, tiled=True)  92 us
    psum x1, waiting for transfers between devices, body(): total = lax.psum(terms, 'replica')  60.6 us
    all_gather x1, blocking collectives, body(): moment_all = lax.all_gather(momentum, 'replica', axis=1, tiled=True)  36.9 us
    unnamed x1, local copies, waits for them, and re-layouts  13.4 us
  transfers between devices with their start and end apart: 2, of which 2 were waited for; matrix products, arithmetic and copies ran while one was open for 0% of the time, Pallas kernels for 0%

commit v1 on v0

v1 whole, which is shorter than its diff:
```python
import jax
import jax.numpy as jnp
from jax import lax
from jax.experimental import pallas as pl
from jax.experimental.pallas import tpu as pltpu
from jax.sharding import PartitionSpec as P

REPLICAS = 8
RUNS, SLOTS, CORES = 2, 8, 2
TILE = (8, 128)
SPLIT = 13


def coords(index):
    return index // (SLOTS * CORES), index // CORES % SLOTS, index % CORES


def fsdp_index(run, slot, core):
    return (run % RUNS * SLOTS + slot % SLOTS) * CORES + core % CORES


def move(array, target):
    return lax.ppermute(array, "fsdp", [(i, fsdp_index(*target(*coords(i)))) for i in range(RUNS * SLOTS * CORES)])


def swap_run(array):
    return move(array, lambda run, slot, core: (run + 1, slot, core))


def swap_core(array):
    return move(array, lambda run, slot, core: (run, slot, core + 1))


def along_slots(array):
    return move(array, lambda run, slot, core: (run, slot + (1 if core == 0 else -1), core))


def swap_replica(array, bits):
    return lax.ppermute(array, "replica", [(i, i ^ bits) for i in range(REPLICAS)])


def by_xor(array, index):
    count = array.shape[0]
    levels = count.bit_length() - 1
    rest = array.shape[1:]
    array = array.reshape((2,) * levels + rest)
    for level in range(levels):
        bit = (index >> (levels - 1 - level)) & 1
        array = jnp.where(bit == 1, jnp.flip(array, level), array)
    return array.reshape((count,) + rest)


def place(out, groups, shape, carried=None):
    arrays = [array for array, *_ in groups]
    through = ([] if out is None else [out]) + ([] if carried is None else [carried])
    blocks = [
        (at, lead, where, first, tiles)
        for at, (_, targets, first, tiles) in enumerate(groups)
        for lead, where in enumerate(targets)
    ]

    def kernel(*refs):
        held, result, sems = refs[: len(arrays)], refs[len(arrays) + len(through)], refs[-1]
        own_run, own_slot, own_core = coords(lax.axis_index("fsdp"))
        copies = []
        for number, (at, lead, (run, hops, core, came), first, tiles) in enumerate(blocks):
            receiver = (own_core + came) % CORES
            block = fsdp_index(own_run + run, own_slot + (2 * receiver - 1) * hops, receiver + core)
            copies.append(
                pltpu.make_async_copy(held[at].at[lead], result.at[block, :, pl.ds(first, tiles)], sems.at[number])
            )
        for copy in copies:
            copy.start()
        for copy in copies:
            copy.wait()

    anywhere = pl.BlockSpec(memory_space=pl.ANY)
    moved = sum(array.size * array.dtype.itemsize for array in arrays)
    results = [jax.ShapeDtypeStruct(shape, jnp.bfloat16)]
    results += [] if carried is None else [jax.ShapeDtypeStruct(carried.shape, carried.dtype)]
    aliases = {len(arrays) + at: at + (out is None) for at in range(len(through))}
    done = pl.pallas_call(
        kernel,
        out_shape=results,
        in_specs=[pl.BlockSpec(memory_space=pltpu.VMEM)] * len(arrays) + [anywhere] * len(through),
        out_specs=[anywhere] * len(results),
        scratch_shapes=[pltpu.SemaphoreType.DMA((len(blocks),))],
        input_output_aliases=aliases,
        compiler_params=pltpu.CompilerParams(vmem_limit_bytes=moved + (1 << 20)),
        cost_estimate=pl.CostEstimate(flops=0, bytes_accessed=2 * moved, transcendentals=0),
    )(*arrays, *through)
    return done[0] if carried is None else done


def step(inner, outer, momentum):
    terms = lax.all_to_all(inner, "replica", 0, 0).astype(jnp.float32)
    average = outer - jnp.sum(terms, axis=0) / REPLICAS
    momentum_new = 0.9 * momentum + average
    outer_new = outer - 0.7 * (average + 0.9 * momentum_new)
    blended = (0.5 * terms + 0.5 * outer_new).astype(jnp.bfloat16)
    return outer_new, momentum_new, lax.all_to_all(blended, "replica", 0, 0)


def gather(split, joined, shape):
    (alone, first_a), (both, first_b) = split, joined
    count_a, count_b = alone.shape[1], both.shape[1]

    def blocks_a(array, hops, came, run=0):
        targets = [(run, hop, core, came) for hop, kinds in hops for core in range(kinds)]
        return array, targets, first_a, count_a

    def blocks_b(array, hops, came):
        targets = [(at % RUNS, hops, at // RUNS, came) for at in range(array.shape[0])]
        return array, targets, first_b, count_b

    alone, both = alone[None], both[None]
    beside = swap_run(both)
    pair = jnp.concatenate([alone, swap_core(alone)])
    y0 = swap_run(alone)
    quad = jnp.concatenate([both, beside])
    quad = jnp.concatenate([quad, swap_core(quad)])
    a, b = along_slots(pair), along_slots(quad)
    cy = swap_core(y0)
    ready = [blocks_a(pair, [(0, 2)], 0), blocks_b(quad, 0, 0)]
    later = [blocks_a(y0, [(0, 1)], 0, 1), blocks_a(cy, [(0, 1)], 1, 1)]
    out = None
    for hops in range(1, SLOTS // 2 + 1):
        kinds = 2 if hops < SLOTS // 2 - 1 else 1
        last = hops == SLOTS // 2
        out, a = place(out, ready, shape, a)
        next_a = None if last else along_slots(a[:kinds])
        held = [(hops, a.shape[0])]
        y, ca = swap_run(a), swap_core(a)
        cy = swap_core(y)
        ready = later + [blocks_a(a, held, 0)]
        later = [blocks_a(y, held, 0, 1), blocks_a(cy, held, 1, 1), blocks_a(ca, held, 1)]
        out, b = place(out, ready, shape, b)
        next_b = None if last else along_slots(b[: RUNS * kinds])
        cb = swap_core(b)
        ready = [blocks_b(b, hops, 0)]
        later += [blocks_b(cb, hops, 1)]
        a, b = next_a, next_b
    return place(out, ready + later, shape)


def body(inner, outer, momentum):
    width = momentum.shape[1] // TILE[1]
    replica = lax.axis_index("replica")

    def tiles(array):
        array = array.reshape(TILE[0], -1, width, TILE[1])
        return array.transpose(1, 2, 0, 3)

    def rows(array):
        return array.transpose(2, 0, 1, 3).reshape(TILE[0], -1)

    inner, outer, momentum = tiles(inner[0]), tiles(outer), tiles(momentum)[0]
    own_outer = lax.dynamic_index_in_dim(outer, replica, 0, keepdims=False)
    shape = (RUNS * SLOTS * CORES, REPLICAS, width) + TILE

    outer_new, momentum_new, blended = step(inner, own_outer, momentum)
    out = gather((blended[:, :SPLIT], 0), (blended[:, SPLIT:], SPLIT), shape)

    pair = by_xor(jnp.stack([outer_new, swap_replica(outer_new, 1)]), replica & 1)
    four = jnp.stack([pair] + [swap_replica(pair, 2 * bits) for bits in range(1, 4)])
    outer_all = by_xor(four, replica >> 1).reshape((REPLICAS,) + outer_new.shape)

    gathered = out.transpose(0, 3, 1, 2, 4).reshape(1, -1, REPLICAS * width * TILE[1])
    return rows(outer_all), rows(momentum_new[None]), gathered


def solution(mesh):
    placed = (P("replica", "fsdp", None), P("fsdp", None), P("fsdp", "replica"))
    return jax.shard_map(
        body,
        mesh=mesh,
        in_specs=placed,
        out_specs=(P("fsdp", None), P("fsdp", "replica"), P("replica", None, None)),
        check_vma=False,
    )
```

time: 223 us -> 152 us (0.68)
  waiting for transfers between devices: 153 us -> 69.1 us
  starting transfers between devices: 0.08 us -> 46.2 us
  blocking collectives: 36.9 us -> 12.4 us
  Pallas kernels: 0 us -> 13.7 us
  between operations: 14 us -> 1.03 us
  local copies, waits for them, and re-layouts: 14 us -> 1.52 us
    all_gather x1 -> x0, waiting for transfers between devices: 92 us -> none  [body(): gathered = lax.all_gather(blended, 'fsdp', axis=0, tiled=True)]
    psum x1 -> x0, waiting for transfers between devices: 60.6 us -> none  [body(): total = lax.psum(terms, 'replica')]
    ppermute x0 -> x33, waiting for transfers between devices: none -> 59.5 us  [the longest x29 52.9 us: move(): lax.ppermute(array, 'fsdp', [(i, fsdp_index(*target(*coords(i)))) for i i...]
    ppermute x0 -> x33, starting transfers between devices: none -> 38.7 us  [the longest x29 34 us: move(): lax.ppermute(array, 'fsdp', [(i, fsdp_index(*target(*coords(i)))) for i i...]
    all_gather x1 -> x0, blocking collectives: 36.9 us -> none  [body(): moment_all = lax.all_gather(momentum, 'replica', axis=1, tiled=True)]
    pallas_call x0 -> x9, Pallas kernels: none -> 13.7 us  [place(): pl.pallas_call(kernel, out_shape=results, in_specs=[pl.BlockSpec(memory_s...]
    unnamed x1 -> x6, local copies, waits for them, and re-layouts: 13.4 us -> 0.65 us
    all_to_all x0 -> x1, blocking collectives: none -> 12.4 us  [step(): return (outer_new, momentum_new, lax.all_to_all(blended, 'replica', 0, 0))]
  transfers between devices with their start and end apart: 2 -> 34, of which waited for: 2 -> 15; matrix products, arithmetic and copies ran while one was open for 0% -> 4% of each run, Pallas kernels for 0% -> 7%
where the time goes in v1:
time: 152 us; the launch traced here: 151 us
  waiting for transfers between devices  69.1 us (45%)
  starting transfers between devices  46.2 us (30%)
  Pallas kernels  13.7 us (9%)
  blocking collectives  12.4 us (8%)
  other arithmetic  7.43 us (5%)
  local copies, waits for them, and re-layouts  1.52 us (1%)
    ppermute x29, waiting for transfers between devices, move(): lax.ppermute(array, 'fsdp', [(i, fsdp_index(*target(*coords(i)))) for i i...  52.9 us
    ppermute x29, starting transfers between devices, move(): lax.ppermute(array, 'fsdp', [(i, fsdp_index(*target(*coords(i)))) for i i...  34 us
    pallas_call x9, Pallas kernels, place(): pl.pallas_call(kernel, out_shape=results, in_specs=[pl.BlockSpec(memory_s...  13.7 us
    all_to_all x1, blocking collectives, step(): return (outer_new, momentum_new, lax.all_to_all(blended, 'replica', 0, 0))  12.4 us
    all_to_all x1, waiting for transfers between devices, step(): terms = lax.all_to_all(inner, 'replica', 0, 0).astype(jnp.float32)  9.63 us
    all_to_all x1, starting transfers between devices, step(): terms = lax.all_to_all(inner, 'replica', 0, 0).astype(jnp.float32)  7.49 us
    ppermute x4, waiting for transfers between devices, swap_replica(): lax.ppermute(array, 'replica', [(i, i ^ bits) for i in range(REPLICAS)])  6.62 us
    ppermute x4, starting transfers between devices, swap_replica(): lax.ppermute(array, 'replica', [(i, i ^ bits) for i in range(REPLICAS)])  4.7 us
  transfers between devices with their start and end apart: 34, of which 15 were waited for; matrix products, arithmetic and copies ran while one was open for 4% of the time, Pallas kernels for 7%

profile of v1, /device:TPU:1, one launch (start us, length us, event | category | flops | bytes accessed | tf_op | source)
XLA Modules:
  0.0 151.5 jit_solution(1944584480374042775)
XLA Ops:
  0.6 7.5 %all-to-all-start = ((bf16[8,28,8,128]{3,2,1,0:T(8,128)(2,1)}), bf16[8,28,8,128]{3,2,1,0:T(8,128)(2,1)S(1)}, u32[]{:S(2)}, u32[]{:S(2)}) async-start(bf16[8,28,8,128]{3,2,1,0:T(8,128)(2,1)} %bitcast.81), calls=%async_computation | async-start | bytes 917504 | tf_op jit(solution)/shard_map/all_to_all | solution.py:96
  8.1 9.6 %all-to-all-done = bf16[8,28,8,128]{3,2,1,0:T(8,128)(2,1)S(1)} async-done(((bf16[8,28,8,128]{3,2,1,0:T(8,128)(2,1)}), bf16[8,28,8,128]{3,2,1,0:T(8,128)(2,1)S(1)}, u32[]{:S(2)}, u32[]{:S(2)}) %all-to-all-start) | async-done | bytes 458784 | tf_op jit(solution)/shard_map/all_to_all | solution.py:96
  17.8 1.6 %multiply_bitcast_fusion = (f32[28,8,128]{2,1,0:T(8,128)S(1)}, f32[1,28,8,128]{3,2,1,0:T(8,128)S(1)}, f32[8,3584]{1,0:T(8,128)}) fusion(f32[8,3584]{1,0:T(8,128)} %param.5, f32[28,8,128]{2,1,0:T(8,128)S(1)} %convert_reduce_fusion, f32[8,8,28,128]{3,0,2,1:T(8,128)} %bitcast.85, s32[]{:T(128)S(6)} %select_n.29), kind=kLoop, calls=%fused_computation.23 | loop fusion | flops 258048 | bytes 688132 | tf_op jit(solution)/shard_map/add | solution.py:100
  19.6 12.4 %all_to_all.10 = bf16[8,28,8,128]{3,2,1,0:T(8,128)(2,1)S(1)} all-to-all(bf16[8,28,8,128]{3,2,1,0:T(8,128)(2,1)S(1)} %fusion.1), channel_id=1, replica_groups=mesh['replica'=8,'fsdp'=32] {'replica'}, dimensions={0} | all-to-all | bytes 917504 | tf_op jit(solution)/shard_map/all_to_all | solution.py:101
  32.5 4.6 %collective-permute-done.5 = bf16[1,8,15,8,128]{4,3,2,1,0:T(8,128)(2,1)S(1)} collective-permute-done((bf16[1,8,15,8,128]{4,3,2,1,0:T(8,128)(2,1)S(1)}, bf16[1,8,15,8,128]{4,3,2,1,0:T(8,128)(2,1)S(1)}, u32[]{:S(2)}, u32[]{:S(2)}) %collective-permute-start.5) | collective-permute-done | bytes 245792 | tf_op jit(solution)/shard_map/ppermute | solution.py:23
  37.2 3.8 %collective-permute-start.6 = (bf16[2,8,15,8,128]{4,3,2,1,0:T(8,128)(2,1)S(1)}, bf16[2,8,15,8,128]{4,3,2,1,0:T(8,128)(2,1)S(1)}, u32[]{:S(2)}, u32[]{:S(2)}) collective-permute-start(bf16[2,8,15,8,128]{4,3,2,1,0:T(8,128)(2,1)S(1)} %pad_maximum_fusion.2), channel_id=1, source_target_pairs={{0,1},{1,0},{2,3},{3,2},{4,5},{5,4},{6,7},{7,6},{8,9},{9,8},{10,11... | collective-permute-start | bytes 1474568 | tf_op jit(solution)/shard_map/ppermute | solution.py:23
  41.0 1.5 collective-permute-done.6
  42.6 5.7 %collective-permute-start.13 = (bf16[4,8,15,8,128]{4,3,2,1,0:T(8,128)(2,1)S(1)}, bf16[4,8,15,8,128]{4,3,2,1,0:T(8,128)(2,1)S(1)}, u32[]{:S(2)}, u32[]{:S(2)}) collective-permute-start(bf16[4,8,15,8,128]{4,3,2,1,0:T(8,128)(2,1)S(1)} %pad_maximum_fusion.refs_1_), channel_id=1, source_target_pairs={{0,2},{1,15},{2,4},{3,1},{4,6},{5,3},{6,8},{7,5},{8,10},{9,7},{10,... | collective-permute-start | bytes 2949128 | tf_op jit(solution)/shard_map/ppermute | solution.py:23
  48.3 1.5 collective-permute-done.4
  49.8 0.8 collective-permute-start.7
  51.0 6.8 %collective-permute-done.11.refs_0_ = bf16[1,8,13,8,128]{4,3,2,1,0:T(8,128)(2,1)S(1)} collective-permute-done((bf16[1,8,13,8,128]{4,3,2,1,0:T(8,128)(2,1)S(1)}, bf16[1,8,13,8,128]{4,3,2,1,0:T(8,128)(2,1)S(1)}, u32[]{:S(2)}, u32[]{:S(2)}) %collective-permute-start.11) | collective-permute-done | bytes 213024 | tf_op jit(solution)/shard_map/ppermute | solution.py:23
  58.2 5.6 %collective-permute-done.7.refs_2_ = bf16[2,8,13,8,128]{4,3,2,1,0:T(8,128)(2,1)S(1)} collective-permute-done((bf16[2,8,13,8,128]{4,3,2,1,0:T(8,128)(2,1)S(1)}, bf16[2,8,13,8,128]{4,3,2,1,0:T(8,128)(2,1)S(1)}, u32[]{:S(2)}, u32[]{:S(2)}) %collective-permute-start.7) | collective-permute-done | bytes 426016 | tf_op jit(solution)/shard_map/ppermute | solution.py:23
  63.8 1.1 shard_map.58
  65.0 1.0 shard_map.59
  66.0 1.8 %collective-permute-start.14 = (bf16[4,8,15,8,128]{4,3,2,1,0:T(8,128)(2,1)S(1)}, bf16[4,8,15,8,128]{4,3,2,1,0:T(8,128)(2,1)S(1)}, u32[]{:S(2)}, u32[]{:S(2)}) collective-permute-start(bf16[4,8,15,8,128]{4,3,2,1,0:T(8,128)(2,1)S(1)} %get-tuple-element.21.refs_0_), channel_id=1, source_target_pairs={{0,1},{1,0},{2,3},{3,2},{4,5},{5,4},{6,7},{7,6},{8,9},{9,8},{10,11... | collective-permute-start | bytes 2949128 | tf_op jit(solution)/shard_map/ppermute | solution.py:23
  67.7 1.7 %collective-permute-start.16 = (bf16[4,8,15,8,128]{4,3,2,1,0:T(8,128)(2,1)S(1)}, bf16[4,8,15,8,128]{4,3,2,1,0:T(8,128)(2,1)S(1)}, u32[]{:S(2)}, u32[]{:S(2)}) collective-permute-start(bf16[4,8,15,8,128]{4,3,2,1,0:T(8,128)(2,1)S(1)} %get-tuple-element.21.refs_0_), channel_id=1, source_target_pairs={{0,2},{1,15},{2,4},{3,1},{4,6},{5,3},{6,8},{7,5},{8,10},{9,7},{10,... | collective-permute-start | bytes 2949128 | tf_op jit(solution)/shard_map/ppermute | solution.py:23
  69.9 0.7 collective-permute-start.15
  70.6 9.6 %collective-permute-done.8.refs_0_ = bf16[2,8,13,8,128]{4,3,2,1,0:T(8,128)(2,1)S(1)} collective-permute-done((bf16[2,8,13,8,128]{4,3,2,1,0:T(8,128)(2,1)S(1)}, bf16[2,8,13,8,128]{4,3,2,1,0:T(8,128)(2,1)S(1)}, u32[]{:S(2)}, u32[]{:S(2)}) %collective-permute-start.8) | collective-permute-done | bytes 426016 | tf_op jit(solution)/shard_map/ppermute | solution.py:23
  80.2 5.3 %collective-permute-done.15.refs_2_ = bf16[2,8,13,8,128]{4,3,2,1,0:T(8,128)(2,1)S(1)} collective-permute-done((bf16[2,8,13,8,128]{4,3,2,1,0:T(8,128)(2,1)S(1)}, bf16[2,8,13,8,128]{4,3,2,1,0:T(8,128)(2,1)S(1)}, u32[]{:S(2)}, u32[]{:S(2)}) %collective-permute-start.15) | collective-permute-done | bytes 426016 | tf_op jit(solution)/shard_map/ppermute | solution.py:23
  85.5 1.0 shard_map.60
  86.6 1.6 %shard_map.61 = (bf16[32,8,28,8,128]{4,3,2,1,0:T(8,128)(2,1)}, bf16[4,8,15,8,128]{4,3,2,1,0:T(8,128)(2,1)S(1)}) custom-call(bf16[2,8,13,8,128]{4,3,2,1,0:T(8,128)(2,1)S(1)} %collective-permute-done.8.refs_0_, bf16[2,8,13,8,128]{4,3,2,1,0:T(8,128)(2,1)S(1)} %collective-permute-done.9.refs_1_, ...), custom_call_target="tpu_custom_call", output_to_operand_aliasing={{0}: (5, {}), {1}: (6, {})} | custom-call | bytes 5373952 | tf_op jit(solution)/shard_map/pallas_call | solution.py:82
  88.2 2.2 %collective-permute-start.24 = (bf16[4,8,15,8,128]{4,3,2,1,0:T(8,128)(2,1)S(1)}, bf16[4,8,15,8,128]{4,3,2,1,0:T(8,128)(2,1)}, u32[]{:S(2)}, u32[]{:S(2)}) collective-permute-start(bf16[4,8,15,8,128]{4,3,2,1,0:T(8,128)(2,1)S(1)} %get-tuple-element.25.refs_0_), channel_id=1, source_target_pairs={{0,1},{1,0},{2,3},{3,2},{4,5},{5,4},{6,7},{7,6},{8,9},{9,8},{10,11... | collective-permute-start | bytes 2949128 | tf_op jit(solution)/shard_map/ppermute | solution.py:23
  92.1 10.8 %collective-permute-done.21.refs_0_ = bf16[2,8,13,8,128]{4,3,2,1,0:T(8,128)(2,1)S(1)} collective-permute-done((bf16[2,8,13,8,128]{4,3,2,1,0:T(8,128)(2,1)S(1)}, bf16[2,8,13,8,128]{4,3,2,1,0:T(8,128)(2,1)S(1)}, u32[]{:S(2)}, u32[]{:S(2)}) %collective-permute-start.21) | collective-permute-done | bytes 426016 | tf_op jit(solution)/shard_map/ppermute | solution.py:23
  103.3 1.6 %fusion.5 = f32[28,8,128]{2,1,0:T(8,128)} fusion(f32[8,3584]{1,0:T(8,128)S(1)} %copy-done, f32[28,8,128]{2,1,0:T(8,128)S(1)} %convert_reduce_fusion, f32[8,8,28,128]{3,0,2,1:T(8,128)} %bitcast.86, s32[]{:T(128)S(6)} %select_n.29), kind=kLoop, calls=%fused_computation.18 | loop fusion | flops 229376 | bytes 458756 | tf_op jit(solution)/shard_map/sub | solution.py:99
  104.9 3.4 %collective-permute-done.17.refs_2_ = bf16[2,8,13,8,128]{4,3,2,1,0:T(8,128)(2,1)S(1)} collective-permute-done((bf16[2,8,13,8,128]{4,3,2,1,0:T(8,128)(2,1)S(1)}, bf16[2,8,13,8,128]{4,3,2,1,0:T(8,128)(2,1)S(1)}, u32[]{:S(2)}, u32[]{:S(2)}) %collective-permute-start.17) | collective-permute-done | bytes 426016 | tf_op jit(solution)/shard_map/ppermute | solution.py:23
  108.3 0.8 collective-permute-start
  109.1 1.0 shard_map.62
  110.1 3.1 %shard_map.63 = (bf16[32,8,28,8,128]{4,3,2,1,0:T(8,128)(2,1)}, bf16[4,8,15,8,128]{4,3,2,1,0:T(8,128)(2,1)S(1)}) custom-call(bf16[2,8,13,8,128]{4,3,2,1,0:T(8,128)(2,1)S(1)} %collective-permute-done.21.refs_0_, bf16[2,8,13,8,128]{4,3,2,1,0:T(8,128)(2,1)} %collective-permute-done.22.refs_1_, ...), custom_call_target="tpu_custom_call", output_to_operand_aliasing={{0}: (5, {}), {1}: (6, {})} | custom-call | bytes 5373952 | tf_op jit(solution)/shard_map/pallas_call | solution.py:82
  113.2 2.5 %collective-permute-start.26 = (bf16[4,8,15,8,128]{4,3,2,1,0:T(8,128)(2,1)S(1)}, bf16[4,8,15,8,128]{4,3,2,1,0:T(8,128)(2,1)S(1)}, u32[]{:S(2)}, u32[]{:S(2)}) collective-permute-start(bf16[4,8,15,8,128]{4,3,2,1,0:T(8,128)(2,1)S(1)} %get-tuple-element.29.refs_0_), channel_id=1, source_target_pairs={{0,1},{1,0},{2,3},{3,2},{4,5},{5,4},{6,7},{7,6},{8,9},{9,8},{10,11... | collective-permute-start | bytes 2949128 | tf_op jit(solution)/shard_map/ppermute | solution.py:23
  115.7 0.6 copy-done.2
  116.4 0.9 pad_maximum_fusion.4
  117.8 0.7 reverse_select_fusion.2
  118.8 1.8 %collective-permute-start.2 = (f32[2,28,8,128]{3,2,1,0:T(8,128)}, f32[2,28,8,128]{3,2,1,0:T(8,128)S(1)}, u32[]{:S(2)}, u32[]{:S(2)}) collective-permute-start(f32[2,28,8,128]{3,2,1,0:T(8,128)} %reverse_select_fusion.2), channel_id=1, source_target_pairs={{0,128},{32,160},{64,192},{96,224},{128,0},{160,32},{192,64},{224,... | collective-permute-start | bytes 688136 | tf_op jit(solution)/shard_map/ppermute | solution.py:39
  120.6 1.8 %collective-permute-start.3 = (f32[2,28,8,128]{3,2,1,0:T(8,128)}, f32[2,28,8,128]{3,2,1,0:T(8,128)}, u32[]{:S(2)}, u32[]{:S(2)}) collective-permute-start(f32[2,28,8,128]{3,2,1,0:T(8,128)} %reverse_select_fusion.2), channel_id=1, source_target_pairs={{0,192},{32,224},{64,128},{96,160},{128,64},{160,96},{192,0},{224,... | collective-permute-start | bytes 688136 | tf_op jit(solution)/shard_map/ppermute | solution.py:39
  122.4 0.8 slice.15
  123.2 1.3 collective-permute-done.1
  124.7 5.2 %collective-permute-done.2 = f32[2,28,8,128]{3,2,1,0:T(8,128)S(1)} collective-permute-done((f32[2,28,8,128]{3,2,1,0:T(8,128)}, f32[2,28,8,128]{3,2,1,0:T(8,128)S(1)}, u32[]{:S(2)}, u32[]{:S(2)}) %collective-permute-start.2) | collective-permute-done | bytes 229408 | tf_op jit(solution)/shard_map/ppermute | solution.py:39
  129.9 2.4 %collective-permute-start.20 = (bf16[2,8,13,8,128]{4,3,2,1,0:T(8,128)(2,1)S(1)}, bf16[2,8,13,8,128]{4,3,2,1,0:T(8,128)(2,1)}, u32[]{:S(2)}, u32[]{:S(2)}) collective-permute-start(bf16[2,8,13,8,128]{4,3,2,1,0:T(8,128)(2,1)S(1)} %get-tuple-element.27.refs_4_), channel_id=1, source_target_pairs={{0,1},{1,0},{2,3},{3,2},{4,5},{5,4},{6,7},{7,6},{8,9},{9,8},{10,11... | collective-permute-start | bytes 1277960 | tf_op jit(solution)/shard_map/ppermute | solution.py:23
  132.4 0.7 collective-permute-start.19
  133.4 1.1 pad_maximum_fusion.1
  134.5 3.7 %collective-permute-done.27.refs_2_ = bf16[1,8,13,8,128]{4,3,2,1,0:T(8,128)(2,1)S(1)} collective-permute-done((bf16[1,8,13,8,128]{4,3,2,1,0:T(8,128)(2,1)S(1)}, bf16[1,8,13,8,128]{4,3,2,1,0:T(8,128)(2,1)S(1)}, u32[]{:S(2)}, u32[]{:S(2)}) %collective-permute-start.27) | collective-permute-done | bytes 213024 | tf_op jit(solution)/shard_map/ppermute | solution.py:23
  138.2 1.0 shard_map.64
  139.2 1.2 collective-permute-start.29
  140.3 2.8 %shard_map.65 = (bf16[32,8,28,8,128]{4,3,2,1,0:T(8,128)(2,1)}, bf16[2,8,15,8,128]{4,3,2,1,0:T(8,128)(2,1)S(1)}) custom-call(bf16[2,8,13,8,128]{4,3,2,1,0:T(8,128)(2,1)} %collective-permute-done.18.refs_0_, bf16[2,8,13,8,128]{4,3,2,1,0:T(8,128)(2,1)} %collective-permute-done.19.refs_1_, ...), custom_call_target="tpu_custom_call", output_to_operand_aliasing={{0}: (5, {}), {1}: (6, {})} | custom-call | bytes 4947968 | tf_op jit(solution)/shard_map/pallas_call | solution.py:82
  143.1 4.3 %collective-permute-start.32 = (bf16[2,8,15,8,128]{4,3,2,1,0:T(8,128)(2,1)S(1)}, bf16[2,8,15,8,128]{4,3,2,1,0:T(8,128)(2,1)S(1)}, u32[]{:S(2)}, u32[]{:S(2)}) collective-permute-start(bf16[2,8,15,8,128]{4,3,2,1,0:T(8,128)(2,1)S(1)} %get-tuple-element.33.refs_0_), channel_id=1, source_target_pairs={{0,1},{1,0},{2,3},{3,2},{4,5},{5,4},{6,7},{7,6},{8,9},{9,8},{10,11... | collective-permute-start | bytes 1474568 | tf_op jit(solution)/shard_map/ppermute | solution.py:23
  147.6 1.4 collective-permute-start.30
  149.0 1.0 reverse_select_fusion
  150.1 1.2 shard_map.66
  (53 shorter events, 6.0 us)
Async XLA Ops:
  0.6 17.1 %all-to-all-start = ((bf16[8,28,8,128]{3,2,1,0:T(8,128)(2,1)}), bf16[8,28,8,128]{3,2,1,0:T(8,128)(2,1)S(1)}, u32[]{:S(2)}, u32[]{:S(2)}) async-start(bf16[8,28,8,128]{3,2,1,0:T(8,128)(2,1)} %bitcast.81), calls=%async_computation | async-start | bytes 917504 | tf_op jit(solution)/shard_map/all_to_all | solution.py:96
  32.0 5.1 %collective-permute-start.5 = (bf16[1,8,15,8,128]{4,3,2,1,0:T(8,128)(2,1)S(1)}, bf16[1,8,15,8,128]{4,3,2,1,0:T(8,128)(2,1)S(1)}, u32[]{:S(2)}, u32[]{:S(2)}) collective-permute-start(bf16[1,8,15,8,128]{4,3,2,1,0:T(8,128)(2,1)S(1)} %slice_bitcast_fusion), channel_id=1, source_target_pairs={{0,16},{1,17},{2,18},{3,19},{4,20},{5,21},{6,22},{7,23},{8,24},{9,... | collective-permute-start | bytes 737288 | tf_op jit(solution)/shard_map/ppermute | solution.py:23
  37.2 5.3 %collective-permute-start.6 = (bf16[2,8,15,8,128]{4,3,2,1,0:T(8,128)(2,1)S(1)}, bf16[2,8,15,8,128]{4,3,2,1,0:T(8,128)(2,1)S(1)}, u32[]{:S(2)}, u32[]{:S(2)}) collective-permute-start(bf16[2,8,15,8,128]{4,3,2,1,0:T(8,128)(2,1)S(1)} %pad_maximum_fusion.2), channel_id=1, source_target_pairs={{0,1},{1,0},{2,3},{3,2},{4,5},{5,4},{6,7},{7,6},{8,9},{9,8},{10,11... | collective-permute-start | bytes 1474568 | tf_op jit(solution)/shard_map/ppermute | solution.py:23
  42.6 22.4 %collective-permute-start.13 = (bf16[4,8,15,8,128]{4,3,2,1,0:T(8,128)(2,1)S(1)}, bf16[4,8,15,8,128]{4,3,2,1,0:T(8,128)(2,1)S(1)}, u32[]{:S(2)}, u32[]{:S(2)}) collective-permute-start(bf16[4,8,15,8,128]{4,3,2,1,0:T(8,128)(2,1)S(1)} %pad_maximum_fusion.refs_1_), channel_id=1, source_target_pairs={{0,2},{1,15},{2,4},{3,1},{4,6},{5,3},{6,8},{7,5},{8,10},{9,7},{10,... | collective-permute-start | bytes 2949128 | tf_op jit(solution)/shard_map/ppermute | solution.py:23
  48.2 1.6 %collective-permute-start.4 = (bf16[1,8,13,8,128]{4,3,2,1,0:T(8,128)(2,1)S(1)}, bf16[1,8,13,8,128]{4,3,2,1,0:T(8,128)(2,1)S(1)}, u32[]{:S(2)}, u32[]{:S(2)}) collective-permute-start(bf16[1,8,13,8,128]{4,3,2,1,0:T(8,128)(2,1)S(1)} %slice_bitcast_fusion.1), channel_id=1, source_target_pairs={{0,1},{1,0},{2,3},{3,2},{4,5},{5,4},{6,7},{7,6},{8,9},{9,8},{10,11... | collective-permute-start | bytes 638984 | tf_op jit(solution)/shard_map/ppermute | solution.py:23
  49.8 14.0 %collective-permute-start.7 = (bf16[2,8,13,8,128]{4,3,2,1,0:T(8,128)(2,1)S(1)}, bf16[2,8,13,8,128]{4,3,2,1,0:T(8,128)(2,1)S(1)}, u32[]{:S(2)}, u32[]{:S(2)}) collective-permute-start(bf16[2,8,13,8,128]{4,3,2,1,0:T(8,128)(2,1)S(1)} %pad_maximum_fusion.3.refs_0_), channel_id=1, source_target_pairs={{0,2},{1,15},{2,4},{3,1},{4,6},{5,3},{6,8},{7,5},{8,10},{9,7},{10,... | collective-permute-start | bytes 1277960 | tf_op jit(solution)/shard_map/ppermute | solution.py:23
  50.6 7.2 %collective-permute-start.11 = (bf16[1,8,13,8,128]{4,3,2,1,0:T(8,128)(2,1)S(1)}, bf16[1,8,13,8,128]{4,3,2,1,0:T(8,128)(2,1)S(1)}, u32[]{:S(2)}, u32[]{:S(2)}) collective-permute-start(bf16[1,8,13,8,128]{4,3,2,1,0:T(8,128)(2,1)S(1)} %slice_bitcast_fusion.1), channel_id=1, source_target_pairs={{0,16},{1,17},{2,18},{3,19},{4,20},{5,21},{6,22},{7,23},{8,24},{9,... | collective-permute-start | bytes 638984 | tf_op jit(solution)/shard_map/ppermute | solution.py:23
  57.9 7.1 %collective-permute-start.12 = (bf16[1,8,13,8,128]{4,3,2,1,0:T(8,128)(2,1)S(1)}, bf16[1,8,13,8,128]{4,3,2,1,0:T(8,128)(2,1)S(1)}, u32[]{:S(2)}, u32[]{:S(2)}) collective-permute-start(bf16[1,8,13,8,128]{4,3,2,1,0:T(8,128)(2,1)S(1)} %collective-permute-done.11.refs_0_), channel_id=1, source_target_pairs={{0,1},{1,0},{2,3},{3,2},{4,5},{5,4},{6,7},{7,6},{8,9},{9,8},{10,11... | collective-permute-start | bytes 638984 | tf_op jit(solution)/shard_map/ppermute | solution.py:23
  66.0 20.6 %collective-permute-start.14 = (bf16[4,8,15,8,128]{4,3,2,1,0:T(8,128)(2,1)S(1)}, bf16[4,8,15,8,128]{4,3,2,1,0:T(8,128)(2,1)S(1)}, u32[]{:S(2)}, u32[]{:S(2)}) collective-permute-start(bf16[4,8,15,8,128]{4,3,2,1,0:T(8,128)(2,1)S(1)} %get-tuple-element.21.refs_0_), channel_id=1, source_target_pairs={{0,1},{1,0},{2,3},{3,2},{4,5},{5,4},{6,7},{7,6},{8,9},{9,8},{10,11... | collective-permute-start | bytes 2949128 | tf_op jit(solution)/shard_map/ppermute | solution.py:23
  67.7 18.8 %collective-permute-start.16 = (bf16[4,8,15,8,128]{4,3,2,1,0:T(8,128)(2,1)S(1)}, bf16[4,8,15,8,128]{4,3,2,1,0:T(8,128)(2,1)S(1)}, u32[]{:S(2)}, u32[]{:S(2)}) collective-permute-start(bf16[4,8,15,8,128]{4,3,2,1,0:T(8,128)(2,1)S(1)} %get-tuple-element.21.refs_0_), channel_id=1, source_target_pairs={{0,2},{1,15},{2,4},{3,1},{4,6},{5,3},{6,8},{7,5},{8,10},{9,7},{10,... | collective-permute-start | bytes 2949128 | tf_op jit(solution)/shard_map/ppermute | solution.py:23
  69.5 10.7 %collective-permute-start.8 = (bf16[2,8,13,8,128]{4,3,2,1,0:T(8,128)(2,1)S(1)}, bf16[2,8,13,8,128]{4,3,2,1,0:T(8,128)(2,1)S(1)}, u32[]{:S(2)}, u32[]{:S(2)}) collective-permute-start(bf16[2,8,13,8,128]{4,3,2,1,0:T(8,128)(2,1)S(1)} %get-tuple-element.19.refs_2_), channel_id=1, source_target_pairs={{0,16},{1,17},{2,18},{3,19},{4,20},{5,21},{6,22},{7,23},{8,24},{9,... | collective-permute-start | bytes 1277960 | tf_op jit(solution)/shard_map/ppermute | solution.py:23
  69.9 15.7 %collective-permute-start.15 = (bf16[2,8,13,8,128]{4,3,2,1,0:T(8,128)(2,1)S(1)}, bf16[2,8,13,8,128]{4,3,2,1,0:T(8,128)(2,1)S(1)}, u32[]{:S(2)}, u32[]{:S(2)}) collective-permute-start(bf16[2,8,13,8,128]{4,3,2,1,0:T(8,128)(2,1)S(1)} %get-tuple-element.19.refs_2_), channel_id=1, source_target_pairs={{0,2},{1,15},{2,4},{3,1},{4,6},{5,3},{6,8},{7,5},{8,10},{9,7},{10,... | collective-permute-start | bytes 1277960 | tf_op jit(solution)/shard_map/ppermute | solution.py:23
  70.6 15.9 %collective-permute-start.10 = (bf16[2,8,13,8,128]{4,3,2,1,0:T(8,128)(2,1)S(1)}, bf16[2,8,13,8,128]{4,3,2,1,0:T(8,128)(2,1)S(1)}, u32[]{:S(2)}, u32[]{:S(2)}) collective-permute-start(bf16[2,8,13,8,128]{4,3,2,1,0:T(8,128)(2,1)S(1)} %get-tuple-element.19.refs_2_), channel_id=1, source_target_pairs={{0,1},{1,0},{2,3},{3,2},{4,5},{5,4},{6,7},{7,6},{8,9},{9,8},{10,11... | collective-permute-start | bytes 1277960 | tf_op jit(solution)/shard_map/ppermute | solution.py:23
  80.2 6.3 %collective-permute-start.9 = (bf16[2,8,13,8,128]{4,3,2,1,0:T(8,128)(2,1)S(1)}, bf16[2,8,13,8,128]{4,3,2,1,0:T(8,128)(2,1)S(1)}, u32[]{:S(2)}, u32[]{:S(2)}) collective-permute-start(bf16[2,8,13,8,128]{4,3,2,1,0:T(8,128)(2,1)S(1)} %collective-permute-done.8.refs_0_), channel_id=1, source_target_pairs={{0,1},{1,0},{2,3},{3,2},{4,5},{5,4},{6,7},{7,6},{8,9},{9,8},{10,11... | collective-permute-start | bytes 1277960 | tf_op jit(solution)/shard_map/ppermute | solution.py:23
  85.5 17.8 %copy-start = (f32[8,3584]{1,0:T(8,128)S(1)}, f32[8,3584]{1,0:T(8,128)}, u32[]{:S(2)}) copy-start(f32[8,3584]{1,0:T(8,128)} %param.5) | copy-start | bytes 344068
  88.2 21.9 %collective-permute-start.24 = (bf16[4,8,15,8,128]{4,3,2,1,0:T(8,128)(2,1)S(1)}, bf16[4,8,15,8,128]{4,3,2,1,0:T(8,128)(2,1)}, u32[]{:S(2)}, u32[]{:S(2)}) collective-permute-start(bf16[4,8,15,8,128]{4,3,2,1,0:T(8,128)(2,1)S(1)} %get-tuple-element.25.refs_0_), channel_id=1, source_target_pairs={{0,1},{1,0},{2,3},{3,2},{4,5},{5,4},{6,7},{7,6},{8,9},{9,8},{10,11... | collective-permute-start | bytes 2949128 | tf_op jit(solution)/shard_map/ppermute | solution.py:23
  90.5 19.7 %collective-permute-start.25 = (bf16[4,8,15,8,128]{4,3,2,1,0:T(8,128)(2,1)S(1)}, bf16[4,8,15,8,128]{4,3,2,1,0:T(8,128)(2,1)S(1)}, u32[]{:S(2)}, u32[]{:S(2)}) collective-permute-start(bf16[4,8,15,8,128]{4,3,2,1,0:T(8,128)(2,1)S(1)} %get-tuple-element.25.refs_0_), channel_id=1, source_target_pairs={{0,2},{1,15},{2,4},{3,1},{4,6},{5,3},{6,8},{7,5},{8,10},{9,7},{10,... | collective-permute-start | bytes 2949128 | tf_op jit(solution)/shard_map/ppermute | solution.py:23
  91.1 11.8 %collective-permute-start.21 = (bf16[2,8,13,8,128]{4,3,2,1,0:T(8,128)(2,1)S(1)}, bf16[2,8,13,8,128]{4,3,2,1,0:T(8,128)(2,1)S(1)}, u32[]{:S(2)}, u32[]{:S(2)}) collective-permute-start(bf16[2,8,13,8,128]{4,3,2,1,0:T(8,128)(2,1)S(1)} %get-tuple-element.23.refs_4_), channel_id=1, source_target_pairs={{0,16},{1,17},{2,18},{3,19},{4,20},{5,21},{6,22},{7,23},{8,24},{9,... | collective-permute-start | bytes 1277960 | tf_op jit(solution)/shard_map/ppermute | solution.py:23
  91.5 16.8 %collective-permute-start.17 = (bf16[2,8,13,8,128]{4,3,2,1,0:T(8,128)(2,1)S(1)}, bf16[2,8,13,8,128]{4,3,2,1,0:T(8,128)(2,1)S(1)}, u32[]{:S(2)}, u32[]{:S(2)}) collective-permute-start(bf16[2,8,13,8,128]{4,3,2,1,0:T(8,128)(2,1)S(1)} %get-tuple-element.23.refs_4_), channel_id=1, source_target_pairs={{0,2},{1,15},{2,4},{3,1},{4,6},{5,3},{6,8},{7,5},{8,10},{9,7},{10,... | collective-permute-start | bytes 1277960 | tf_op jit(solution)/shard_map/ppermute | solution.py:23
  92.1 18.0 %collective-permute-start.23 = (bf16[2,8,13,8,128]{4,3,2,1,0:T(8,128)(2,1)S(1)}, bf16[2,8,13,8,128]{4,3,2,1,0:T(8,128)(2,1)}, u32[]{:S(2)}, u32[]{:S(2)}) collective-permute-start(bf16[2,8,13,8,128]{4,3,2,1,0:T(8,128)(2,1)S(1)} %get-tuple-element.23.refs_4_), channel_id=1, source_target_pairs={{0,1},{1,0},{2,3},{3,2},{4,5},{5,4},{6,7},{7,6},{8,9},{9,8},{10,11... | collective-permute-start | bytes 1277960 | tf_op jit(solution)/shard_map/ppermute | solution.py:23
  102.9 7.2 %collective-permute-start.22 = (bf16[2,8,13,8,128]{4,3,2,1,0:T(8,128)(2,1)S(1)}, bf16[2,8,13,8,128]{4,3,2,1,0:T(8,128)(2,1)}, u32[]{:S(2)}, u32[]{:S(2)}) collective-permute-start(bf16[2,8,13,8,128]{4,3,2,1,0:T(8,128)(2,1)S(1)} %collective-permute-done.21.refs_0_), channel_id=1, source_target_pairs={{0,1},{1,0},{2,3},{3,2},{4,5},{5,4},{6,7},{7,6},{8,9},{9,8},{10,11... | collective-permute-start | bytes 1277960 | tf_op jit(solution)/shard_map/ppermute | solution.py:23
  108.3 7.5 %collective-permute-start = (f32[28,8,128]{2,1,0:T(8,128)}, f32[28,8,128]{2,1,0:T(8,128)S(1)}, u32[]{:S(2)}, u32[]{:S(2)}) collective-permute-start(f32[28,8,128]{2,1,0:T(8,128)} %fusion.5), channel_id=1, source_target_pairs={{0,32},{32,0},{64,96},{96,64},{128,160},{160,128},{192,224},{224,1... | collective-permute-start | bytes 344072 | tf_op jit(solution)/shard_map/ppermute | solution.py:39
  113.2 27.1 %collective-permute-start.26 = (bf16[4,8,15,8,128]{4,3,2,1,0:T(8,128)(2,1)S(1)}, bf16[4,8,15,8,128]{4,3,2,1,0:T(8,128)(2,1)S(1)}, u32[]{:S(2)}, u32[]{:S(2)}) collective-permute-start(bf16[4,8,15,8,128]{4,3,2,1,0:T(8,128)(2,1)S(1)} %get-tuple-element.29.refs_0_), channel_id=1, source_target_pairs={{0,1},{1,0},{2,3},{3,2},{4,5},{5,4},{6,7},{7,6},{8,9},{9,8},{10,11... | collective-permute-start | bytes 2949128 | tf_op jit(solution)/shard_map/ppermute | solution.py:23
  115.7 0.6 copy-start.2
  117.3 15.1 %collective-permute-start.18 = (bf16[2,8,13,8,128]{4,3,2,1,0:T(8,128)(2,1)S(1)}, bf16[2,8,13,8,128]{4,3,2,1,0:T(8,128)(2,1)}, u32[]{:S(2)}, u32[]{:S(2)}) collective-permute-start(bf16[2,8,13,8,128]{4,3,2,1,0:T(8,128)(2,1)S(1)} %get-tuple-element.27.refs_4_), channel_id=1, source_target_pairs={{0,16},{1,17},{2,18},{3,19},{4,20},{5,21},{6,22},{7,23},{8,24},{9,... | collective-permute-start | bytes 1277960 | tf_op jit(solution)/shard_map/ppermute | solution.py:23
  118.5 5.9 %collective-permute-start.1 = (f32[2,28,8,128]{3,2,1,0:T(8,128)}, f32[2,28,8,128]{3,2,1,0:T(8,128)S(1)}, u32[]{:S(2)}, u32[]{:S(2)}) collective-permute-start(f32[2,28,8,128]{3,2,1,0:T(8,128)} %reverse_select_fusion.2), channel_id=1, source_target_pairs={{0,64},{32,96},{64,0},{96,32},{128,192},{160,224},{192,128},{224,1... | collective-permute-start | bytes 688136 | tf_op jit(solution)/shard_map/ppermute | solution.py:39
  118.8 11.2 %collective-permute-start.2 = (f32[2,28,8,128]{3,2,1,0:T(8,128)}, f32[2,28,8,128]{3,2,1,0:T(8,128)S(1)}, u32[]{:S(2)}, u32[]{:S(2)}) collective-permute-start(f32[2,28,8,128]{3,2,1,0:T(8,128)} %reverse_select_fusion.2), channel_id=1, source_target_pairs={{0,128},{32,160},{64,192},{96,224},{128,0},{160,32},{192,64},{224,... | collective-permute-start | bytes 688136 | tf_op jit(solution)/shard_map/ppermute | solution.py:39
  120.6 12.6 %collective-permute-start.3 = (f32[2,28,8,128]{3,2,1,0:T(8,128)}, f32[2,28,8,128]{3,2,1,0:T(8,128)}, u32[]{:S(2)}, u32[]{:S(2)}) collective-permute-start(f32[2,28,8,128]{3,2,1,0:T(8,128)} %reverse_select_fusion.2), channel_id=1, source_target_pairs={{0,192},{32,224},{64,128},{96,160},{128,64},{160,96},{192,0},{224,... | collective-permute-start | bytes 688136 | tf_op jit(solution)/shard_map/ppermute | solution.py:39
  124.4 15.9 %collective-permute-start.28 = (bf16[2,8,15,8,128]{4,3,2,1,0:T(8,128)(2,1)}, bf16[2,8,15,8,128]{4,3,2,1,0:T(8,128)(2,1)S(1)}, u32[]{:S(2)}, u32[]{:S(2)}) collective-permute-start(bf16[2,8,15,8,128]{4,3,2,1,0:T(8,128)(2,1)} %slice.15), channel_id=1, source_target_pairs={{0,2},{1,15},{2,4},{3,1},{4,6},{5,3},{6,8},{7,5},{8,10},{9,7},{10,... | collective-permute-start | bytes 1474568 | tf_op jit(solution)/shard_map/ppermute | solution.py:23
  129.9 2.4 %copy-start.1 = (f32[2,28,8,128]{3,2,1,0:T(8,128)}, f32[2,28,8,128]{3,2,1,0:T(8,128)S(1)}, u32[]{:S(2)}) copy-start(f32[2,28,8,128]{3,2,1,0:T(8,128)S(1)} %collective-permute-done.2) | copy-start | bytes 688132
  129.9 10.4 %collective-permute-start.20 = (bf16[2,8,13,8,128]{4,3,2,1,0:T(8,128)(2,1)S(1)}, bf16[2,8,13,8,128]{4,3,2,1,0:T(8,128)(2,1)}, u32[]{:S(2)}, u32[]{:S(2)}) collective-permute-start(bf16[2,8,13,8,128]{4,3,2,1,0:T(8,128)(2,1)S(1)} %get-tuple-element.27.refs_4_), channel_id=1, source_target_pairs={{0,1},{1,0},{2,3},{3,2},{4,5},{5,4},{6,7},{7,6},{8,9},{9,8},{10,11... | collective-permute-start | bytes 1277960 | tf_op jit(solution)/shard_map/ppermute | solution.py:23
  132.4 8.0 %collective-permute-start.19 = (bf16[2,8,13,8,128]{4,3,2,1,0:T(8,128)(2,1)}, bf16[2,8,13,8,128]{4,3,2,1,0:T(8,128)(2,1)}, u32[]{:S(2)}, u32[]{:S(2)}) collective-permute-start(bf16[2,8,13,8,128]{4,3,2,1,0:T(8,128)(2,1)} %collective-permute-done.18.refs_0_), channel_id=1, source_target_pairs={{0,1},{1,0},{2,3},{3,2},{4,5},{5,4},{6,7},{7,6},{8,9},{9,8},{10,11... | collective-permute-start | bytes 1277960 | tf_op jit(solution)/shard_map/ppermute | solution.py:23
  133.2 5.0 %collective-permute-start.27 = (bf16[1,8,13,8,128]{4,3,2,1,0:T(8,128)(2,1)S(1)}, bf16[1,8,13,8,128]{4,3,2,1,0:T(8,128)(2,1)S(1)}, u32[]{:S(2)}, u32[]{:S(2)}) collective-permute-start(bf16[1,8,13,8,128]{4,3,2,1,0:T(8,128)(2,1)S(1)} %slice.14), channel_id=1, source_target_pairs={{0,2},{1,15},{2,4},{3,1},{4,6},{5,3},{6,8},{7,5},{8,10},{9,7},{10,... | collective-permute-start | bytes 638984 | tf_op jit(solution)/shard_map/ppermute | solution.py:23
  139.2 8.4 %collective-permute-start.29 = (bf16[1,8,13,8,128]{4,3,2,1,0:T(8,128)(2,1)S(1)}, bf16[1,8,13,8,128]{4,3,2,1,0:T(8,128)(2,1)S(1)}, u32[]{:S(2)}, u32[]{:S(2)}) collective-permute-start(bf16[1,8,13,8,128]{4,3,2,1,0:T(8,128)(2,1)S(1)} %get-tuple-element.31.refs_4_), channel_id=1, source_target_pairs={{0,16},{1,17},{2,18},{3,19},{4,20},{5,21},{6,22},{7,23},{8,24},{9,... | collective-permute-start | bytes 638984 | tf_op jit(solution)/shard_map/ppermute | solution.py:23
  143.1 6.9 %collective-permute-start.32 = (bf16[2,8,15,8,128]{4,3,2,1,0:T(8,128)(2,1)S(1)}, bf16[2,8,15,8,128]{4,3,2,1,0:T(8,128)(2,1)S(1)}, u32[]{:S(2)}, u32[]{:S(2)}) collective-permute-start(bf16[2,8,15,8,128]{4,3,2,1,0:T(8,128)(2,1)S(1)} %get-tuple-element.33.refs_0_), channel_id=1, source_target_pairs={{0,1},{1,0},{2,3},{3,2},{4,5},{5,4},{6,7},{7,6},{8,9},{9,8},{10,11... | collective-permute-start | bytes 1474568 | tf_op jit(solution)/shard_map/ppermute | solution.py:23
  147.5 2.5 %collective-permute-start.31 = (bf16[1,8,13,8,128]{4,3,2,1,0:T(8,128)(2,1)S(1)}, bf16[1,8,13,8,128]{4,3,2,1,0:T(8,128)(2,1)S(1)}, u32[]{:S(2)}, u32[]{:S(2)}) collective-permute-start(bf16[1,8,13,8,128]{4,3,2,1,0:T(8,128)(2,1)S(1)} %get-tuple-element.31.refs_4_), channel_id=1, source_target_pairs={{0,1},{1,0},{2,3},{3,2},{4,5},{5,4},{6,7},{7,6},{8,9},{9,8},{10,11... | collective-permute-start | bytes 638984 | tf_op jit(solution)/shard_map/ppermute | solution.py:23
  147.6 2.5 %collective-permute-start.30 = (bf16[1,8,13,8,128]{4,3,2,1,0:T(8,128)(2,1)S(1)}, bf16[1,8,13,8,128]{4,3,2,1,0:T(8,128)(2,1)S(1)}, u32[]{:S(2)}, u32[]{:S(2)}) collective-permute-start(bf16[1,8,13,8,128]{4,3,2,1,0:T(8,128)(2,1)S(1)} %collective-permute-done.29.refs_1_), channel_id=1, source_target_pairs={{0,1},{1,0},{2,3},{3,2},{4,5},{5,4},{6,7},{7,6},{8,9},{9,8},{10,11... | collective-permute-start | bytes 638984 | tf_op jit(solution)/shard_map/ppermute | solution.py:23

commit v2 on v1

v2 whole, which is shorter than its diff:
```python
import jax
import jax.numpy as jnp
from jax import lax
from jax.experimental import pallas as pl
from jax.experimental.pallas import tpu as pltpu
from jax.sharding import PartitionSpec as P

REPLICAS = 8
RUNS, SLOTS, CORES = 2, 8, 2
TILE = (8, 128)
GATE_FLOPS, PLACE_FLOPS = 6_000_000_000, 2_000_000_000
SPLIT = 14


def coords(index):
    return index // (SLOTS * CORES), index // CORES % SLOTS, index % CORES


def fsdp_index(run, slot, core):
    return (run % RUNS * SLOTS + slot % SLOTS) * CORES + core % CORES


def move(array, target):
    return lax.ppermute(array, "fsdp", [(i, fsdp_index(*target(*coords(i)))) for i in range(RUNS * SLOTS * CORES)])


def swap_run(array):
    return move(array, lambda run, slot, core: (run + 1, slot, core))


def swap_core(array):
    return move(array, lambda run, slot, core: (run, slot, core + 1))


def along_slots(array):
    return move(array, lambda run, slot, core: (run, slot + (1 if core == 0 else -1), core))


def place(out, groups, shape):
    arrays = [array for array, *_ in groups]
    through = [] if out is None else [out]
    blocks = [
        (at, lead, where, first, tiles)
        for at, (_, targets, first, tiles) in enumerate(groups)
        for lead, where in enumerate(targets)
    ]

    def kernel(*refs):
        held, result, sems = refs[: len(arrays)], refs[-2], refs[-1]
        own_run, own_slot, own_core = coords(lax.axis_index("fsdp"))
        copies = []
        for number, (at, lead, (run, hops, core, came), first, tiles) in enumerate(blocks):
            receiver = (own_core + came) % CORES
            block = fsdp_index(own_run + run, own_slot + (2 * receiver - 1) * hops, receiver + core)
            copies.append(
                pltpu.make_async_copy(held[at].at[lead], result.at[block, :, pl.ds(first, tiles)], sems.at[number])
            )
        for copy in copies:
            copy.start()
        for copy in copies:
            copy.wait()

    anywhere = pl.BlockSpec(memory_space=pl.ANY)
    moved = sum(array.size * array.dtype.itemsize for array in arrays)
    return pl.pallas_call(
        kernel,
        out_shape=jax.ShapeDtypeStruct(shape, jnp.bfloat16),
        in_specs=[pl.BlockSpec(memory_space=pltpu.VMEM)] * len(arrays) + [anywhere] * len(through),
        out_specs=anywhere,
        scratch_shapes=[pltpu.SemaphoreType.DMA((len(blocks),))],
        input_output_aliases={len(arrays): 0} if through else {},
        compiler_params=pltpu.CompilerParams(vmem_limit_bytes=moved + (1 << 20)),
        cost_estimate=pl.CostEstimate(flops=PLACE_FLOPS, bytes_accessed=2 * moved, transcendentals=0),
    )(*arrays, *through)


def gate(*arrays):
    anywhere = pl.BlockSpec(memory_space=pl.ANY)
    return pl.pallas_call(
        lambda *refs: None,
        out_shape=[jax.ShapeDtypeStruct(array.shape, array.dtype) for array in arrays],
        in_specs=[anywhere] * len(arrays),
        out_specs=[anywhere] * len(arrays),
        input_output_aliases={at: at for at in range(len(arrays))},
        compiler_params=pltpu.CompilerParams(vmem_limit_bytes=1 << 20),
        cost_estimate=pl.CostEstimate(flops=GATE_FLOPS, bytes_accessed=0, transcendentals=0),
    )(*arrays)


def step(inner, outer, momentum):
    terms = lax.all_to_all(inner, "replica", 0, 0).astype(jnp.float32)
    average = outer - jnp.sum(terms, axis=0) / REPLICAS
    momentum_new = 0.9 * momentum + average
    return outer - 0.7 * (average + 0.9 * momentum_new), momentum_new


def to_all(array):
    return lax.all_to_all(jnp.broadcast_to(array, (REPLICAS,) + array.shape), "replica", 0, 0)


def write(token, *arrays):
    count = len(arrays)

    def kernel(*refs):
        held, results, sems = refs[1 : 1 + count], refs[2 + count : -1], refs[-1]
        copies = [pltpu.make_async_copy(held[at], results[at], sems.at[at]) for at in range(count)]
        for copy in copies:
            copy.start()
        for copy in copies:
            copy.wait()

    anywhere = pl.BlockSpec(memory_space=pl.ANY)
    moved = sum(array.size * array.dtype.itemsize for array in arrays)
    return pl.pallas_call(
        kernel,
        out_shape=[jax.ShapeDtypeStruct(array.shape, array.dtype) for array in (token,) + arrays],
        in_specs=[anywhere] + [pl.BlockSpec(memory_space=pltpu.VMEM)] * count,
        out_specs=[anywhere] * (1 + count),
        scratch_shapes=[pltpu.SemaphoreType.DMA((count,))],
        input_output_aliases={0: 0},
        compiler_params=pltpu.CompilerParams(vmem_limit_bytes=moved + (1 << 20)),
        cost_estimate=pl.CostEstimate(flops=PLACE_FLOPS, bytes_accessed=2 * moved, transcendentals=0),
    )(token, *arrays)


def gather(own, head, rest, outer_all, momentum_new, shape):
    width, split = own.shape[1], head.shape[1]

    def group(array, hops, came=0, run=0, first=0):
        targets = [(run, hops, core, came) for core in range(array.shape[0])]
        return array, targets, first, array.shape[2]

    def head_of(array):
        return array[:, :, :split]

    def q(array, hops, came=0):
        return group(array, hops, came, 1, split)

    def y(array, hops, came=0):
        return group(array, hops, came, 1)

    own, head, rest = own[None], head[None], rest[None]
    beside = swap_run(rest)
    p0 = jnp.concatenate([own, swap_core(own)])
    token, p0 = gate(jnp.zeros(TILE, jnp.float32), p0)
    p1 = along_slots(p0)
    token, outer_all, momentum_new = write(token, outer_all, momentum_new)

    token, beside = gate(token, beside)
    q0 = jnp.concatenate([beside, swap_core(beside)])
    q1 = along_slots(q0)
    out = place(None, [group(p0, 0)], shape)

    token, out, p1 = gate(token, out, p1)
    p2, y1, cp1 = along_slots(p1), swap_run(head_of(p1)), swap_core(p1)
    out = place(out, [q(q0, 0)], shape)

    token, out, q1 = gate(token, out, q1)
    q2, cq1, y0 = along_slots(q1), swap_core(q1), swap_run(head)
    out = place(out, [group(p1, 1)], shape)

    token, out, p2, y1, cp1 = gate(token, out, p2, y1, cp1)
    p3, y2, cp2, cy1 = along_slots(p2), swap_run(head_of(p2)), swap_core(p2), swap_core(y1)
    out = place(out, [q(q1, 1)], shape)

    token, out, q2, cq1, y0 = gate(token, out, q2, cq1, y0)
    q3, cq2, cy0 = along_slots(q2), swap_core(q2), swap_core(y0)
    out = place(out, [group(p2, 2), y(y1, 1), group(cp1, 1, 1)], shape)

    token, out, p3, y2, cp2, cy1 = gate(token, out, p3, y2, cp2, cy1)
    p4, y3, cp3, cy2 = along_slots(p3[:1]), swap_run(head_of(p3)), swap_core(p3), swap_core(y2)
    out = place(out, [q(q2, 2), q(cq1, 1, 1), y(y0, 0)], shape)

    token, out, q3, cq2, cy0 = gate(token, out, q3, cq2, cy0)
    q4, cq3 = along_slots(q3[:1]), swap_core(q3)
    out = place(out, [group(p3, 3), y(y2, 2), group(cp2, 2, 1), y(cy1, 1, 1)], shape)

    token, out, p4, y3, cp3, cy2 = gate(token, out, p4, y3, cp3, cy2)
    y4, cp4, cy3 = swap_run(head_of(p4)), swap_core(p4), swap_core(y3)
    out = place(out, [q(q3, 3), q(cq2, 2, 1), y(cy0, 0, 1)], shape)

    token, out, q4, cq3 = gate(token, out, q4, cq3)
    cq4 = swap_core(q4)
    out = place(out, [group(p4, 4), y(y3, 3), group(cp3, 3, 1), y(cy2, 2, 1)], shape)

    token, out, y4, cp4, cy3 = gate(token, out, y4, cp4, cy3)
    cy4 = swap_core(y4)
    out = place(out, [q(q4, 4), q(cq3, 3, 1), y(y4, 4), group(cp4, 4, 1), y(cy3, 3, 1)], shape)
    return place(out, [q(cq4, 4, 1), y(cy4, 4, 1)], shape), outer_all, momentum_new


def body(inner, outer, momentum):
    width = momentum.shape[1] // TILE[1]
    replica = lax.axis_index("replica")

    def tiles(array):
        array = array.reshape(TILE[0], -1, width, TILE[1])
        return array.transpose(1, 2, 0, 3)

    def rows(array):
        return array.transpose(2, 0, 1, 3).reshape(TILE[0], -1)

    inner, outer, momentum = tiles(inner[0]), tiles(outer), tiles(momentum)[0]
    own_outer = lax.dynamic_index_in_dim(outer, replica, 0, keepdims=False)
    shape = (RUNS * SLOTS * CORES, REPLICAS, width) + TILE

    outer_new, momentum_new = step(inner, own_outer, momentum)
    outer_all = to_all(outer_new)

    def blend(at):
        return (0.5 * inner[:, at].astype(jnp.float32) + 0.5 * outer_all[:, at]).astype(jnp.bfloat16)

    parts = blend(slice(0, None)), blend(slice(0, SPLIT)), blend(slice(SPLIT, None))
    out, outer_all, momentum_new = gather(*parts, outer_all, momentum_new, shape)
    gathered = out.transpose(0, 3, 1, 2, 4).reshape(1, -1, REPLICAS * width * TILE[1])
    return rows(outer_all), rows(momentum_new[None]), gathered


def solution(mesh):
    placed = (P("replica", "fsdp", None), P("fsdp", None), P("fsdp", "replica"))
    return jax.shard_map(
        body,
        mesh=mesh,
        in_specs=placed,
        out_specs=(P("fsdp", None), P("fsdp", "replica"), P("replica", None, None)),
        check_vma=False,
    )
```

time: 152 us -> 117 us (0.77)
  waiting for transfers between devices: 69.1 us -> 34.5 us
  blocking collectives: 12.4 us -> 17 us
  other arithmetic: 7.43 us -> 3.46 us
    ppermute x29, waiting for transfers between devices: 52.9 us -> 24.9 us  [move(): lax.ppermute(array, 'fsdp', [(i, fsdp_index(*target(*coords(i)))) for i i...]
    ppermute x4 -> x0, waiting for transfers between devices: 6.62 us -> none  [swap_replica(): lax.ppermute(array, 'replica', [(i, i ^ bits) for i in range(REPLICAS)])]
    ppermute x29, starting transfers between devices: 34 us -> 39.7 us  [move(): lax.ppermute(array, 'fsdp', [(i, fsdp_index(*target(*coords(i)))) for i i...]
    ppermute x4 -> x0, starting transfers between devices: 4.7 us -> none  [swap_replica(): lax.ppermute(array, 'replica', [(i, i ^ bits) for i in range(REPLICAS)])]
    all_to_all x1, blocking collectives: 12.4 us -> 17 us  [to_all(): lax.all_to_all(jnp.broadcast_to(array, (REPLICAS,) + array.shape), 'repli...]
    broadcast_in_dim x0 -> x2, other arithmetic: none -> 2.31 us  [gather(): own, head, rest = (own[None], head[None], rest[None])]
    another operation x3 -> x0, other arithmetic: 2.04 us -> none  [the longest x2 1.13 us: body(): jnp.stack([pair] + [swap_replica(pair, 2 * bits) for bits in range(1, 4)])]
    select_n x3 -> x0, other arithmetic: 1.78 us -> none  [by_xor(): array = jnp.where(bit == 1, jnp.flip(array, level), array)]
  transfers between devices with their start and end apart: 34 -> 30, of which waited for: 15 -> 10; matrix products, arithmetic and copies ran while one was open for 4% -> 1% of each run, Pallas kernels for 7% -> 11%
where the time goes in v2:
time: 117 us
  starting transfers between devices  47.1 us (40%)
  waiting for transfers between devices  34.5 us (29%)
  blocking collectives  17 us (15%)
  Pallas kernels  13.1 us (11%)
  other arithmetic  3.46 us (3%)
    ppermute x29, starting transfers between devices, move(): lax.ppermute(array, 'fsdp', [(i, fsdp_index(*target(*coords(i)))) for i i...  39.7 us
    ppermute x29, waiting for transfers between devices, move(): lax.ppermute(array, 'fsdp', [(i, fsdp_index(*target(*coords(i)))) for i i...  24.9 us
    all_to_all x1, blocking collectives, to_all(): lax.all_to_all(jnp.broadcast_to(array, (REPLICAS,) + array.shape), 'repli...  17 us
    pallas_call x11, Pallas kernels, place(): pl.pallas_call(kernel, out_shape=jax.ShapeDtypeStruct(shape, jnp.bfloat16...  12.1 us
    all_to_all x1, waiting for transfers between devices, step(): terms = lax.all_to_all(inner, 'replica', 0, 0).astype(jnp.float32)  9.63 us
    all_to_all x1, starting transfers between devices, step(): terms = lax.all_to_all(inner, 'replica', 0, 0).astype(jnp.float32)  7.49 us
  transfers between devices with their start and end apart: 30, of which 10 were waited for; matrix products, arithmetic and copies ran while one was open for 1% of the time, Pallas kernels for 11%

profile of v2, /device:TPU:1, one launch (start us, length us, event | category | flops | bytes accessed | tf_op | source)
XLA Modules:
  0.0 116.6 jit_solution(2669701448264762596)
XLA Ops:
  0.6 7.5 %all-to-all-start = ((bf16[8,28,8,128]{3,2,1,0:T(8,128)(2,1)}), bf16[8,28,8,128]{3,2,1,0:T(8,128)(2,1)S(1)}, u32[]{:S(2)}, u32[]{:S(2)}) async-start(bf16[8,28,8,128]{3,2,1,0:T(8,128)(2,1)} %bitcast.39), calls=%async_computation | async-start | bytes 917504 | tf_op jit(solution)/shard_map/all_to_all | solution.py:91
  8.1 9.6 %all-to-all-done = bf16[8,28,8,128]{3,2,1,0:T(8,128)(2,1)S(1)} async-done(((bf16[8,28,8,128]{3,2,1,0:T(8,128)(2,1)}), bf16[8,28,8,128]{3,2,1,0:T(8,128)(2,1)S(1)}, u32[]{:S(2)}, u32[]{:S(2)}) %all-to-all-start) | async-done | bytes 458784 | tf_op jit(solution)/shard_map/all_to_all | solution.py:91
  17.8 1.0 bitcast_subtract_fusion
  18.9 17.0 %all_to_all.10.refs_1_ = f32[8,28,8,128]{3,2,1,0:T(8,128)S(1)} all-to-all(f32[8,28,8,128]{3,2,1,0:T(8,128)S(1)} %broadcast_in_dim.19), channel_id=1, replica_groups=mesh['replica'=8,'fsdp'=32] {'replica'}, dimensions={0} | all-to-all | bytes 1835008 | tf_op jit(solution)/shard_map/all_to_all | solution.py:98
  35.9 1.1 fusion
  37.0 3.0 %collective-permute-start = (bf16[1,8,28,8,128]{4,3,2,1,0:T(8,128)(2,1)S(1)}, bf16[1,8,28,8,128]{4,3,2,1,0:T(8,128)(2,1)S(1)}, u32[]{:S(2)}, u32[]{:S(2)}) collective-permute-start(bf16[1,8,28,8,128]{4,3,2,1,0:T(8,128)(2,1)S(1)} %fusion), channel_id=1, source_target_pairs={{0,1},{1,0},{2,3},{3,2},{4,5},{5,4},{6,7},{7,6},{8,9},{9,8},{10,11... | collective-permute-start | bytes 1376264 | tf_op jit(solution)/shard_map/ppermute | solution.py:24
  40.1 1.2 %fusion.6 = (bf16[1,8,14,8,128]{4,3,2,1,0:T(8,128)(2,1)S(1)}, bf16[1,8,14,8,128]{4,3,2,1,0:T(8,128)(2,1)S(1)}) fusion(f32[8,28,8,128]{3,2,1,0:T(8,128)S(1)} %all_to_all.10.refs_1_, bf16[8,28,8,128]{3,2,1,0:T(8,128)(2,1)} %bitcast.41), kind=kLoop, calls=%fused_computation.11 | loop fusion | flops 917504 | bytes 1835008 | tf_op jit(solution)/shard_map/broadcast_in_dim | solution.py:142
  41.2 0.5 collective-permute-start.1
  41.7 1.1 collective-permute-start.10
  42.9 5.7 %collective-permute-start.2 = (bf16[2,8,28,8,128]{4,3,2,1,0:T(8,128)(2,1)S(1)}, bf16[2,8,28,8,128]{4,3,2,1,0:T(8,128)(2,1)S(1)}, u32[]{:S(2)}, u32[]{:S(2)}) collective-permute-start(bf16[2,8,28,8,128]{4,3,2,1,0:T(8,128)(2,1)S(1)} %get-tuple-element.56.refs_0_), channel_id=1, source_target_pairs={{0,2},{1,15},{2,4},{3,1},{4,6},{5,3},{6,8},{7,5},{8,10},{9,7},{10,... | collective-permute-start | bytes 2752520 | tf_op jit(solution)/shard_map/ppermute | solution.py:24
  48.6 1.0 shard_map.59
  49.8 1.0 shard_map.61.refs_1_
  50.7 0.4 collective-permute-done.3
  51.2 5.4 %collective-permute-start.4 = (bf16[2,8,14,8,128]{4,3,2,1,0:T(8,128)(2,1)S(1)}, bf16[2,8,14,8,128]{4,3,2,1,0:T(8,128)(2,1)S(1)}, u32[]{:S(2)}, u32[]{:S(2)}) collective-permute-start(bf16[2,8,14,8,128]{4,3,2,1,0:T(8,128)(2,1)S(1)} %constant_dynamic-update-slice_fusion.refs_0_), channel_id=1, source_target_pairs={{0,2},{1,15},{2,4},{3,1},{4,6},{5,3},{6,8},{7,5},{8,10},{9,7},{10,... | collective-permute-start | bytes 1376264 | tf_op jit(solution)/shard_map/ppermute | solution.py:24
  56.5 2.3 %collective-permute-done.2.refs_2_ = bf16[2,8,28,8,128]{4,3,2,1,0:T(8,128)(2,1)S(1)} collective-permute-done((bf16[2,8,28,8,128]{4,3,2,1,0:T(8,128)(2,1)S(1)}, bf16[2,8,28,8,128]{4,3,2,1,0:T(8,128)(2,1)S(1)}, u32[]{:S(2)}, u32[]{:S(2)}) %collective-permute-start.2) | collective-permute-done | bytes 917536 | tf_op jit(solution)/shard_map/ppermute | solution.py:24
  58.9 3.1 %collective-permute-start.5 = (bf16[2,8,28,8,128]{4,3,2,1,0:T(8,128)(2,1)S(1)}, bf16[2,8,28,8,128]{4,3,2,1,0:T(8,128)(2,1)S(1)}, u32[]{:S(2)}, u32[]{:S(2)}) collective-permute-start(bf16[2,8,28,8,128]{4,3,2,1,0:T(8,128)(2,1)S(1)} %get-tuple-element.61.refs_0_), channel_id=1, source_target_pairs={{0,2},{1,15},{2,4},{3,1},{4,6},{5,3},{6,8},{7,5},{8,10},{9,7},{10,... | collective-permute-start | bytes 2752520 | tf_op jit(solution)/shard_map/ppermute | solution.py:24
  62.1 0.5 collective-permute-start.6
  62.6 0.8 shard_map.63.refs_1_
  63.4 0.4 collective-permute-done.4.refs_2_
  63.8 3.1 %collective-permute-start.8 = (bf16[2,8,14,8,128]{4,3,2,1,0:T(8,128)(2,1)S(1)}, bf16[2,8,14,8,128]{4,3,2,1,0:T(8,128)(2,1)S(1)}, u32[]{:S(2)}, u32[]{:S(2)}) collective-permute-start(bf16[2,8,14,8,128]{4,3,2,1,0:T(8,128)(2,1)S(1)} %get-tuple-element.64.refs_0_), channel_id=1, source_target_pairs={{0,2},{1,15},{2,4},{3,1},{4,6},{5,3},{6,8},{7,5},{8,10},{9,7},{10,... | collective-permute-start | bytes 1376264 | tf_op jit(solution)/shard_map/ppermute | solution.py:24
  66.9 0.9 shard_map.65.refs_1_
  67.9 6.1 %collective-permute-done.6.refs_3_ = bf16[2,8,14,8,128]{4,3,2,1,0:T(8,128)(2,1)S(1)} collective-permute-done((bf16[2,8,14,8,128]{4,3,2,1,0:T(8,128)(2,1)S(1)}, bf16[2,8,14,8,128]{4,3,2,1,0:T(8,128)(2,1)S(1)}, u32[]{:S(2)}, u32[]{:S(2)}) %collective-permute-start.6) | collective-permute-done | bytes 458784 | tf_op jit(solution)/shard_map/ppermute | solution.py:24
  73.9 1.2 %collective-permute-start.9 = (bf16[2,8,14,8,128]{4,3,2,1,0:T(8,128)(2,1)S(1)}, bf16[2,8,14,8,128]{4,3,2,1,0:T(8,128)(2,1)S(1)}, u32[]{:S(2)}, u32[]{:S(2)}) collective-permute-start(bf16[2,8,14,8,128]{4,3,2,1,0:T(8,128)(2,1)S(1)} %get-tuple-element.64.refs_0_), channel_id=1, source_target_pairs={{0,1},{1,0},{2,3},{3,2},{4,5},{5,4},{6,7},{7,6},{8,9},{9,8},{10,11... | collective-permute-start | bytes 1376264 | tf_op jit(solution)/shard_map/ppermute | solution.py:24
  75.2 1.7 %collective-permute-start.11 = (bf16[2,8,28,8,128]{4,3,2,1,0:T(8,128)(2,1)S(1)}, bf16[2,8,28,8,128]{4,3,2,1,0:T(8,128)(2,1)S(1)}, u32[]{:S(2)}, u32[]{:S(2)}) collective-permute-start(bf16[2,8,28,8,128]{4,3,2,1,0:T(8,128)(2,1)S(1)} %get-tuple-element.67.refs_0_), channel_id=1, source_target_pairs={{0,2},{1,15},{2,4},{3,1},{4,6},{5,3},{6,8},{7,5},{8,10},{9,7},{10,... | collective-permute-start | bytes 2752520 | tf_op jit(solution)/shard_map/ppermute | solution.py:24
  77.0 0.8 shard_map.67.refs_1_
  77.8 0.5 collective-permute-start.12
  78.6 1.9 %collective-permute-start.14 = (bf16[2,8,14,8,128]{4,3,2,1,0:T(8,128)(2,1)S(1)}, bf16[2,8,14,8,128]{4,3,2,1,0:T(8,128)(2,1)S(1)}, u32[]{:S(2)}, u32[]{:S(2)}) collective-permute-start(bf16[2,8,14,8,128]{4,3,2,1,0:T(8,128)(2,1)S(1)} %get-tuple-element.68.refs_1_), channel_id=1, source_target_pairs={{0,1},{1,0},{2,3},{3,2},{4,5},{5,4},{6,7},{7,6},{8,9},{9,8},{10,11... | collective-permute-start | bytes 1376264 | tf_op jit(solution)/shard_map/ppermute | solution.py:24
  80.5 1.7 %collective-permute-start.15 = (bf16[2,8,14,8,128]{4,3,2,1,0:T(8,128)(2,1)S(1)}, bf16[2,8,14,8,128]{4,3,2,1,0:T(8,128)(2,1)S(1)}, u32[]{:S(2)}, u32[]{:S(2)}) collective-permute-start(bf16[2,8,14,8,128]{4,3,2,1,0:T(8,128)(2,1)S(1)} %get-tuple-element.72.refs_0_), channel_id=1, source_target_pairs={{0,2},{1,15},{2,4},{3,1},{4,6},{5,3},{6,8},{7,5},{8,10},{9,7},{10,... | collective-permute-start | bytes 1376264 | tf_op jit(solution)/shard_map/ppermute | solution.py:24
  82.2 1.4 %shard_map.69.refs_1_ = bf16[32,8,28,8,128]{4,3,2,1,0:T(8,128)(2,1)} custom-call(bf16[2,8,28,8,128]{4,3,2,1,0:T(8,128)(2,1)S(1)} %get-tuple-element.67.refs_0_, bf16[2,8,14,8,128]{4,3,2,1,0:T(8,128)(2,1)S(1)} %get-tuple-element.68.refs_1_, bf16[2,8,28,8,128]{4,3,2,1,0:T(8,128)(2,1)S(1)} %get-tuple-element.69.refs_2_, ...), custom_call_target="tpu_custom_call", output_to_operand_aliasing={{}: (3, {})} | custom-call | flops 2000000000 | bytes 4587520 | tf_op jit(solution)/shard_map/pallas_call | solution.py:65
  83.6 5.9 %collective-permute-done.12.refs_3_ = bf16[2,8,14,8,128]{4,3,2,1,0:T(8,128)(2,1)S(1)} collective-permute-done((bf16[2,8,14,8,128]{4,3,2,1,0:T(8,128)(2,1)S(1)}, bf16[2,8,14,8,128]{4,3,2,1,0:T(8,128)(2,1)S(1)}, u32[]{:S(2)}, u32[]{:S(2)}) %collective-permute-start.12) | collective-permute-done | bytes 458784 | tf_op jit(solution)/shard_map/ppermute | solution.py:24
  89.5 1.3 %collective-permute-start.16 = (bf16[2,8,14,8,128]{4,3,2,1,0:T(8,128)(2,1)S(1)}, bf16[2,8,14,8,128]{4,3,2,1,0:T(8,128)(2,1)S(1)}, u32[]{:S(2)}, u32[]{:S(2)}) collective-permute-start(bf16[2,8,14,8,128]{4,3,2,1,0:T(8,128)(2,1)S(1)} %get-tuple-element.72.refs_0_), channel_id=1, source_target_pairs={{0,1},{1,0},{2,3},{3,2},{4,5},{5,4},{6,7},{7,6},{8,9},{9,8},{10,11... | collective-permute-start | bytes 1376264 | tf_op jit(solution)/shard_map/ppermute | solution.py:24
  90.9 0.6 collective-permute-start.20
  91.5 1.6 %collective-permute-start.18 = (bf16[1,8,28,8,128]{4,3,2,1,0:T(8,128)(2,1)S(1)}, bf16[1,8,28,8,128]{4,3,2,1,0:T(8,128)(2,1)S(1)}, u32[]{:S(2)}, u32[]{:S(2)}) collective-permute-start(bf16[1,8,28,8,128]{4,3,2,1,0:T(8,128)(2,1)S(1)} %slice.36), channel_id=1, source_target_pairs={{0,2},{1,15},{2,4},{3,1},{4,6},{5,3},{6,8},{7,5},{8,10},{9,7},{10,... | collective-permute-start | bytes 1376264 | tf_op jit(solution)/shard_map/ppermute | solution.py:24
  93.1 1.0 shard_map.71.refs_1_
  94.2 0.5 collective-permute-start.19
  94.7 0.5 collective-permute-start.21
  95.3 1.6 %shard_map.73.refs_1_ = bf16[32,8,28,8,128]{4,3,2,1,0:T(8,128)(2,1)} custom-call(bf16[2,8,28,8,128]{4,3,2,1,0:T(8,128)(2,1)S(1)} %get-tuple-element.77.refs_0_, bf16[2,8,14,8,128]{4,3,2,1,0:T(8,128)(2,1)S(1)} %get-tuple-element.78.refs_1_, bf16[2,8,28,8,128]{4,3,2,1,0:T(8,128)(2,1)S(1)} %get-tuple-element.79.refs_2_, ...), custom_call_target="tpu_custom_call", output_to_operand_aliasing={{}: (4, {})} | custom-call | flops 2000000000 | bytes 5505024 | tf_op jit(solution)/shard_map/pallas_call | solution.py:65
  97.0 2.2 %collective-permute-done.18.refs_2_ = bf16[1,8,28,8,128]{4,3,2,1,0:T(8,128)(2,1)S(1)} collective-permute-done((bf16[1,8,28,8,128]{4,3,2,1,0:T(8,128)(2,1)S(1)}, bf16[1,8,28,8,128]{4,3,2,1,0:T(8,128)(2,1)S(1)}, u32[]{:S(2)}, u32[]{:S(2)}) %collective-permute-start.18) | collective-permute-done | bytes 458784 | tf_op jit(solution)/shard_map/ppermute | solution.py:24
  99.1 2.5 %collective-permute-start.22 = (bf16[1,8,14,8,128]{4,3,2,1,0:T(8,128)(2,1)S(1)}, bf16[1,8,14,8,128]{4,3,2,1,0:T(8,128)(2,1)S(1)}, u32[]{:S(2)}, u32[]{:S(2)}) collective-permute-start(bf16[1,8,14,8,128]{4,3,2,1,0:T(8,128)(2,1)S(1)} %slice.38), channel_id=1, source_target_pairs={{0,2},{1,15},{2,4},{3,1},{4,6},{5,3},{6,8},{7,5},{8,10},{9,7},{10,... | collective-permute-start | bytes 688136 | tf_op jit(solution)/shard_map/ppermute | solution.py:24
  101.7 4.3 %collective-permute-done.19.refs_3_ = bf16[2,8,14,8,128]{4,3,2,1,0:T(8,128)(2,1)S(1)} collective-permute-done((bf16[2,8,14,8,128]{4,3,2,1,0:T(8,128)(2,1)S(1)}, bf16[2,8,14,8,128]{4,3,2,1,0:T(8,128)(2,1)S(1)}, u32[]{:S(2)}, u32[]{:S(2)}) %collective-permute-start.19) | collective-permute-done | bytes 458784 | tf_op jit(solution)/shard_map/ppermute | solution.py:24
  106.1 0.5 collective-permute-start.25
  106.6 0.7 collective-permute-start.27
  107.3 1.0 shard_map.75.refs_1_
  108.5 1.4 %shard_map.77.refs_1_ = bf16[32,8,28,8,128]{4,3,2,1,0:T(8,128)(2,1)} custom-call(bf16[1,8,28,8,128]{4,3,2,1,0:T(8,128)(2,1)S(1)} %get-tuple-element.89.refs_0_, bf16[2,8,14,8,128]{4,3,2,1,0:T(8,128)(2,1)S(1)} %get-tuple-element.90.refs_1_, bf16[2,8,28,8,128]{4,3,2,1,0:T(8,128)(2,1)S(1)} %get-tuple-element.91.refs_2_, ...), custom_call_target="tpu_custom_call", output_to_operand_aliasing={{}: (4, {})} | custom-call | flops 2000000000 | bytes 4587520 | tf_op jit(solution)/shard_map/pallas_call | solution.py:65
  110.0 3.0 %collective-permute-done.25.refs_2_ = bf16[1,8,14,8,128]{4,3,2,1,0:T(8,128)(2,1)S(1)} collective-permute-done((bf16[1,8,14,8,128]{4,3,2,1,0:T(8,128)(2,1)S(1)}, bf16[1,8,14,8,128]{4,3,2,1,0:T(8,128)(2,1)S(1)}, u32[]{:S(2)}, u32[]{:S(2)}) %collective-permute-start.25) | collective-permute-done | bytes 229408 | tf_op jit(solution)/shard_map/ppermute | solution.py:24
  113.0 1.3 %collective-permute-start.28 = (bf16[1,8,14,8,128]{4,3,2,1,0:T(8,128)(2,1)S(1)}, bf16[1,8,14,8,128]{4,3,2,1,0:T(8,128)(2,1)S(1)}, u32[]{:S(2)}, u32[]{:S(2)}) collective-permute-start(bf16[1,8,14,8,128]{4,3,2,1,0:T(8,128)(2,1)S(1)} %get-tuple-element.94.refs_2_), channel_id=1, source_target_pairs={{0,1},{1,0},{2,3},{3,2},{4,5},{5,4},{6,7},{7,6},{8,9},{9,8},{10,11... | collective-permute-start | bytes 688136 | tf_op jit(solution)/shard_map/ppermute | solution.py:24
  114.3 1.3 %shard_map.79.refs_2_ = bf16[32,8,28,8,128]{4,3,2,1,0:T(8,128)(2,1)} custom-call(bf16[1,8,14,8,128]{4,3,2,1,0:T(8,128)(2,1)S(1)} %get-tuple-element.87.refs_0_, bf16[2,8,14,8,128]{4,3,2,1,0:T(8,128)(2,1)S(1)} %get-tuple-element.95.refs_1_, bf16[1,8,14,8,128]{4,3,2,1,0:T(8,128)(2,1)S(1)} %get-tuple-element.94.refs_2_, ...), custom_call_target="tpu_custom_call", output_to_operand_aliasing={{}: (5, {})} | custom-call | flops 2000000000 | bytes 3670016 | tf_op jit(solution)/shard_map/pallas_call | solution.py:65
  115.6 0.8 shard_map.80
  (51 shorter events, 1.5 us)
Async XLA Ops:
  0.6 17.1 %all-to-all-start = ((bf16[8,28,8,128]{3,2,1,0:T(8,128)(2,1)}), bf16[8,28,8,128]{3,2,1,0:T(8,128)(2,1)S(1)}, u32[]{:S(2)}, u32[]{:S(2)}) async-start(bf16[8,28,8,128]{3,2,1,0:T(8,128)(2,1)} %bitcast.39), calls=%async_computation | async-start | bytes 917504 | tf_op jit(solution)/shard_map/all_to_all | solution.py:91
  37.0 5.8 %collective-permute-start = (bf16[1,8,28,8,128]{4,3,2,1,0:T(8,128)(2,1)S(1)}, bf16[1,8,28,8,128]{4,3,2,1,0:T(8,128)(2,1)S(1)}, u32[]{:S(2)}, u32[]{:S(2)}) collective-permute-start(bf16[1,8,28,8,128]{4,3,2,1,0:T(8,128)(2,1)S(1)} %fusion), channel_id=1, source_target_pairs={{0,1},{1,0},{2,3},{3,2},{4,5},{5,4},{6,7},{7,6},{8,9},{9,8},{10,11... | collective-permute-start | bytes 1376264 | tf_op jit(solution)/shard_map/ppermute | solution.py:24
  41.2 8.3 %collective-permute-start.1 = (bf16[1,8,14,8,128]{4,3,2,1,0:T(8,128)(2,1)S(1)}, bf16[1,8,14,8,128]{4,3,2,1,0:T(8,128)(2,1)S(1)}, u32[]{:S(2)}, u32[]{:S(2)}) collective-permute-start(bf16[1,8,14,8,128]{4,3,2,1,0:T(8,128)(2,1)S(1)} %get-tuple-element.102), channel_id=1, source_target_pairs={{0,16},{1,17},{2,18},{3,19},{4,20},{5,21},{6,22},{7,23},{8,24},{9,... | collective-permute-start | bytes 688136 | tf_op jit(solution)/shard_map/ppermute | solution.py:24
  41.7 36.1 %collective-permute-start.10 = (bf16[1,8,14,8,128]{4,3,2,1,0:T(8,128)(2,1)S(1)}, bf16[1,8,14,8,128]{4,3,2,1,0:T(8,128)(2,1)S(1)}, u32[]{:S(2)}, u32[]{:S(2)}) collective-permute-start(bf16[1,8,14,8,128]{4,3,2,1,0:T(8,128)(2,1)S(1)} %get-tuple-element.101), channel_id=1, source_target_pairs={{0,16},{1,17},{2,18},{3,19},{4,20},{5,21},{6,22},{7,23},{8,24},{9,... | collective-permute-start | bytes 688136 | tf_op jit(solution)/shard_map/ppermute | solution.py:24
  42.9 16.0 %collective-permute-start.2 = (bf16[2,8,28,8,128]{4,3,2,1,0:T(8,128)(2,1)S(1)}, bf16[2,8,28,8,128]{4,3,2,1,0:T(8,128)(2,1)S(1)}, u32[]{:S(2)}, u32[]{:S(2)}) collective-permute-start(bf16[2,8,28,8,128]{4,3,2,1,0:T(8,128)(2,1)S(1)} %get-tuple-element.56.refs_0_), channel_id=1, source_target_pairs={{0,2},{1,15},{2,4},{3,1},{4,6},{5,3},{6,8},{7,5},{8,10},{9,7},{10,... | collective-permute-start | bytes 2752520 | tf_op jit(solution)/shard_map/ppermute | solution.py:24
  49.5 1.6 %collective-permute-start.3 = (bf16[1,8,14,8,128]{4,3,2,1,0:T(8,128)(2,1)S(1)}, bf16[1,8,14,8,128]{4,3,2,1,0:T(8,128)(2,1)S(1)}, u32[]{:S(2)}, u32[]{:S(2)}) collective-permute-start(bf16[1,8,14,8,128]{4,3,2,1,0:T(8,128)(2,1)S(1)} %get-tuple-element.58), channel_id=1, source_target_pairs={{0,1},{1,0},{2,3},{3,2},{4,5},{5,4},{6,7},{7,6},{8,9},{9,8},{10,11... | collective-permute-start | bytes 688136 | tf_op jit(solution)/shard_map/ppermute | solution.py:24
  51.2 12.7 %collective-permute-start.4 = (bf16[2,8,14,8,128]{4,3,2,1,0:T(8,128)(2,1)S(1)}, bf16[2,8,14,8,128]{4,3,2,1,0:T(8,128)(2,1)S(1)}, u32[]{:S(2)}, u32[]{:S(2)}) collective-permute-start(bf16[2,8,14,8,128]{4,3,2,1,0:T(8,128)(2,1)S(1)} %constant_dynamic-update-slice_fusion.refs_0_), channel_id=1, source_target_pairs={{0,2},{1,15},{2,4},{3,1},{4,6},{5,3},{6,8},{7,5},{8,10},{9,7},{10,... | collective-permute-start | bytes 1376264 | tf_op jit(solution)/shard_map/ppermute | solution.py:24
  58.9 16.3 %collective-permute-start.5 = (bf16[2,8,28,8,128]{4,3,2,1,0:T(8,128)(2,1)S(1)}, bf16[2,8,28,8,128]{4,3,2,1,0:T(8,128)(2,1)S(1)}, u32[]{:S(2)}, u32[]{:S(2)}) collective-permute-start(bf16[2,8,28,8,128]{4,3,2,1,0:T(8,128)(2,1)S(1)} %get-tuple-element.61.refs_0_), channel_id=1, source_target_pairs={{0,2},{1,15},{2,4},{3,1},{4,6},{5,3},{6,8},{7,5},{8,10},{9,7},{10,... | collective-permute-start | bytes 2752520 | tf_op jit(solution)/shard_map/ppermute | solution.py:24
  62.0 13.1 %collective-permute-start.7 = (bf16[2,8,28,8,128]{4,3,2,1,0:T(8,128)(2,1)S(1)}, bf16[2,8,28,8,128]{4,3,2,1,0:T(8,128)(2,1)S(1)}, u32[]{:S(2)}, u32[]{:S(2)}) collective-permute-start(bf16[2,8,28,8,128]{4,3,2,1,0:T(8,128)(2,1)S(1)} %get-tuple-element.61.refs_0_), channel_id=1, source_target_pairs={{0,1},{1,0},{2,3},{3,2},{4,5},{5,4},{6,7},{7,6},{8,9},{9,8},{10,11... | collective-permute-start | bytes 2752520 | tf_op jit(solution)/shard_map/ppermute | solution.py:24
  62.1 11.8 %collective-permute-start.6 = (bf16[2,8,14,8,128]{4,3,2,1,0:T(8,128)(2,1)S(1)}, bf16[2,8,14,8,128]{4,3,2,1,0:T(8,128)(2,1)S(1)}, u32[]{:S(2)}, u32[]{:S(2)}) collective-permute-start(bf16[2,8,14,8,128]{4,3,2,1,0:T(8,128)(2,1)S(1)} %slice.32), channel_id=1, source_target_pairs={{0,16},{1,17},{2,18},{3,19},{4,20},{5,21},{6,22},{7,23},{8,24},{9,... | collective-permute-start | bytes 1376264 | tf_op jit(solution)/shard_map/ppermute | solution.py:24
  63.8 14.7 %collective-permute-start.8 = (bf16[2,8,14,8,128]{4,3,2,1,0:T(8,128)(2,1)S(1)}, bf16[2,8,14,8,128]{4,3,2,1,0:T(8,128)(2,1)S(1)}, u32[]{:S(2)}, u32[]{:S(2)}) collective-permute-start(bf16[2,8,14,8,128]{4,3,2,1,0:T(8,128)(2,1)S(1)} %get-tuple-element.64.refs_0_), channel_id=1, source_target_pairs={{0,2},{1,15},{2,4},{3,1},{4,6},{5,3},{6,8},{7,5},{8,10},{9,7},{10,... | collective-permute-start | bytes 1376264 | tf_op jit(solution)/shard_map/ppermute | solution.py:24
  73.9 6.5 %collective-permute-start.9 = (bf16[2,8,14,8,128]{4,3,2,1,0:T(8,128)(2,1)S(1)}, bf16[2,8,14,8,128]{4,3,2,1,0:T(8,128)(2,1)S(1)}, u32[]{:S(2)}, u32[]{:S(2)}) collective-permute-start(bf16[2,8,14,8,128]{4,3,2,1,0:T(8,128)(2,1)S(1)} %get-tuple-element.64.refs_0_), channel_id=1, source_target_pairs={{0,1},{1,0},{2,3},{3,2},{4,5},{5,4},{6,7},{7,6},{8,9},{9,8},{10,11... | collective-permute-start | bytes 1376264 | tf_op jit(solution)/shard_map/ppermute | solution.py:24
  75.2 15.7 %collective-permute-start.11 = (bf16[2,8,28,8,128]{4,3,2,1,0:T(8,128)(2,1)S(1)}, bf16[2,8,28,8,128]{4,3,2,1,0:T(8,128)(2,1)S(1)}, u32[]{:S(2)}, u32[]{:S(2)}) collective-permute-start(bf16[2,8,28,8,128]{4,3,2,1,0:T(8,128)(2,1)S(1)} %get-tuple-element.67.refs_0_), channel_id=1, source_target_pairs={{0,2},{1,15},{2,4},{3,1},{4,6},{5,3},{6,8},{7,5},{8,10},{9,7},{10,... | collective-permute-start | bytes 2752520 | tf_op jit(solution)/shard_map/ppermute | solution.py:24
  76.9 14.0 %collective-permute-start.13 = (bf16[2,8,28,8,128]{4,3,2,1,0:T(8,128)(2,1)S(1)}, bf16[2,8,28,8,128]{4,3,2,1,0:T(8,128)(2,1)S(1)}, u32[]{:S(2)}, u32[]{:S(2)}) collective-permute-start(bf16[2,8,28,8,128]{4,3,2,1,0:T(8,128)(2,1)S(1)} %get-tuple-element.67.refs_0_), channel_id=1, source_target_pairs={{0,1},{1,0},{2,3},{3,2},{4,5},{5,4},{6,7},{7,6},{8,9},{9,8},{10,11... | collective-permute-start | bytes 2752520 | tf_op jit(solution)/shard_map/ppermute | solution.py:24
  77.8 11.7 %collective-permute-start.12 = (bf16[2,8,14,8,128]{4,3,2,1,0:T(8,128)(2,1)S(1)}, bf16[2,8,14,8,128]{4,3,2,1,0:T(8,128)(2,1)S(1)}, u32[]{:S(2)}, u32[]{:S(2)}) collective-permute-start(bf16[2,8,14,8,128]{4,3,2,1,0:T(8,128)(2,1)S(1)} %slice.35), channel_id=1, source_target_pairs={{0,16},{1,17},{2,18},{3,19},{4,20},{5,21},{6,22},{7,23},{8,24},{9,... | collective-permute-start | bytes 1376264 | tf_op jit(solution)/shard_map/ppermute | solution.py:24
  78.6 12.3 %collective-permute-start.14 = (bf16[2,8,14,8,128]{4,3,2,1,0:T(8,128)(2,1)S(1)}, bf16[2,8,14,8,128]{4,3,2,1,0:T(8,128)(2,1)S(1)}, u32[]{:S(2)}, u32[]{:S(2)}) collective-permute-start(bf16[2,8,14,8,128]{4,3,2,1,0:T(8,128)(2,1)S(1)} %get-tuple-element.68.refs_1_), channel_id=1, source_target_pairs={{0,1},{1,0},{2,3},{3,2},{4,5},{5,4},{6,7},{7,6},{8,9},{9,8},{10,11... | collective-permute-start | bytes 1376264 | tf_op jit(solution)/shard_map/ppermute | solution.py:24
  80.5 14.2 %collective-permute-start.15 = (bf16[2,8,14,8,128]{4,3,2,1,0:T(8,128)(2,1)S(1)}, bf16[2,8,14,8,128]{4,3,2,1,0:T(8,128)(2,1)S(1)}, u32[]{:S(2)}, u32[]{:S(2)}) collective-permute-start(bf16[2,8,14,8,128]{4,3,2,1,0:T(8,128)(2,1)S(1)} %get-tuple-element.72.refs_0_), channel_id=1, source_target_pairs={{0,2},{1,15},{2,4},{3,1},{4,6},{5,3},{6,8},{7,5},{8,10},{9,7},{10,... | collective-permute-start | bytes 1376264 | tf_op jit(solution)/shard_map/ppermute | solution.py:24
  89.5 5.7 %collective-permute-start.16 = (bf16[2,8,14,8,128]{4,3,2,1,0:T(8,128)(2,1)S(1)}, bf16[2,8,14,8,128]{4,3,2,1,0:T(8,128)(2,1)S(1)}, u32[]{:S(2)}, u32[]{:S(2)}) collective-permute-start(bf16[2,8,14,8,128]{4,3,2,1,0:T(8,128)(2,1)S(1)} %get-tuple-element.72.refs_0_), channel_id=1, source_target_pairs={{0,1},{1,0},{2,3},{3,2},{4,5},{5,4},{6,7},{7,6},{8,9},{9,8},{10,11... | collective-permute-start | bytes 1376264 | tf_op jit(solution)/shard_map/ppermute | solution.py:24
  90.8 3.3 %collective-permute-start.17 = (bf16[1,8,14,8,128]{4,3,2,1,0:T(8,128)(2,1)S(1)}, bf16[1,8,14,8,128]{4,3,2,1,0:T(8,128)(2,1)S(1)}, u32[]{:S(2)}, u32[]{:S(2)}) collective-permute-start(bf16[1,8,14,8,128]{4,3,2,1,0:T(8,128)(2,1)S(1)} %get-tuple-element.74.refs_2_), channel_id=1, source_target_pairs={{0,1},{1,0},{2,3},{3,2},{4,5},{5,4},{6,7},{7,6},{8,9},{9,8},{10,11... | collective-permute-start | bytes 688136 | tf_op jit(solution)/shard_map/ppermute | solution.py:24
  90.9 15.0 %collective-permute-start.20 = (bf16[2,8,28,8,128]{4,3,2,1,0:T(8,128)(2,1)S(1)}, bf16[2,8,28,8,128]{4,3,2,1,0:T(8,128)(2,1)S(1)}, u32[]{:S(2)}, u32[]{:S(2)}) collective-permute-start(bf16[2,8,28,8,128]{4,3,2,1,0:T(8,128)(2,1)S(1)} %get-tuple-element.77.refs_0_), channel_id=1, source_target_pairs={{0,1},{1,0},{2,3},{3,2},{4,5},{5,4},{6,7},{7,6},{8,9},{9,8},{10,11... | collective-permute-start | bytes 2752520 | tf_op jit(solution)/shard_map/ppermute | solution.py:24
  91.5 7.6 %collective-permute-start.18 = (bf16[1,8,28,8,128]{4,3,2,1,0:T(8,128)(2,1)S(1)}, bf16[1,8,28,8,128]{4,3,2,1,0:T(8,128)(2,1)S(1)}, u32[]{:S(2)}, u32[]{:S(2)}) collective-permute-start(bf16[1,8,28,8,128]{4,3,2,1,0:T(8,128)(2,1)S(1)} %slice.36), channel_id=1, source_target_pairs={{0,2},{1,15},{2,4},{3,1},{4,6},{5,3},{6,8},{7,5},{8,10},{9,7},{10,... | collective-permute-start | bytes 1376264 | tf_op jit(solution)/shard_map/ppermute | solution.py:24
  94.2 11.8 %collective-permute-start.19 = (bf16[2,8,14,8,128]{4,3,2,1,0:T(8,128)(2,1)S(1)}, bf16[2,8,14,8,128]{4,3,2,1,0:T(8,128)(2,1)S(1)}, u32[]{:S(2)}, u32[]{:S(2)}) collective-permute-start(bf16[2,8,14,8,128]{4,3,2,1,0:T(8,128)(2,1)S(1)} %slice.37), channel_id=1, source_target_pairs={{0,16},{1,17},{2,18},{3,19},{4,20},{5,21},{6,22},{7,23},{8,24},{9,... | collective-permute-start | bytes 1376264 | tf_op jit(solution)/shard_map/ppermute | solution.py:24
  94.7 11.3 %collective-permute-start.21 = (bf16[2,8,14,8,128]{4,3,2,1,0:T(8,128)(2,1)S(1)}, bf16[2,8,14,8,128]{4,3,2,1,0:T(8,128)(2,1)S(1)}, u32[]{:S(2)}, u32[]{:S(2)}) collective-permute-start(bf16[2,8,14,8,128]{4,3,2,1,0:T(8,128)(2,1)S(1)} %get-tuple-element.78.refs_1_), channel_id=1, source_target_pairs={{0,1},{1,0},{2,3},{3,2},{4,5},{5,4},{6,7},{7,6},{8,9},{9,8},{10,11... | collective-permute-start | bytes 1376264 | tf_op jit(solution)/shard_map/ppermute | solution.py:24
  95.2 13.1 %collective-permute-start.23 = (bf16[2,8,14,8,128]{4,3,2,1,0:T(8,128)(2,1)S(1)}, bf16[2,8,14,8,128]{4,3,2,1,0:T(8,128)(2,1)S(1)}, u32[]{:S(2)}, u32[]{:S(2)}) collective-permute-start(bf16[2,8,14,8,128]{4,3,2,1,0:T(8,128)(2,1)S(1)} %get-tuple-element.83.refs_0_), channel_id=1, source_target_pairs={{0,1},{1,0},{2,3},{3,2},{4,5},{5,4},{6,7},{7,6},{8,9},{9,8},{10,11... | collective-permute-start | bytes 1376264 | tf_op jit(solution)/shard_map/ppermute | solution.py:24
  99.1 9.2 %collective-permute-start.22 = (bf16[1,8,14,8,128]{4,3,2,1,0:T(8,128)(2,1)S(1)}, bf16[1,8,14,8,128]{4,3,2,1,0:T(8,128)(2,1)S(1)}, u32[]{:S(2)}, u32[]{:S(2)}) collective-permute-start(bf16[1,8,14,8,128]{4,3,2,1,0:T(8,128)(2,1)S(1)} %slice.38), channel_id=1, source_target_pairs={{0,2},{1,15},{2,4},{3,1},{4,6},{5,3},{6,8},{7,5},{8,10},{9,7},{10,... | collective-permute-start | bytes 688136 | tf_op jit(solution)/shard_map/ppermute | solution.py:24
  106.0 7.0 %collective-permute-start.26 = (bf16[1,8,28,8,128]{4,3,2,1,0:T(8,128)(2,1)S(1)}, bf16[1,8,28,8,128]{4,3,2,1,0:T(8,128)(2,1)S(1)}, u32[]{:S(2)}, u32[]{:S(2)}) collective-permute-start(bf16[1,8,28,8,128]{4,3,2,1,0:T(8,128)(2,1)S(1)} %get-tuple-element.89.refs_0_), channel_id=1, source_target_pairs={{0,1},{1,0},{2,3},{3,2},{4,5},{5,4},{6,7},{7,6},{8,9},{9,8},{10,11... | collective-permute-start | bytes 1376264 | tf_op jit(solution)/shard_map/ppermute | solution.py:24
  106.1 6.9 %collective-permute-start.25 = (bf16[1,8,14,8,128]{4,3,2,1,0:T(8,128)(2,1)S(1)}, bf16[1,8,14,8,128]{4,3,2,1,0:T(8,128)(2,1)S(1)}, u32[]{:S(2)}, u32[]{:S(2)}) collective-permute-start(bf16[1,8,14,8,128]{4,3,2,1,0:T(8,128)(2,1)S(1)} %slice.39), channel_id=1, source_target_pairs={{0,16},{1,17},{2,18},{3,19},{4,20},{5,21},{6,22},{7,23},{8,24},{9,... | collective-permute-start | bytes 688136 | tf_op jit(solution)/shard_map/ppermute | solution.py:24
  106.6 6.4 %collective-permute-start.27 = (bf16[2,8,14,8,128]{4,3,2,1,0:T(8,128)(2,1)S(1)}, bf16[2,8,14,8,128]{4,3,2,1,0:T(8,128)(2,1)S(1)}, u32[]{:S(2)}, u32[]{:S(2)}) collective-permute-start(bf16[2,8,14,8,128]{4,3,2,1,0:T(8,128)(2,1)S(1)} %get-tuple-element.90.refs_1_), channel_id=1, source_target_pairs={{0,1},{1,0},{2,3},{3,2},{4,5},{5,4},{6,7},{7,6},{8,9},{9,8},{10,11... | collective-permute-start | bytes 1376264 | tf_op jit(solution)/shard_map/ppermute | solution.py:24
  108.3 7.2 %collective-permute-start.24 = (bf16[1,8,14,8,128]{4,3,2,1,0:T(8,128)(2,1)S(1)}, bf16[1,8,14,8,128]{4,3,2,1,0:T(8,128)(2,1)S(1)}, u32[]{:S(2)}, u32[]{:S(2)}) collective-permute-start(bf16[1,8,14,8,128]{4,3,2,1,0:T(8,128)(2,1)S(1)} %get-tuple-element.87.refs_0_), channel_id=1, source_target_pairs={{0,1},{1,0},{2,3},{3,2},{4,5},{5,4},{6,7},{7,6},{8,9},{9,8},{10,11... | collective-permute-start | bytes 688136 | tf_op jit(solution)/shard_map/ppermute | solution.py:24
  113.0 2.6 %collective-permute-start.28 = (bf16[1,8,14,8,128]{4,3,2,1,0:T(8,128)(2,1)S(1)}, bf16[1,8,14,8,128]{4,3,2,1,0:T(8,128)(2,1)S(1)}, u32[]{:S(2)}, u32[]{:S(2)}) collective-permute-start(bf16[1,8,14,8,128]{4,3,2,1,0:T(8,128)(2,1)S(1)} %get-tuple-element.94.refs_2_), channel_id=1, source_target_pairs={{0,1},{1,0},{2,3},{3,2},{4,5},{5,4},{6,7},{7,6},{8,9},{9,8},{10,11... | collective-permute-start | bytes 688136 | tf_op jit(solution)/shard_map/ppermute | solution.py:24

commit v3 on v2

--- a/solution.py
+++ b/solution.py
@@ -9,7 +9,6 @@
 RUNS, SLOTS, CORES = 2, 8, 2
 TILE = (8, 128)
 GATE_FLOPS, PLACE_FLOPS = 6_000_000_000, 2_000_000_000
-SPLIT = 14
 
 
 def coords(index):
@@ -37,24 +36,18 @@
 
 
 def place(out, groups, shape):
-    arrays = [array for array, *_ in groups]
+    arrays = [array for array, _ in groups]
     through = [] if out is None else [out]
-    blocks = [
-        (at, lead, where, first, tiles)
-        for at, (_, targets, first, tiles) in enumerate(groups)
-        for lead, where in enumerate(targets)
-    ]
+    blocks = [(at, lead, where) for at, (_, targets) in enumerate(groups) for lead, where in enumerate(targets)]
 
     def kernel(*refs):
-        held, result, sems = refs[: len(arrays)], refs[-2], refs[-1]
+        result, sems = refs[-2:]
         own_run, own_slot, own_core = coords(lax.axis_index("fsdp"))
         copies = []
-        for number, (at, lead, (run, hops, core, came), first, tiles) in enumerate(blocks):
+        for number, (at, lead, (run, hops, kind, came)) in enumerate(blocks):
             receiver = (own_core + came) % CORES
-            block = fsdp_index(own_run + run, own_slot + (2 * receiver - 1) * hops, receiver + core)
-            copies.append(
-                pltpu.make_async_copy(held[at].at[lead], result.at[block, :, pl.ds(first, tiles)], sems.at[number])
-            )
+            block = fsdp_index(own_run + run, own_slot + (2 * receiver - 1) * hops, receiver + kind)
+            copies.append(pltpu.make_async_copy(refs[at].at[lead], result.at[block], sems.at[number]))
         for copy in copies:
             copy.start()
         for copy in copies:
@@ -123,70 +116,65 @@
     )(token, *arrays)
 
 
-def gather(own, head, rest, outer_all, momentum_new, shape):
-    width, split = own.shape[1], head.shape[1]
-
-    def group(array, hops, came=0, run=0, first=0):
-        targets = [(run, hops, core, came) for core in range(array.shape[0])]
-        return array, targets, first, array.shape[2]
-
-    def head_of(array):
-        return array[:, :, :split]
-
-    def q(array, hops, came=0):
-        return group(array, hops, came, 1, split)
-
-    def y(array, hops, came=0):
-        return group(array, hops, came, 1)
-
-    own, head, rest = own[None], head[None], rest[None]
-    beside = swap_run(rest)
+def gather(own, outer_all, momentum_new, shape):
+    def rows(array, hops, kinds=(0,), came=0, run=0):
+        return array, [(run, hops, kind, came) for kind in kinds]
+
+    own = own[None]
+    q0 = swap_run(own)
     p0 = jnp.concatenate([own, swap_core(own)])
     token, p0 = gate(jnp.zeros(TILE, jnp.float32), p0)
     p1 = along_slots(p0)
     token, outer_all, momentum_new = write(token, outer_all, momentum_new)
 
-    token, beside = gate(token, beside)
-    q0 = jnp.concatenate([beside, swap_core(beside)])
-    q1 = along_slots(q0)
-    out = place(None, [group(p0, 0)], shape)
+    token, q0 = gate(token, q0)
+    q1, cq0 = along_slots(q0), swap_core(q0)
+    out = place(None, [rows(p0, 0, (0, 1))], shape)
 
     token, out, p1 = gate(token, out, p1)
-    p2, y1, cp1 = along_slots(p1), swap_run(head_of(p1)), swap_core(p1)
-    out = place(out, [q(q0, 0)], shape)
-
-    token, out, q1 = gate(token, out, q1)
-    q2, cq1, y0 = along_slots(q1), swap_core(q1), swap_run(head)
-    out = place(out, [group(p1, 1)], shape)
-
-    token, out, p2, y1, cp1 = gate(token, out, p2, y1, cp1)
-    p3, y2, cp2, cy1 = along_slots(p2), swap_run(head_of(p2)), swap_core(p2), swap_core(y1)
-    out = place(out, [q(q1, 1)], shape)
-
-    token, out, q2, cq1, y0 = gate(token, out, q2, cq1, y0)
-    q3, cq2, cy0 = along_slots(q2), swap_core(q2), swap_core(y0)
-    out = place(out, [group(p2, 2), y(y1, 1), group(cp1, 1, 1)], shape)
-
-    token, out, p3, y2, cp2, cy1 = gate(token, out, p3, y2, cp2, cy1)
-    p4, y3, cp3, cy2 = along_slots(p3[:1]), swap_run(head_of(p3)), swap_core(p3), swap_core(y2)
-    out = place(out, [q(q2, 2), q(cq1, 1, 1), y(y0, 0)], shape)
-
-    token, out, q3, cq2, cy0 = gate(token, out, q3, cq2, cy0)
-    q4, cq3 = along_slots(q3[:1]), swap_core(q3)
-    out = place(out, [group(p3, 3), y(y2, 2), group(cp2, 2, 1), y(cy1, 1, 1)], shape)
-
-    token, out, p4, y3, cp3, cy2 = gate(token, out, p4, y3, cp3, cy2)
-    y4, cp4, cy3 = swap_run(head_of(p4)), swap_core(p4), swap_core(y3)
-    out = place(out, [q(q3, 3), q(cq2, 2, 1), y(cy0, 0, 1)], shape)
+    p2, y1, cp1 = along_slots(p1), swap_run(p1[1:]), swap_core(p1)
+    out = place(out, [rows(q0, 0, run=1)], shape)
+
+    token, out, q1, cq0 = gate(token, out, q1, cq0)
+    q2, cq1 = along_slots(q1), swap_core(q1)
+    out = place(out, [rows(p1, 1, (0, 1))], shape)
+
+    token, out, p2, cp1, y1 = gate(token, out, p2, cp1, y1)
+    p3, y2, cp2, cy1 = along_slots(p2), swap_run(p2[1:]), swap_core(p2), swap_core(y1)
+    out = place(out, [rows(q1, 1, run=1), rows(cq0, 0, came=1, run=1)], shape)
+
+    token, out, q2, cq1 = gate(token, out, q2, cq1)
+    q3, cq2 = along_slots(q2), swap_core(q2)
+    out = place(out, [rows(p2, 2, (0, 1)), rows(cp1, 1, (0, 1), 1), rows(y1, 1, (1,), run=1)], shape)
+
+    token, out, p3, cp2, y2 = gate(token, out, p3, cp2, y2)
+    p4, y3, cp3, cy2 = along_slots(p3[:1]), swap_run(p3[1:]), swap_core(p3), swap_core(y2)
+    out = place(out, [rows(q2, 2, run=1), rows(cq1, 1, came=1, run=1), rows(cy1, 1, (1,), 1, 1)], shape)
+
+    token, out, q3, cq2 = gate(token, out, q3, cq2)
+    q4, cq3 = along_slots(q3), swap_core(q3)
+    out = place(out, [rows(p3, 3, (0, 1)), rows(cp2, 2, (0, 1), 1), rows(y2, 2, (1,), run=1)], shape)
+
+    token, out, p4, cp3, y3 = gate(token, out, p4, cp3, y3)
+    cp4, cy3 = swap_core(p4), swap_core(y3)
+    out = place(out, [rows(q3, 3, run=1), rows(cq2, 2, came=1, run=1), rows(cy2, 2, (1,), 1, 1)], shape)
 
     token, out, q4, cq3 = gate(token, out, q4, cq3)
     cq4 = swap_core(q4)
-    out = place(out, [group(p4, 4), y(y3, 3), group(cp3, 3, 1), y(cy2, 2, 1)], shape)
-
-    token, out, y4, cp4, cy3 = gate(token, out, y4, cp4, cy3)
-    cy4 = swap_core(y4)
-    out = place(out, [q(q4, 4), q(cq3, 3, 1), y(y4, 4), group(cp4, 4, 1), y(cy3, 3, 1)], shape)
-    return place(out, [q(cq4, 4, 1), y(cy4, 4, 1)], shape), outer_all, momentum_new
+    out = place(
+        out,
+        [
+            rows(p4, 4),
+            rows(cp3, 3, (0, 1), 1),
+            rows(y3, 3, (1,), run=1),
+            rows(cq3, 3, came=1, run=1),
+            rows(cp4, 4, came=1),
+            rows(cy3, 3, (1,), 1, 1),
+            rows(q4, 4, run=1),
+        ],
+        shape,
+    )
+    return place(out, [rows(cq4, 4, came=1, run=1)], shape), outer_all, momentum_new
 
 
 def body(inner, outer, momentum):
@@ -207,11 +195,8 @@
     outer_new, momentum_new = step(inner, own_outer, momentum)
     outer_all = to_all(outer_new)
 
-    def blend(at):
-        return (0.5 * inner[:, at].astype(jnp.float32) + 0.5 * outer_all[:, at]).astype(jnp.bfloat16)
-
-    parts = blend(slice(0, None)), blend(slice(0, SPLIT)), blend(slice(SPLIT, None))
-    out, outer_all, momentum_new = gather(*parts, outer_all, momentum_new, shape)
+    blended = (0.5 * inner.astype(jnp.float32) + 0.5 * outer_all).astype(jnp.bfloat16)
+    out, outer_all, momentum_new = gather(blended, outer_all, momentum_new, shape)
     gathered = out.transpose(0, 3, 1, 2, 4).reshape(1, -1, REPLICAS * width * TILE[1])
     return rows(outer_all), rows(momentum_new[None]), gathered
 

time: 117 us -> 109 us (0.932)
  waiting for transfers between devices: 34.5 us -> 30.4 us
  starting transfers between devices: 47.1 us -> 45.5 us
    ppermute x29 -> x25, waiting for transfers between devices: 24.9 us -> 20.8 us  [move(): lax.ppermute(array, 'fsdp', [(i, fsdp_index(*target(*coords(i)))) for i i...]
    ppermute x29 -> x25, starting transfers between devices: 39.7 us -> 38 us  [move(): lax.ppermute(array, 'fsdp', [(i, fsdp_index(*target(*coords(i)))) for i i...]
    pallas_call x11 -> x10, Pallas kernels: 12.1 us -> 11.3 us  [place(): pl.pallas_call(kernel, out_shape=jax.ShapeDtypeStruct(shape, jnp.bfloat16...]
  transfers between devices with their start and end apart: 30 -> 26, of which waited for: 10 -> 10; matrix products, arithmetic and copies ran while one was open for 1% -> 0% of each run, Pallas kernels for 11% -> 11%
where the time goes in v3:
time: 109 us
  starting transfers between devices  45.5 us (42%)
  waiting for transfers between devices  30.4 us (28%)
  blocking collectives  17 us (16%)
  Pallas kernels  12.3 us (11%)
  other arithmetic  2.31 us (2%)
    ppermute x25, starting transfers between devices, move(): lax.ppermute(array, 'fsdp', [(i, fsdp_index(*target(*coords(i)))) for i i...  38 us
    ppermute x25, waiting for transfers between devices, move(): lax.ppermute(array, 'fsdp', [(i, fsdp_index(*target(*coords(i)))) for i i...  20.8 us
    all_to_all x1, blocking collectives, to_all(): lax.all_to_all(jnp.broadcast_to(array, (REPLICAS,) + array.shape), 'repli...  17 us
    pallas_call x10, Pallas kernels, place(): pl.pallas_call(kernel, out_shape=jax.ShapeDtypeStruct(shape, jnp.bfloat16...  11.3 us
    all_to_all x1, waiting for transfers between devices, step(): terms = lax.all_to_all(inner, 'replica', 0, 0).astype(jnp.float32)  9.63 us
    all_to_all x1, starting transfers between devices, step(): terms = lax.all_to_all(inner, 'replica', 0, 0).astype(jnp.float32)  7.49 us
  transfers between devices with their start and end apart: 26, of which 10 were waited for; matrix products, arithmetic and copies ran while one was open for 0% of the time, Pallas kernels for 11%

profile of v3, /device:TPU:1, one launch (start us, length us, event | category | flops | bytes accessed | tf_op | source)
XLA Modules:
  0.0 108.7 jit_solution(318687959699433695)
XLA Ops:
  0.6 7.5 %all-to-all-start = ((bf16[8,28,8,128]{3,2,1,0:T(8,128)(2,1)}), bf16[8,28,8,128]{3,2,1,0:T(8,128)(2,1)S(1)}, u32[]{:S(2)}, u32[]{:S(2)}) async-start(bf16[8,28,8,128]{3,2,1,0:T(8,128)(2,1)} %bitcast.35), calls=%async_computation | async-start | bytes 917504 | tf_op jit(solution)/shard_map/all_to_all | solution.py:84
  8.1 9.6 %all-to-all-done = bf16[8,28,8,128]{3,2,1,0:T(8,128)(2,1)S(1)} async-done(((bf16[8,28,8,128]{3,2,1,0:T(8,128)(2,1)}), bf16[8,28,8,128]{3,2,1,0:T(8,128)(2,1)S(1)}, u32[]{:S(2)}, u32[]{:S(2)}) %all-to-all-start) | async-done | bytes 458784 | tf_op jit(solution)/shard_map/all_to_all | solution.py:84
  17.8 0.1 convert_reduce_fusion
  17.8 1.0 bitcast_subtract_fusion
  18.8 0.1 broadcast_in_dim.13
  18.9 17.0 %all_to_all.10.refs_1_ = f32[8,28,8,128]{3,2,1,0:T(8,128)S(1)} all-to-all(f32[8,28,8,128]{3,2,1,0:T(8,128)S(1)} %broadcast_in_dim.13), channel_id=1, replica_groups=mesh['replica'=8,'fsdp'=32] {'replica'}, dimensions={0} | all-to-all | bytes 1835008 | tf_op jit(solution)/shard_map/all_to_all | solution.py:91
  35.9 1.2 %fusion = bf16[1,8,28,8,128]{4,3,2,1,0:T(8,128)(2,1)S(1)} fusion(f32[8,28,8,128]{3,2,1,0:T(8,128)S(1)} %all_to_all.10.refs_1_, bf16[8,28,8,128]{3,2,1,0:T(8,128)(2,1)} %bitcast.36), kind=kLoop, calls=%fused_computation.3 | loop fusion | flops 917504 | bytes 1835008 | tf_op jit(solution)/shard_map/broadcast_in_dim | solution.py:123
  37.0 3.0 %collective-permute-start = (bf16[1,8,28,8,128]{4,3,2,1,0:T(8,128)(2,1)S(1)}, bf16[1,8,28,8,128]{4,3,2,1,0:T(8,128)(2,1)S(1)}, u32[]{:S(2)}, u32[]{:S(2)}) collective-permute-start(bf16[1,8,28,8,128]{4,3,2,1,0:T(8,128)(2,1)S(1)} %fusion), channel_id=1, source_target_pairs={{0,1},{1,0},{2,3},{3,2},{4,5},{5,4},{6,7},{7,6},{8,9},{9,8},{10,11... | collective-permute-start | bytes 1376264 | tf_op jit(solution)/shard_map/ppermute | solution.py:23
  40.1 0.4 collective-permute-start.1
  40.5 1.0 collective-permute-done
  41.5 0.1 pad_maximum_fusion.refs_1_
  41.6 5.7 %collective-permute-start.2 = (bf16[2,8,28,8,128]{4,3,2,1,0:T(8,128)(2,1)S(1)}, bf16[2,8,28,8,128]{4,3,2,1,0:T(8,128)(2,1)S(1)}, u32[]{:S(2)}, u32[]{:S(2)}) collective-permute-start(bf16[2,8,28,8,128]{4,3,2,1,0:T(8,128)(2,1)S(1)} %get-tuple-element.48.refs_0_), channel_id=1, source_target_pairs={{0,2},{1,15},{2,4},{3,1},{4,6},{5,3},{6,8},{7,5},{8,10},{9,7},{10,... | collective-permute-start | bytes 2752520 | tf_op jit(solution)/shard_map/ppermute | solution.py:23
  47.3 1.0 shard_map.59
  48.3 3.9 %collective-permute-done.1.refs_1_ = bf16[1,8,28,8,128]{4,3,2,1,0:T(8,128)(2,1)S(1)} collective-permute-done((bf16[1,8,28,8,128]{4,3,2,1,0:T(8,128)(2,1)S(1)}, bf16[1,8,28,8,128]{4,3,2,1,0:T(8,128)(2,1)S(1)}, u32[]{:S(2)}, u32[]{:S(2)}) %collective-permute-start.1) | collective-permute-done | bytes 458784 | tf_op jit(solution)/shard_map/ppermute | solution.py:23
  52.2 5.6 %collective-permute-start.3 = (bf16[1,8,28,8,128]{4,3,2,1,0:T(8,128)(2,1)S(1)}, bf16[1,8,28,8,128]{4,3,2,1,0:T(8,128)(2,1)S(1)}, u32[]{:S(2)}, u32[]{:S(2)}) collective-permute-start(bf16[1,8,28,8,128]{4,3,2,1,0:T(8,128)(2,1)S(1)} %get-tuple-element.50.refs_0_), channel_id=1, source_target_pairs={{0,2},{1,15},{2,4},{3,1},{4,6},{5,3},{6,8},{7,5},{8,10},{9,7},{10,... | collective-permute-start | bytes 1376264 | tf_op jit(solution)/shard_map/ppermute | solution.py:23
  57.7 0.9 shard_map.61.refs_1_
  58.7 2.0 %collective-permute-start.5 = (bf16[2,8,28,8,128]{4,3,2,1,0:T(8,128)(2,1)S(1)}, bf16[2,8,28,8,128]{4,3,2,1,0:T(8,128)(2,1)S(1)}, u32[]{:S(2)}, u32[]{:S(2)}) collective-permute-start(bf16[2,8,28,8,128]{4,3,2,1,0:T(8,128)(2,1)S(1)} %get-tuple-element.53.refs_0_), channel_id=1, source_target_pairs={{0,2},{1,15},{2,4},{3,1},{4,6},{5,3},{6,8},{7,5},{8,10},{9,7},{10,... | collective-permute-start | bytes 2752520 | tf_op jit(solution)/shard_map/ppermute | solution.py:23
  60.8 0.5 collective-permute-start.7
  61.3 0.8 shard_map.63.refs_1_
  62.0 1.1 %collective-permute-done.3.refs_2_ = bf16[1,8,28,8,128]{4,3,2,1,0:T(8,128)(2,1)S(1)} collective-permute-done((bf16[1,8,28,8,128]{4,3,2,1,0:T(8,128)(2,1)S(1)}, bf16[1,8,28,8,128]{4,3,2,1,0:T(8,128)(2,1)S(1)}, u32[]{:S(2)}, u32[]{:S(2)}) %collective-permute-start.3) | collective-permute-done | bytes 458784 | tf_op jit(solution)/shard_map/ppermute | solution.py:23
  63.2 3.1 %collective-permute-start.8 = (bf16[1,8,28,8,128]{4,3,2,1,0:T(8,128)(2,1)S(1)}, bf16[1,8,28,8,128]{4,3,2,1,0:T(8,128)(2,1)S(1)}, u32[]{:S(2)}, u32[]{:S(2)}) collective-permute-start(bf16[1,8,28,8,128]{4,3,2,1,0:T(8,128)(2,1)S(1)} %get-tuple-element.56.refs_0_), channel_id=1, source_target_pairs={{0,2},{1,15},{2,4},{3,1},{4,6},{5,3},{6,8},{7,5},{8,10},{9,7},{10,... | collective-permute-start | bytes 1376264 | tf_op jit(solution)/shard_map/ppermute | solution.py:23
  66.3 0.9 shard_map.65.refs_1_
  67.2 5.2 %collective-permute-done.7.refs_4_ = bf16[1,8,28,8,128]{4,3,2,1,0:T(8,128)(2,1)S(1)} collective-permute-done((bf16[1,8,28,8,128]{4,3,2,1,0:T(8,128)(2,1)S(1)}, bf16[1,8,28,8,128]{4,3,2,1,0:T(8,128)(2,1)S(1)}, u32[]{:S(2)}, u32[]{:S(2)}) %collective-permute-start.7) | collective-permute-done | bytes 458784 | tf_op jit(solution)/shard_map/ppermute | solution.py:23
  72.4 0.6 collective-permute-done.5.refs_2_
  73.0 3.1 %collective-permute-start.10 = (bf16[2,8,28,8,128]{4,3,2,1,0:T(8,128)(2,1)S(1)}, bf16[2,8,28,8,128]{4,3,2,1,0:T(8,128)(2,1)S(1)}, u32[]{:S(2)}, u32[]{:S(2)}) collective-permute-start(bf16[2,8,28,8,128]{4,3,2,1,0:T(8,128)(2,1)S(1)} %get-tuple-element.60.refs_0_), channel_id=1, source_target_pairs={{0,2},{1,15},{2,4},{3,1},{4,6},{5,3},{6,8},{7,5},{8,10},{9,7},{10,... | collective-permute-start | bytes 2752520 | tf_op jit(solution)/shard_map/ppermute | solution.py:23
  76.2 0.5 collective-permute-start.12
  76.6 0.9 shard_map.67.refs_1_
  77.6 0.3 collective-permute-done.8.refs_2_
  77.9 2.2 %collective-permute-start.13 = (bf16[1,8,28,8,128]{4,3,2,1,0:T(8,128)(2,1)S(1)}, bf16[1,8,28,8,128]{4,3,2,1,0:T(8,128)(2,1)S(1)}, u32[]{:S(2)}, u32[]{:S(2)}) collective-permute-start(bf16[1,8,28,8,128]{4,3,2,1,0:T(8,128)(2,1)S(1)} %get-tuple-element.62.refs_2_), channel_id=1, source_target_pairs={{0,1},{1,0},{2,3},{3,2},{4,5},{5,4},{6,7},{7,6},{8,9},{9,8},{10,11... | collective-permute-start | bytes 1376264 | tf_op jit(solution)/shard_map/ppermute | solution.py:23
  80.1 1.7 %collective-permute-start.14 = (bf16[1,8,28,8,128]{4,3,2,1,0:T(8,128)(2,1)S(1)}, bf16[1,8,28,8,128]{4,3,2,1,0:T(8,128)(2,1)S(1)}, u32[]{:S(2)}, u32[]{:S(2)}) collective-permute-start(bf16[1,8,28,8,128]{4,3,2,1,0:T(8,128)(2,1)S(1)} %get-tuple-element.65.refs_0_), channel_id=1, source_target_pairs={{0,2},{1,15},{2,4},{3,1},{4,6},{5,3},{6,8},{7,5},{8,10},{9,7},{10,... | collective-permute-start | bytes 1376264 | tf_op jit(solution)/shard_map/ppermute | solution.py:23
  81.8 1.4 %shard_map.69.refs_1_ = bf16[32,8,28,8,128]{4,3,2,1,0:T(8,128)(2,1)} custom-call(bf16[2,8,28,8,128]{4,3,2,1,0:T(8,128)(2,1)S(1)} %get-tuple-element.60.refs_0_, bf16[2,8,28,8,128]{4,3,2,1,0:T(8,128)(2,1)S(1)} %get-tuple-element.61.refs_1_, bf16[1,8,28,8,128]{4,3,2,1,0:T(8,128)(2,1)S(1)} %get-tuple-element.62.refs_2_, ...), custom_call_target="tpu_custom_call", output_to_operand_aliasing={{}: (3, {})} | custom-call | flops 2000000000 | bytes 4587520 | tf_op jit(solution)/shard_map/pallas_call | solution.py:58
  83.3 4.6 %collective-permute-done.12.refs_4_ = bf16[1,8,28,8,128]{4,3,2,1,0:T(8,128)(2,1)S(1)} collective-permute-done((bf16[1,8,28,8,128]{4,3,2,1,0:T(8,128)(2,1)S(1)}, bf16[1,8,28,8,128]{4,3,2,1,0:T(8,128)(2,1)S(1)}, u32[]{:S(2)}, u32[]{:S(2)}) %collective-permute-start.12) | collective-permute-done | bytes 458784 | tf_op jit(solution)/shard_map/ppermute | solution.py:23
  87.8 1.4 %collective-permute-start.15 = (bf16[1,8,28,8,128]{4,3,2,1,0:T(8,128)(2,1)S(1)}, bf16[1,8,28,8,128]{4,3,2,1,0:T(8,128)(2,1)S(1)}, u32[]{:S(2)}, u32[]{:S(2)}) collective-permute-start(bf16[1,8,28,8,128]{4,3,2,1,0:T(8,128)(2,1)S(1)} %get-tuple-element.65.refs_0_), channel_id=1, source_target_pairs={{0,1},{1,0},{2,3},{3,2},{4,5},{5,4},{6,7},{7,6},{8,9},{9,8},{10,11... | collective-permute-start | bytes 1376264 | tf_op jit(solution)/shard_map/ppermute | solution.py:23
  89.2 0.7 collective-permute-start.17
  90.0 2.0 %collective-permute-start.16 = (bf16[1,8,28,8,128]{4,3,2,1,0:T(8,128)(2,1)S(1)}, bf16[1,8,28,8,128]{4,3,2,1,0:T(8,128)(2,1)S(1)}, u32[]{:S(2)}, u32[]{:S(2)}) collective-permute-start(bf16[1,8,28,8,128]{4,3,2,1,0:T(8,128)(2,1)S(1)} %get-tuple-element.86), channel_id=1, source_target_pairs={{0,2},{1,15},{2,4},{3,1},{4,6},{5,3},{6,8},{7,5},{8,10},{9,7},{10,... | collective-permute-start | bytes 1376264 | tf_op jit(solution)/shard_map/ppermute | solution.py:23
  92.0 0.4 collective-permute-start.18
  92.4 1.1 %shard_map.71.refs_1_ = bf16[32,8,28,8,128]{4,3,2,1,0:T(8,128)(2,1)} custom-call(bf16[1,8,28,8,128]{4,3,2,1,0:T(8,128)(2,1)S(1)} %get-tuple-element.65.refs_0_, bf16[1,8,28,8,128]{4,3,2,1,0:T(8,128)(2,1)S(1)} %get-tuple-element.66.refs_1_, bf16[1,8,28,8,128]{4,3,2,1,0:T(8,128)(2,1)S(1)} %collective-permute-done.13.refs_2_, ...), custom_call_target="tpu_custom_call", output_to_operand_aliasing={{}: (3, {})} | custom-call | flops 2000000000 | bytes 2752512 | tf_op jit(solution)/shard_map/pallas_call | solution.py:58
  93.5 1.3 %collective-permute-start.19 = (bf16[1,8,28,8,128]{4,3,2,1,0:T(8,128)(2,1)S(1)}, bf16[1,8,28,8,128]{4,3,2,1,0:T(8,128)(2,1)S(1)}, u32[]{:S(2)}, u32[]{:S(2)}) collective-permute-start(bf16[1,8,28,8,128]{4,3,2,1,0:T(8,128)(2,1)S(1)} %get-tuple-element.71.refs_2_), channel_id=1, source_target_pairs={{0,1},{1,0},{2,3},{3,2},{4,5},{5,4},{6,7},{7,6},{8,9},{9,8},{10,11... | collective-permute-start | bytes 1376264 | tf_op jit(solution)/shard_map/ppermute | solution.py:23
  94.8 1.7 %collective-permute-start.20 = (bf16[1,8,28,8,128]{4,3,2,1,0:T(8,128)(2,1)S(1)}, bf16[1,8,28,8,128]{4,3,2,1,0:T(8,128)(2,1)S(1)}, u32[]{:S(2)}, u32[]{:S(2)}) collective-permute-start(bf16[1,8,28,8,128]{4,3,2,1,0:T(8,128)(2,1)S(1)} %get-tuple-element.74.refs_0_), channel_id=1, source_target_pairs={{0,2},{1,15},{2,4},{3,1},{4,6},{5,3},{6,8},{7,5},{8,10},{9,7},{10,... | collective-permute-start | bytes 1376264 | tf_op jit(solution)/shard_map/ppermute | solution.py:23
  96.6 1.4 %shard_map.73.refs_1_ = bf16[32,8,28,8,128]{4,3,2,1,0:T(8,128)(2,1)} custom-call(bf16[2,8,28,8,128]{4,3,2,1,0:T(8,128)(2,1)S(1)} %get-tuple-element.69.refs_0_, bf16[2,8,28,8,128]{4,3,2,1,0:T(8,128)(2,1)S(1)} %get-tuple-element.70.refs_1_, bf16[1,8,28,8,128]{4,3,2,1,0:T(8,128)(2,1)S(1)} %get-tuple-element.71.refs_2_, ...), custom_call_target="tpu_custom_call", output_to_operand_aliasing={{}: (3, {})} | custom-call | flops 2000000000 | bytes 4587520 | tf_op jit(solution)/shard_map/pallas_call | solution.py:58
  98.0 1.9 %collective-permute-start.21 = (bf16[1,8,28,8,128]{4,3,2,1,0:T(8,128)(2,1)S(1)}, bf16[1,8,28,8,128]{4,3,2,1,0:T(8,128)(2,1)S(1)}, u32[]{:S(2)}, u32[]{:S(2)}) collective-permute-start(bf16[1,8,28,8,128]{4,3,2,1,0:T(8,128)(2,1)S(1)} %get-tuple-element.74.refs_0_), channel_id=1, source_target_pairs={{0,1},{1,0},{2,3},{3,2},{4,5},{5,4},{6,7},{7,6},{8,9},{9,8},{10,11... | collective-permute-start | bytes 1376264 | tf_op jit(solution)/shard_map/ppermute | solution.py:23
  99.9 3.4 %collective-permute-done.18.refs_4_ = bf16[1,8,28,8,128]{4,3,2,1,0:T(8,128)(2,1)S(1)} collective-permute-done((bf16[1,8,28,8,128]{4,3,2,1,0:T(8,128)(2,1)S(1)}, bf16[1,8,28,8,128]{4,3,2,1,0:T(8,128)(2,1)S(1)}, u32[]{:S(2)}, u32[]{:S(2)}) %collective-permute-start.18) | collective-permute-done | bytes 458784 | tf_op jit(solution)/shard_map/ppermute | solution.py:23
  103.4 0.5 collective-permute-start.24
  103.9 1.1 %shard_map.75.refs_1_ = bf16[32,8,28,8,128]{4,3,2,1,0:T(8,128)(2,1)} custom-call(bf16[1,8,28,8,128]{4,3,2,1,0:T(8,128)(2,1)S(1)} %get-tuple-element.74.refs_0_, bf16[1,8,28,8,128]{4,3,2,1,0:T(8,128)(2,1)S(1)} %get-tuple-element.75.refs_1_, bf16[1,8,28,8,128]{4,3,2,1,0:T(8,128)(2,1)S(1)} %collective-permute-done.19.refs_2_, ...), custom_call_target="tpu_custom_call", output_to_operand_aliasing={{}: (3, {})} | custom-call | flops 2000000000 | bytes 2752512 | tf_op jit(solution)/shard_map/pallas_call | solution.py:58
  105.0 0.2 collective-permute-start.22
  105.2 0.6 collective-permute-done.24.refs_5_
  105.8 1.9 %shard_map.77.refs_1_ = bf16[32,8,28,8,128]{4,3,2,1,0:T(8,128)(2,1)} custom-call(bf16[1,8,28,8,128]{4,3,2,1,0:T(8,128)(2,1)S(1)} %get-tuple-element.78.refs_0_, bf16[2,8,28,8,128]{4,3,2,1,0:T(8,128)(2,1)S(1)} %get-tuple-element.79.refs_1_, bf16[1,8,28,8,128]{4,3,2,1,0:T(8,128)(2,1)S(1)} %get-tuple-element.80.refs_2_, ...), custom_call_target="tpu_custom_call", output_to_operand_aliasing={{}: (7, {})} | custom-call | flops 2000000000 | bytes 7340032 | tf_op jit(solution)/shard_map/pallas_call | solution.py:58
  107.8 0.8 shard_map.78
  (35 shorter events, 0.2 us)
Async XLA Ops:
  0.6 17.1 %all-to-all-start = ((bf16[8,28,8,128]{3,2,1,0:T(8,128)(2,1)}), bf16[8,28,8,128]{3,2,1,0:T(8,128)(2,1)S(1)}, u32[]{:S(2)}, u32[]{:S(2)}) async-start(bf16[8,28,8,128]{3,2,1,0:T(8,128)(2,1)} %bitcast.35), calls=%async_computation | async-start | bytes 917504 | tf_op jit(solution)/shard_map/all_to_all | solution.py:84
  37.0 4.5 %collective-permute-start = (bf16[1,8,28,8,128]{4,3,2,1,0:T(8,128)(2,1)S(1)}, bf16[1,8,28,8,128]{4,3,2,1,0:T(8,128)(2,1)S(1)}, u32[]{:S(2)}, u32[]{:S(2)}) collective-permute-start(bf16[1,8,28,8,128]{4,3,2,1,0:T(8,128)(2,1)S(1)} %fusion), channel_id=1, source_target_pairs={{0,1},{1,0},{2,3},{3,2},{4,5},{5,4},{6,7},{7,6},{8,9},{9,8},{10,11... | collective-permute-start | bytes 1376264 | tf_op jit(solution)/shard_map/ppermute | solution.py:23
  40.1 12.1 %collective-permute-start.1 = (bf16[1,8,28,8,128]{4,3,2,1,0:T(8,128)(2,1)S(1)}, bf16[1,8,28,8,128]{4,3,2,1,0:T(8,128)(2,1)S(1)}, u32[]{:S(2)}, u32[]{:S(2)}) collective-permute-start(bf16[1,8,28,8,128]{4,3,2,1,0:T(8,128)(2,1)S(1)} %fusion), channel_id=1, source_target_pairs={{0,16},{1,17},{2,18},{3,19},{4,20},{5,21},{6,22},{7,23},{8,24},{9,... | collective-permute-start | bytes 1376264 | tf_op jit(solution)/shard_map/ppermute | solution.py:23
  41.6 17.1 %collective-permute-start.2 = (bf16[2,8,28,8,128]{4,3,2,1,0:T(8,128)(2,1)S(1)}, bf16[2,8,28,8,128]{4,3,2,1,0:T(8,128)(2,1)S(1)}, u32[]{:S(2)}, u32[]{:S(2)}) collective-permute-start(bf16[2,8,28,8,128]{4,3,2,1,0:T(8,128)(2,1)S(1)} %get-tuple-element.48.refs_0_), channel_id=1, source_target_pairs={{0,2},{1,15},{2,4},{3,1},{4,6},{5,3},{6,8},{7,5},{8,10},{9,7},{10,... | collective-permute-start | bytes 2752520 | tf_op jit(solution)/shard_map/ppermute | solution.py:23
  52.2 11.0 %collective-permute-start.3 = (bf16[1,8,28,8,128]{4,3,2,1,0:T(8,128)(2,1)S(1)}, bf16[1,8,28,8,128]{4,3,2,1,0:T(8,128)(2,1)S(1)}, u32[]{:S(2)}, u32[]{:S(2)}) collective-permute-start(bf16[1,8,28,8,128]{4,3,2,1,0:T(8,128)(2,1)S(1)} %get-tuple-element.50.refs_0_), channel_id=1, source_target_pairs={{0,2},{1,15},{2,4},{3,1},{4,6},{5,3},{6,8},{7,5},{8,10},{9,7},{10,... | collective-permute-start | bytes 1376264 | tf_op jit(solution)/shard_map/ppermute | solution.py:23
  57.7 5.4 %collective-permute-start.4 = (bf16[1,8,28,8,128]{4,3,2,1,0:T(8,128)(2,1)S(1)}, bf16[1,8,28,8,128]{4,3,2,1,0:T(8,128)(2,1)S(1)}, u32[]{:S(2)}, u32[]{:S(2)}) collective-permute-start(bf16[1,8,28,8,128]{4,3,2,1,0:T(8,128)(2,1)S(1)} %get-tuple-element.50.refs_0_), channel_id=1, source_target_pairs={{0,1},{1,0},{2,3},{3,2},{4,5},{5,4},{6,7},{7,6},{8,9},{9,8},{10,11... | collective-permute-start | bytes 1376264 | tf_op jit(solution)/shard_map/ppermute | solution.py:23
  58.7 14.3 %collective-permute-start.5 = (bf16[2,8,28,8,128]{4,3,2,1,0:T(8,128)(2,1)S(1)}, bf16[2,8,28,8,128]{4,3,2,1,0:T(8,128)(2,1)S(1)}, u32[]{:S(2)}, u32[]{:S(2)}) collective-permute-start(bf16[2,8,28,8,128]{4,3,2,1,0:T(8,128)(2,1)S(1)} %get-tuple-element.53.refs_0_), channel_id=1, source_target_pairs={{0,2},{1,15},{2,4},{3,1},{4,6},{5,3},{6,8},{7,5},{8,10},{9,7},{10,... | collective-permute-start | bytes 2752520 | tf_op jit(solution)/shard_map/ppermute | solution.py:23
  60.7 12.3 %collective-permute-start.6 = (bf16[2,8,28,8,128]{4,3,2,1,0:T(8,128)(2,1)S(1)}, bf16[2,8,28,8,128]{4,3,2,1,0:T(8,128)(2,1)S(1)}, u32[]{:S(2)}, u32[]{:S(2)}) collective-permute-start(bf16[2,8,28,8,128]{4,3,2,1,0:T(8,128)(2,1)S(1)} %get-tuple-element.53.refs_0_), channel_id=1, source_target_pairs={{0,1},{1,0},{2,3},{3,2},{4,5},{5,4},{6,7},{7,6},{8,9},{9,8},{10,11... | collective-permute-start | bytes 2752520 | tf_op jit(solution)/shard_map/ppermute | solution.py:23
  60.8 11.7 %collective-permute-start.7 = (bf16[1,8,28,8,128]{4,3,2,1,0:T(8,128)(2,1)S(1)}, bf16[1,8,28,8,128]{4,3,2,1,0:T(8,128)(2,1)S(1)}, u32[]{:S(2)}, u32[]{:S(2)}) collective-permute-start(bf16[1,8,28,8,128]{4,3,2,1,0:T(8,128)(2,1)S(1)} %slice.12), channel_id=1, source_target_pairs={{0,16},{1,17},{2,18},{3,19},{4,20},{5,21},{6,22},{7,23},{8,24},{9,... | collective-permute-start | bytes 1376264 | tf_op jit(solution)/shard_map/ppermute | solution.py:23
  63.2 14.7 %collective-permute-start.8 = (bf16[1,8,28,8,128]{4,3,2,1,0:T(8,128)(2,1)S(1)}, bf16[1,8,28,8,128]{4,3,2,1,0:T(8,128)(2,1)S(1)}, u32[]{:S(2)}, u32[]{:S(2)}) collective-permute-start(bf16[1,8,28,8,128]{4,3,2,1,0:T(8,128)(2,1)S(1)} %get-tuple-element.56.refs_0_), channel_id=1, source_target_pairs={{0,2},{1,15},{2,4},{3,1},{4,6},{5,3},{6,8},{7,5},{8,10},{9,7},{10,... | collective-permute-start | bytes 1376264 | tf_op jit(solution)/shard_map/ppermute | solution.py:23
  66.3 13.8 %collective-permute-start.9 = (bf16[1,8,28,8,128]{4,3,2,1,0:T(8,128)(2,1)S(1)}, bf16[1,8,28,8,128]{4,3,2,1,0:T(8,128)(2,1)S(1)}, u32[]{:S(2)}, u32[]{:S(2)}) collective-permute-start(bf16[1,8,28,8,128]{4,3,2,1,0:T(8,128)(2,1)S(1)} %get-tuple-element.56.refs_0_), channel_id=1, source_target_pairs={{0,1},{1,0},{2,3},{3,2},{4,5},{5,4},{6,7},{7,6},{8,9},{9,8},{10,11... | collective-permute-start | bytes 1376264 | tf_op jit(solution)/shard_map/ppermute | solution.py:23
  73.0 16.2 %collective-permute-start.10 = (bf16[2,8,28,8,128]{4,3,2,1,0:T(8,128)(2,1)S(1)}, bf16[2,8,28,8,128]{4,3,2,1,0:T(8,128)(2,1)S(1)}, u32[]{:S(2)}, u32[]{:S(2)}) collective-permute-start(bf16[2,8,28,8,128]{4,3,2,1,0:T(8,128)(2,1)S(1)} %get-tuple-element.60.refs_0_), channel_id=1, source_target_pairs={{0,2},{1,15},{2,4},{3,1},{4,6},{5,3},{6,8},{7,5},{8,10},{9,7},{10,... | collective-permute-start | bytes 2752520 | tf_op jit(solution)/shard_map/ppermute | solution.py:23
  76.1 13.1 %collective-permute-start.11 = (bf16[2,8,28,8,128]{4,3,2,1,0:T(8,128)(2,1)S(1)}, bf16[2,8,28,8,128]{4,3,2,1,0:T(8,128)(2,1)S(1)}, u32[]{:S(2)}, u32[]{:S(2)}) collective-permute-start(bf16[2,8,28,8,128]{4,3,2,1,0:T(8,128)(2,1)S(1)} %get-tuple-element.60.refs_0_), channel_id=1, source_target_pairs={{0,1},{1,0},{2,3},{3,2},{4,5},{5,4},{6,7},{7,6},{8,9},{9,8},{10,11... | collective-permute-start | bytes 2752520 | tf_op jit(solution)/shard_map/ppermute | solution.py:23
  76.2 11.7 %collective-permute-start.12 = (bf16[1,8,28,8,128]{4,3,2,1,0:T(8,128)(2,1)S(1)}, bf16[1,8,28,8,128]{4,3,2,1,0:T(8,128)(2,1)S(1)}, u32[]{:S(2)}, u32[]{:S(2)}) collective-permute-start(bf16[1,8,28,8,128]{4,3,2,1,0:T(8,128)(2,1)S(1)} %slice.13), channel_id=1, source_target_pairs={{0,16},{1,17},{2,18},{3,19},{4,20},{5,21},{6,22},{7,23},{8,24},{9,... | collective-permute-start | bytes 1376264 | tf_op jit(solution)/shard_map/ppermute | solution.py:23
  77.9 14.1 %collective-permute-start.13 = (bf16[1,8,28,8,128]{4,3,2,1,0:T(8,128)(2,1)S(1)}, bf16[1,8,28,8,128]{4,3,2,1,0:T(8,128)(2,1)S(1)}, u32[]{:S(2)}, u32[]{:S(2)}) collective-permute-start(bf16[1,8,28,8,128]{4,3,2,1,0:T(8,128)(2,1)S(1)} %get-tuple-element.62.refs_2_), channel_id=1, source_target_pairs={{0,1},{1,0},{2,3},{3,2},{4,5},{5,4},{6,7},{7,6},{8,9},{9,8},{10,11... | collective-permute-start | bytes 1376264 | tf_op jit(solution)/shard_map/ppermute | solution.py:23
  80.1 13.4 %collective-permute-start.14 = (bf16[1,8,28,8,128]{4,3,2,1,0:T(8,128)(2,1)S(1)}, bf16[1,8,28,8,128]{4,3,2,1,0:T(8,128)(2,1)S(1)}, u32[]{:S(2)}, u32[]{:S(2)}) collective-permute-start(bf16[1,8,28,8,128]{4,3,2,1,0:T(8,128)(2,1)S(1)} %get-tuple-element.65.refs_0_), channel_id=1, source_target_pairs={{0,2},{1,15},{2,4},{3,1},{4,6},{5,3},{6,8},{7,5},{8,10},{9,7},{10,... | collective-permute-start | bytes 1376264 | tf_op jit(solution)/shard_map/ppermute | solution.py:23
  87.8 7.0 %collective-permute-start.15 = (bf16[1,8,28,8,128]{4,3,2,1,0:T(8,128)(2,1)S(1)}, bf16[1,8,28,8,128]{4,3,2,1,0:T(8,128)(2,1)S(1)}, u32[]{:S(2)}, u32[]{:S(2)}) collective-permute-start(bf16[1,8,28,8,128]{4,3,2,1,0:T(8,128)(2,1)S(1)} %get-tuple-element.65.refs_0_), channel_id=1, source_target_pairs={{0,1},{1,0},{2,3},{3,2},{4,5},{5,4},{6,7},{7,6},{8,9},{9,8},{10,11... | collective-permute-start | bytes 1376264 | tf_op jit(solution)/shard_map/ppermute | solution.py:23
  89.2 14.2 %collective-permute-start.17 = (bf16[2,8,28,8,128]{4,3,2,1,0:T(8,128)(2,1)S(1)}, bf16[2,8,28,8,128]{4,3,2,1,0:T(8,128)(2,1)S(1)}, u32[]{:S(2)}, u32[]{:S(2)}) collective-permute-start(bf16[2,8,28,8,128]{4,3,2,1,0:T(8,128)(2,1)S(1)} %get-tuple-element.69.refs_0_), channel_id=1, source_target_pairs={{0,1},{1,0},{2,3},{3,2},{4,5},{5,4},{6,7},{7,6},{8,9},{9,8},{10,11... | collective-permute-start | bytes 2752520 | tf_op jit(solution)/shard_map/ppermute | solution.py:23
  90.0 8.0 %collective-permute-start.16 = (bf16[1,8,28,8,128]{4,3,2,1,0:T(8,128)(2,1)S(1)}, bf16[1,8,28,8,128]{4,3,2,1,0:T(8,128)(2,1)S(1)}, u32[]{:S(2)}, u32[]{:S(2)}) collective-permute-start(bf16[1,8,28,8,128]{4,3,2,1,0:T(8,128)(2,1)S(1)} %get-tuple-element.86), channel_id=1, source_target_pairs={{0,2},{1,15},{2,4},{3,1},{4,6},{5,3},{6,8},{7,5},{8,10},{9,7},{10,... | collective-permute-start | bytes 1376264 | tf_op jit(solution)/shard_map/ppermute | solution.py:23
  92.0 11.4 %collective-permute-start.18 = (bf16[1,8,28,8,128]{4,3,2,1,0:T(8,128)(2,1)S(1)}, bf16[1,8,28,8,128]{4,3,2,1,0:T(8,128)(2,1)S(1)}, u32[]{:S(2)}, u32[]{:S(2)}) collective-permute-start(bf16[1,8,28,8,128]{4,3,2,1,0:T(8,128)(2,1)S(1)} %get-tuple-element.85), channel_id=1, source_target_pairs={{0,16},{1,17},{2,18},{3,19},{4,20},{5,21},{6,22},{7,23},{8,24},{9,... | collective-permute-start | bytes 1376264 | tf_op jit(solution)/shard_map/ppermute | solution.py:23
  93.5 10.4 %collective-permute-start.19 = (bf16[1,8,28,8,128]{4,3,2,1,0:T(8,128)(2,1)S(1)}, bf16[1,8,28,8,128]{4,3,2,1,0:T(8,128)(2,1)S(1)}, u32[]{:S(2)}, u32[]{:S(2)}) collective-permute-start(bf16[1,8,28,8,128]{4,3,2,1,0:T(8,128)(2,1)S(1)} %get-tuple-element.71.refs_2_), channel_id=1, source_target_pairs={{0,1},{1,0},{2,3},{3,2},{4,5},{5,4},{6,7},{7,6},{8,9},{9,8},{10,11... | collective-permute-start | bytes 1376264 | tf_op jit(solution)/shard_map/ppermute | solution.py:23
  94.8 10.1 %collective-permute-start.20 = (bf16[1,8,28,8,128]{4,3,2,1,0:T(8,128)(2,1)S(1)}, bf16[1,8,28,8,128]{4,3,2,1,0:T(8,128)(2,1)S(1)}, u32[]{:S(2)}, u32[]{:S(2)}) collective-permute-start(bf16[1,8,28,8,128]{4,3,2,1,0:T(8,128)(2,1)S(1)} %get-tuple-element.74.refs_0_), channel_id=1, source_target_pairs={{0,2},{1,15},{2,4},{3,1},{4,6},{5,3},{6,8},{7,5},{8,10},{9,7},{10,... | collective-permute-start | bytes 1376264 | tf_op jit(solution)/shard_map/ppermute | solution.py:23
  98.0 7.0 %collective-permute-start.21 = (bf16[1,8,28,8,128]{4,3,2,1,0:T(8,128)(2,1)S(1)}, bf16[1,8,28,8,128]{4,3,2,1,0:T(8,128)(2,1)S(1)}, u32[]{:S(2)}, u32[]{:S(2)}) collective-permute-start(bf16[1,8,28,8,128]{4,3,2,1,0:T(8,128)(2,1)S(1)} %get-tuple-element.74.refs_0_), channel_id=1, source_target_pairs={{0,1},{1,0},{2,3},{3,2},{4,5},{5,4},{6,7},{7,6},{8,9},{9,8},{10,11... | collective-permute-start | bytes 1376264 | tf_op jit(solution)/shard_map/ppermute | solution.py:23
  103.4 1.8 %collective-permute-start.23 = (bf16[1,8,28,8,128]{4,3,2,1,0:T(8,128)(2,1)S(1)}, bf16[1,8,28,8,128]{4,3,2,1,0:T(8,128)(2,1)S(1)}, u32[]{:S(2)}, u32[]{:S(2)}) collective-permute-start(bf16[1,8,28,8,128]{4,3,2,1,0:T(8,128)(2,1)S(1)} %get-tuple-element.78.refs_0_), channel_id=1, source_target_pairs={{0,1},{1,0},{2,3},{3,2},{4,5},{5,4},{6,7},{7,6},{8,9},{9,8},{10,11... | collective-permute-start | bytes 1376264 | tf_op jit(solution)/shard_map/ppermute | solution.py:23
  103.4 2.5 %collective-permute-start.24 = (bf16[1,8,28,8,128]{4,3,2,1,0:T(8,128)(2,1)S(1)}, bf16[1,8,28,8,128]{4,3,2,1,0:T(8,128)(2,1)S(1)}, u32[]{:S(2)}, u32[]{:S(2)}) collective-permute-start(bf16[1,8,28,8,128]{4,3,2,1,0:T(8,128)(2,1)S(1)} %get-tuple-element.80.refs_2_), channel_id=1, source_target_pairs={{0,1},{1,0},{2,3},{3,2},{4,5},{5,4},{6,7},{7,6},{8,9},{9,8},{10,11... | collective-permute-start | bytes 1376264 | tf_op jit(solution)/shard_map/ppermute | solution.py:23
  105.0 2.7 %collective-permute-start.22 = (bf16[1,8,28,8,128]{4,3,2,1,0:T(8,128)(2,1)S(1)}, bf16[1,8,28,8,128]{4,3,2,1,0:T(8,128)(2,1)S(1)}, u32[]{:S(2)}, u32[]{:S(2)}) collective-permute-start(bf16[1,8,28,8,128]{4,3,2,1,0:T(8,128)(2,1)S(1)} %get-tuple-element.77.refs_6_), channel_id=1, source_target_pairs={{0,1},{1,0},{2,3},{3,2},{4,5},{5,4},{6,7},{7,6},{8,9},{9,8},{10,11... | collective-permute-start | bytes 1376264 | tf_op jit(solution)/shard_map/ppermute | solution.py:23

commit v4 on v3

--- a/solution.py
+++ b/solution.py
@@ -121,60 +121,57 @@
         return array, [(run, hops, kind, came) for kind in kinds]
 
     own = own[None]
-    q0 = swap_run(own)
-    p0 = jnp.concatenate([own, swap_core(own)])
-    token, p0 = gate(jnp.zeros(TILE, jnp.float32), p0)
-    p1 = along_slots(p0)
+    a1, q0, other = along_slots(own), swap_run(own), swap_core(own)
+    token, other = gate(jnp.zeros(TILE, jnp.float32), other)
+    b1 = along_slots(other)
     token, outer_all, momentum_new = write(token, outer_all, momentum_new)
 
     token, q0 = gate(token, q0)
-    q1, cq0 = along_slots(q0), swap_core(q0)
-    out = place(None, [rows(p0, 0, (0, 1))], shape)
-
-    token, out, p1 = gate(token, out, p1)
-    p2, y1, cp1 = along_slots(p1), swap_run(p1[1:]), swap_core(p1)
-    out = place(out, [rows(q0, 0, run=1)], shape)
-
-    token, out, q1, cq0 = gate(token, out, q1, cq0)
-    q2, cq1 = along_slots(q1), swap_core(q1)
+    q1 = along_slots(q0)
+
+    token, a1, b1 = gate(token, a1, b1)
+    p1 = jnp.concatenate([a1, b1])
+    p2, y1, cp1 = along_slots(p1), swap_run(b1), swap_core(p1)
+    out = place(None, [rows(own, 0), rows(other, 0, (1,)), rows(q0, 0, run=1)], shape)
+
+    token, out, q1 = gate(token, out, q1)
+    q2, cq01 = along_slots(q1), swap_core(jnp.concatenate([q0, q1]))
     out = place(out, [rows(p1, 1, (0, 1))], shape)
 
     token, out, p2, cp1, y1 = gate(token, out, p2, cp1, y1)
     p3, y2, cp2, cy1 = along_slots(p2), swap_run(p2[1:]), swap_core(p2), swap_core(y1)
-    out = place(out, [rows(q1, 1, run=1), rows(cq0, 0, came=1, run=1)], shape)
-
-    token, out, q2, cq1 = gate(token, out, q2, cq1)
+    out = place(out, [rows(q1, 1, run=1)], shape)
+
+    token, out, q2, cq01 = gate(token, out, q2, cq01)
     q3, cq2 = along_slots(q2), swap_core(q2)
     out = place(out, [rows(p2, 2, (0, 1)), rows(cp1, 1, (0, 1), 1), rows(y1, 1, (1,), run=1)], shape)
 
     token, out, p3, cp2, y2 = gate(token, out, p3, cp2, y2)
     p4, y3, cp3, cy2 = along_slots(p3[:1]), swap_run(p3[1:]), swap_core(p3), swap_core(y2)
-    out = place(out, [rows(q2, 2, run=1), rows(cq1, 1, came=1, run=1), rows(cy1, 1, (1,), 1, 1)], shape)
+    out = place(out, [rows(q2, 2, run=1), (cq01, [(1, 0, 0, 1), (1, 1, 0, 1)]), rows(cy1, 1, (1,), 1, 1)], shape)
 
     token, out, q3, cq2 = gate(token, out, q3, cq2)
     q4, cq3 = along_slots(q3), swap_core(q3)
     out = place(out, [rows(p3, 3, (0, 1)), rows(cp2, 2, (0, 1), 1), rows(y2, 2, (1,), run=1)], shape)
 
-    token, out, p4, cp3, y3 = gate(token, out, p4, cp3, y3)
-    cp4, cy3 = swap_core(p4), swap_core(y3)
-    out = place(out, [rows(q3, 3, run=1), rows(cq2, 2, came=1, run=1), rows(cy2, 2, (1,), 1, 1)], shape)
-
-    token, out, q4, cq3 = gate(token, out, q4, cq3)
-    cq4 = swap_core(q4)
+    token, out, p4, cp3, y3, q4, cq3 = gate(token, out, p4, cp3, y3, q4, cq3)
+    cp4, cy3, cq4 = swap_core(p4), swap_core(y3), swap_core(q4)
     out = place(
         out,
         [
+            rows(q3, 3, run=1),
+            rows(cq2, 2, came=1, run=1),
+            rows(cy2, 2, (1,), 1, 1),
             rows(p4, 4),
             rows(cp3, 3, (0, 1), 1),
             rows(y3, 3, (1,), run=1),
             rows(cq3, 3, came=1, run=1),
-            rows(cp4, 4, came=1),
-            rows(cy3, 3, (1,), 1, 1),
             rows(q4, 4, run=1),
         ],
         shape,
     )
-    return place(out, [rows(cq4, 4, came=1, run=1)], shape), outer_all, momentum_new
+    out = place(out, [rows(cp4, 4, came=1), rows(cy3, 3, (1,), 1, 1), rows(cq4, 4, came=1, run=1)], shape)
+    return out, outer_all, momentum_new
 
 
 def body(inner, outer, momentum):

time: 109 us -> 109 us (level)
  starting transfers between devices: 45.5 us -> 47.6 us
  Pallas kernels: 12.3 us -> 11 us
    ppermute x25, starting transfers between devices: 38 us -> 40.1 us  [move(): lax.ppermute(array, 'fsdp', [(i, fsdp_index(*target(*coords(i)))) for i i...]
    pallas_call x10 -> x8, Pallas kernels: 11.3 us -> 10.1 us  [place(): pl.pallas_call(kernel, out_shape=jax.ShapeDtypeStruct(shape, jnp.bfloat16...]
  transfers between devices with their start and end apart: 26 -> 26, of which waited for: 10 -> 10; matrix products, arithmetic and copies ran while one was open for 0% -> 0% of each run, Pallas kernels for 11% -> 9%
where the time goes in v4:
time: 109 us
  starting transfers between devices  47.6 us (44%)
  waiting for transfers between devices  29.8 us (27%)
  blocking collectives  17 us (16%)
  Pallas kernels  11 us (10%)
  other arithmetic  2.31 us (2%)
    ppermute x25, starting transfers between devices, move(): lax.ppermute(array, 'fsdp', [(i, fsdp_index(*target(*coords(i)))) for i i...  40.1 us
    ppermute x25, waiting for transfers between devices, move(): lax.ppermute(array, 'fsdp', [(i, fsdp_index(*target(*coords(i)))) for i i...  20.2 us
    all_to_all x1, blocking collectives, to_all(): lax.all_to_all(jnp.broadcast_to(array, (REPLICAS,) + array.shape), 'repli...  17 us
    pallas_call x8, Pallas kernels, place(): pl.pallas_call(kernel, out_shape=jax.ShapeDtypeStruct(shape, jnp.bfloat16...  10.1 us
    all_to_all x1, waiting for transfers between devices, step(): terms = lax.all_to_all(inner, 'replica', 0, 0).astype(jnp.float32)  9.63 us
    all_to_all x1, starting transfers between devices, step(): terms = lax.all_to_all(inner, 'replica', 0, 0).astype(jnp.float32)  7.49 us
  transfers between devices with their start and end apart: 26, of which 10 were waited for; matrix products, arithmetic and copies ran while one was open for 0% of the time, Pallas kernels for 9%

profile of v4, /device:TPU:1, one launch (start us, length us, event | category | flops | bytes accessed | tf_op | source)
XLA Modules:
  0.0 109.0 jit_solution(15605524996308032790)
XLA Ops:
  0.6 7.5 %all-to-all-start = ((bf16[8,28,8,128]{3,2,1,0:T(8,128)(2,1)}), bf16[8,28,8,128]{3,2,1,0:T(8,128)(2,1)S(1)}, u32[]{:S(2)}, u32[]{:S(2)}) async-start(bf16[8,28,8,128]{3,2,1,0:T(8,128)(2,1)} %bitcast.35), calls=%async_computation | async-start | bytes 917504 | tf_op jit(solution)/shard_map/all_to_all | solution.py:84
  8.1 9.6 %all-to-all-done = bf16[8,28,8,128]{3,2,1,0:T(8,128)(2,1)S(1)} async-done(((bf16[8,28,8,128]{3,2,1,0:T(8,128)(2,1)}), bf16[8,28,8,128]{3,2,1,0:T(8,128)(2,1)S(1)}, u32[]{:S(2)}, u32[]{:S(2)}) %all-to-all-start) | async-done | bytes 458784 | tf_op jit(solution)/shard_map/all_to_all | solution.py:84
  17.8 0.1 convert_reduce_fusion
  17.8 1.0 bitcast_subtract_fusion
  18.9 17.0 %all_to_all.10.refs_1_ = f32[8,28,8,128]{3,2,1,0:T(8,128)S(1)} all-to-all(f32[8,28,8,128]{3,2,1,0:T(8,128)S(1)} %broadcast_in_dim.13), channel_id=1, replica_groups=mesh['replica'=8,'fsdp'=32] {'replica'}, dimensions={0} | all-to-all | bytes 1835008 | tf_op jit(solution)/shard_map/all_to_all | solution.py:91
  35.9 1.2 %fusion.refs_0_ = bf16[1,8,28,8,128]{4,3,2,1,0:T(8,128)(2,1)S(1)} fusion(f32[8,28,8,128]{3,2,1,0:T(8,128)S(1)} %all_to_all.10.refs_1_, bf16[8,28,8,128]{3,2,1,0:T(8,128)(2,1)} %bitcast.36), kind=kLoop, calls=%fused_computation.3 | loop fusion | flops 917504 | bytes 1835008 | tf_op jit(solution)/shard_map/broadcast_in_dim | solution.py:123
  37.0 3.0 %collective-permute-start = (bf16[1,8,28,8,128]{4,3,2,1,0:T(8,128)(2,1)S(1)}, bf16[1,8,28,8,128]{4,3,2,1,0:T(8,128)(2,1)S(1)}, u32[]{:S(2)}, u32[]{:S(2)}) collective-permute-start(bf16[1,8,28,8,128]{4,3,2,1,0:T(8,128)(2,1)S(1)} %fusion.refs_0_), channel_id=1, source_target_pairs={{0,1},{1,0},{2,3},{3,2},{4,5},{5,4},{6,7},{7,6},{8,9},{9,8},{10,11... | collective-permute-start | bytes 1376264 | tf_op jit(solution)/shard_map/ppermute | solution.py:23
  40.1 0.4 collective-permute-start.1
  40.5 5.6 %collective-permute-start.2 = (bf16[1,8,28,8,128]{4,3,2,1,0:T(8,128)(2,1)S(1)}, bf16[1,8,28,8,128]{4,3,2,1,0:T(8,128)(2,1)S(1)}, u32[]{:S(2)}, u32[]{:S(2)}) collective-permute-start(bf16[1,8,28,8,128]{4,3,2,1,0:T(8,128)(2,1)S(1)} %fusion.refs_0_), channel_id=1, source_target_pairs={{0,2},{1,15},{2,4},{3,1},{4,6},{5,3},{6,8},{7,5},{8,10},{9,7},{10,... | collective-permute-start | bytes 1376264 | tf_op jit(solution)/shard_map/ppermute | solution.py:23
  46.1 1.0 collective-permute-start.3
  47.1 1.0 shard_map.59
  48.1 4.1 %collective-permute-done.1.refs_1_ = bf16[1,8,28,8,128]{4,3,2,1,0:T(8,128)(2,1)S(1)} collective-permute-done((bf16[1,8,28,8,128]{4,3,2,1,0:T(8,128)(2,1)S(1)}, bf16[1,8,28,8,128]{4,3,2,1,0:T(8,128)(2,1)S(1)}, u32[]{:S(2)}, u32[]{:S(2)}) %collective-permute-start.1) | collective-permute-done | bytes 458784 | tf_op jit(solution)/shard_map/ppermute | solution.py:23
  52.2 5.6 %collective-permute-start.4 = (bf16[1,8,28,8,128]{4,3,2,1,0:T(8,128)(2,1)S(1)}, bf16[1,8,28,8,128]{4,3,2,1,0:T(8,128)(2,1)S(1)}, u32[]{:S(2)}, u32[]{:S(2)}) collective-permute-start(bf16[1,8,28,8,128]{4,3,2,1,0:T(8,128)(2,1)S(1)} %get-tuple-element.47.refs_2_), channel_id=1, source_target_pairs={{0,2},{1,15},{2,4},{3,1},{4,6},{5,3},{6,8},{7,5},{8,10},{9,7},{10,... | collective-permute-start | bytes 1376264 | tf_op jit(solution)/shard_map/ppermute | solution.py:23
  57.8 0.1 constant_dynamic-update-slice_fusion.refs_0_
  57.9 1.9 %collective-permute-start.5 = (bf16[2,8,28,8,128]{4,3,2,1,0:T(8,128)(2,1)S(1)}, bf16[2,8,28,8,128]{4,3,2,1,0:T(8,128)(2,1)S(1)}, u32[]{:S(2)}, u32[]{:S(2)}) collective-permute-start(bf16[2,8,28,8,128]{4,3,2,1,0:T(8,128)(2,1)S(1)} %constant_dynamic-update-slice_fusion.refs_0_), channel_id=1, source_target_pairs={{0,2},{1,15},{2,4},{3,1},{4,6},{5,3},{6,8},{7,5},{8,10},{9,7},{10,... | collective-permute-start | bytes 2752520 | tf_op jit(solution)/shard_map/ppermute | solution.py:23
  59.7 1.1 %shard_map.62.refs_1_ = bf16[32,8,28,8,128]{4,3,2,1,0:T(8,128)(2,1)} custom-call(bf16[1,8,28,8,128]{4,3,2,1,0:T(8,128)(2,1)S(1)} %fusion.refs_0_, bf16[1,8,28,8,128]{4,3,2,1,0:T(8,128)(2,1)S(1)} %get-tuple-element.45.refs_1_, bf16[1,8,28,8,128]{4,3,2,1,0:T(8,128)(2,1)S(1)} %get-tuple-element.47.refs_2_), custom_call_target="tpu_custom_call" | custom-call | flops 2000000000 | bytes 2752512 | tf_op jit(solution)/shard_map/pallas_call | solution.py:58
  60.8 1.2 %collective-permute-start.7 = (bf16[1,8,28,8,128]{4,3,2,1,0:T(8,128)(2,1)S(1)}, bf16[1,8,28,8,128]{4,3,2,1,0:T(8,128)(2,1)S(1)}, u32[]{:S(2)}, u32[]{:S(2)}) collective-permute-start(bf16[1,8,28,8,128]{4,3,2,1,0:T(8,128)(2,1)S(1)} %get-tuple-element.50), channel_id=1, source_target_pairs={{0,16},{1,17},{2,18},{3,19},{4,20},{5,21},{6,22},{7,23},{8,24},{9,... | collective-permute-start | bytes 1376264 | tf_op jit(solution)/shard_map/ppermute | solution.py:23
  62.0 1.2 %collective-permute-done.4.refs_2_ = bf16[1,8,28,8,128]{4,3,2,1,0:T(8,128)(2,1)S(1)} collective-permute-done((bf16[1,8,28,8,128]{4,3,2,1,0:T(8,128)(2,1)S(1)}, bf16[1,8,28,8,128]{4,3,2,1,0:T(8,128)(2,1)S(1)}, u32[]{:S(2)}, u32[]{:S(2)}) %collective-permute-start.4) | collective-permute-done | bytes 458784 | tf_op jit(solution)/shard_map/ppermute | solution.py:23
  63.2 3.1 %collective-permute-start.8 = (bf16[1,8,28,8,128]{4,3,2,1,0:T(8,128)(2,1)S(1)}, bf16[1,8,28,8,128]{4,3,2,1,0:T(8,128)(2,1)S(1)}, u32[]{:S(2)}, u32[]{:S(2)}) collective-permute-start(bf16[1,8,28,8,128]{4,3,2,1,0:T(8,128)(2,1)S(1)} %get-tuple-element.53.refs_0_), channel_id=1, source_target_pairs={{0,2},{1,15},{2,4},{3,1},{4,6},{5,3},{6,8},{7,5},{8,10},{9,7},{10,... | collective-permute-start | bytes 1376264 | tf_op jit(solution)/shard_map/ppermute | solution.py:23
  66.3 0.1 pad_maximum_fusion
  66.4 0.1 collective-permute-start.9
  66.5 1.0 shard_map.64.refs_1_
  67.4 5.0 %collective-permute-done.7.refs_4_ = bf16[1,8,28,8,128]{4,3,2,1,0:T(8,128)(2,1)S(1)} collective-permute-done((bf16[1,8,28,8,128]{4,3,2,1,0:T(8,128)(2,1)S(1)}, bf16[1,8,28,8,128]{4,3,2,1,0:T(8,128)(2,1)S(1)}, u32[]{:S(2)}, u32[]{:S(2)}) %collective-permute-start.7) | collective-permute-done | bytes 458784 | tf_op jit(solution)/shard_map/ppermute | solution.py:23
  72.5 0.5 collective-permute-done.5.refs_2_
  73.0 3.1 %collective-permute-start.10 = (bf16[2,8,28,8,128]{4,3,2,1,0:T(8,128)(2,1)S(1)}, bf16[2,8,28,8,128]{4,3,2,1,0:T(8,128)(2,1)S(1)}, u32[]{:S(2)}, u32[]{:S(2)}) collective-permute-start(bf16[2,8,28,8,128]{4,3,2,1,0:T(8,128)(2,1)S(1)} %get-tuple-element.56.refs_0_), channel_id=1, source_target_pairs={{0,2},{1,15},{2,4},{3,1},{4,6},{5,3},{6,8},{7,5},{8,10},{9,7},{10,... | collective-permute-start | bytes 2752520 | tf_op jit(solution)/shard_map/ppermute | solution.py:23
  76.2 0.5 collective-permute-start.12
  76.6 0.8 shard_map.66.refs_1_
  77.4 0.5 collective-permute-done.8.refs_2_
  77.9 2.2 %collective-permute-start.13 = (bf16[1,8,28,8,128]{4,3,2,1,0:T(8,128)(2,1)S(1)}, bf16[1,8,28,8,128]{4,3,2,1,0:T(8,128)(2,1)S(1)}, u32[]{:S(2)}, u32[]{:S(2)}) collective-permute-start(bf16[1,8,28,8,128]{4,3,2,1,0:T(8,128)(2,1)S(1)} %get-tuple-element.58.refs_2_), channel_id=1, source_target_pairs={{0,1},{1,0},{2,3},{3,2},{4,5},{5,4},{6,7},{7,6},{8,9},{9,8},{10,11... | collective-permute-start | bytes 1376264 | tf_op jit(solution)/shard_map/ppermute | solution.py:23
  80.1 1.7 %collective-permute-start.14 = (bf16[1,8,28,8,128]{4,3,2,1,0:T(8,128)(2,1)S(1)}, bf16[1,8,28,8,128]{4,3,2,1,0:T(8,128)(2,1)S(1)}, u32[]{:S(2)}, u32[]{:S(2)}) collective-permute-start(bf16[1,8,28,8,128]{4,3,2,1,0:T(8,128)(2,1)S(1)} %get-tuple-element.61.refs_0_), channel_id=1, source_target_pairs={{0,2},{1,15},{2,4},{3,1},{4,6},{5,3},{6,8},{7,5},{8,10},{9,7},{10,... | collective-permute-start | bytes 1376264 | tf_op jit(solution)/shard_map/ppermute | solution.py:23
  81.8 1.4 %shard_map.68.refs_1_ = bf16[32,8,28,8,128]{4,3,2,1,0:T(8,128)(2,1)} custom-call(bf16[2,8,28,8,128]{4,3,2,1,0:T(8,128)(2,1)S(1)} %get-tuple-element.56.refs_0_, bf16[2,8,28,8,128]{4,3,2,1,0:T(8,128)(2,1)S(1)} %get-tuple-element.57.refs_1_, bf16[1,8,28,8,128]{4,3,2,1,0:T(8,128)(2,1)S(1)} %get-tuple-element.58.refs_2_, ...), custom_call_target="tpu_custom_call", output_to_operand_aliasing={{}: (3, {})} | custom-call | flops 2000000000 | bytes 4587520 | tf_op jit(solution)/shard_map/pallas_call | solution.py:58
  83.3 4.6 %collective-permute-done.12.refs_4_ = bf16[1,8,28,8,128]{4,3,2,1,0:T(8,128)(2,1)S(1)} collective-permute-done((bf16[1,8,28,8,128]{4,3,2,1,0:T(8,128)(2,1)S(1)}, bf16[1,8,28,8,128]{4,3,2,1,0:T(8,128)(2,1)S(1)}, u32[]{:S(2)}, u32[]{:S(2)}) %collective-permute-start.12) | collective-permute-done | bytes 458784 | tf_op jit(solution)/shard_map/ppermute | solution.py:23
  87.8 1.4 %collective-permute-start.15 = (bf16[1,8,28,8,128]{4,3,2,1,0:T(8,128)(2,1)S(1)}, bf16[1,8,28,8,128]{4,3,2,1,0:T(8,128)(2,1)S(1)}, u32[]{:S(2)}, u32[]{:S(2)}) collective-permute-start(bf16[1,8,28,8,128]{4,3,2,1,0:T(8,128)(2,1)S(1)} %get-tuple-element.61.refs_0_), channel_id=1, source_target_pairs={{0,1},{1,0},{2,3},{3,2},{4,5},{5,4},{6,7},{7,6},{8,9},{9,8},{10,11... | collective-permute-start | bytes 1376264 | tf_op jit(solution)/shard_map/ppermute | solution.py:23
  89.2 0.7 collective-permute-start.17
  90.0 2.0 %collective-permute-start.16 = (bf16[1,8,28,8,128]{4,3,2,1,0:T(8,128)(2,1)S(1)}, bf16[1,8,28,8,128]{4,3,2,1,0:T(8,128)(2,1)S(1)}, u32[]{:S(2)}, u32[]{:S(2)}) collective-permute-start(bf16[1,8,28,8,128]{4,3,2,1,0:T(8,128)(2,1)S(1)} %get-tuple-element.80), channel_id=1, source_target_pairs={{0,2},{1,15},{2,4},{3,1},{4,6},{5,3},{6,8},{7,5},{8,10},{9,7},{10,... | collective-permute-start | bytes 1376264 | tf_op jit(solution)/shard_map/ppermute | solution.py:23
  92.0 0.4 collective-permute-start.18
  92.4 1.3 %shard_map.70.refs_1_ = bf16[32,8,28,8,128]{4,3,2,1,0:T(8,128)(2,1)} custom-call(bf16[1,8,28,8,128]{4,3,2,1,0:T(8,128)(2,1)S(1)} %get-tuple-element.61.refs_0_, bf16[2,8,28,8,128]{4,3,2,1,0:T(8,128)(2,1)S(1)} %get-tuple-element.62.refs_1_, bf16[1,8,28,8,128]{4,3,2,1,0:T(8,128)(2,1)S(1)} %collective-permute-done.13.refs_2_, ...), custom_call_target="tpu_custom_call", output_to_operand_aliasing={{}: (3, {})} | custom-call | flops 2000000000 | bytes 3670016 | tf_op jit(solution)/shard_map/pallas_call | solution.py:58
  93.7 2.1 %collective-permute-start.19 = (bf16[1,8,28,8,128]{4,3,2,1,0:T(8,128)(2,1)S(1)}, bf16[1,8,28,8,128]{4,3,2,1,0:T(8,128)(2,1)S(1)}, u32[]{:S(2)}, u32[]{:S(2)}) collective-permute-start(bf16[1,8,28,8,128]{4,3,2,1,0:T(8,128)(2,1)S(1)} %get-tuple-element.69.refs_0_), channel_id=1, source_target_pairs={{0,2},{1,15},{2,4},{3,1},{4,6},{5,3},{6,8},{7,5},{8,10},{9,7},{10,... | collective-permute-start | bytes 1376264 | tf_op jit(solution)/shard_map/ppermute | solution.py:23
  95.8 1.4 %shard_map.72.refs_1_ = bf16[32,8,28,8,128]{4,3,2,1,0:T(8,128)(2,1)} custom-call(bf16[2,8,28,8,128]{4,3,2,1,0:T(8,128)(2,1)S(1)} %get-tuple-element.65.refs_0_, bf16[2,8,28,8,128]{4,3,2,1,0:T(8,128)(2,1)S(1)} %get-tuple-element.66.refs_1_, bf16[1,8,28,8,128]{4,3,2,1,0:T(8,128)(2,1)S(1)} %get-tuple-element.67.refs_2_, ...), custom_call_target="tpu_custom_call", output_to_operand_aliasing={{}: (3, {})} | custom-call | flops 2000000000 | bytes 4587520 | tf_op jit(solution)/shard_map/pallas_call | solution.py:58
  97.2 0.7 collective-permute-done.16.refs_2_
  97.9 2.1 %collective-permute-start.24 = (bf16[1,8,28,8,128]{4,3,2,1,0:T(8,128)(2,1)S(1)}, bf16[1,8,28,8,128]{4,3,2,1,0:T(8,128)(2,1)S(1)}, u32[]{:S(2)}, u32[]{:S(2)}) collective-permute-start(bf16[1,8,28,8,128]{4,3,2,1,0:T(8,128)(2,1)S(1)} %get-tuple-element.67.refs_2_), channel_id=1, source_target_pairs={{0,1},{1,0},{2,3},{3,2},{4,5},{5,4},{6,7},{7,6},{8,9},{9,8},{10,11... | collective-permute-start | bytes 1376264 | tf_op jit(solution)/shard_map/ppermute | solution.py:23
  99.9 3.4 %collective-permute-done.18.refs_4_ = bf16[1,8,28,8,128]{4,3,2,1,0:T(8,128)(2,1)S(1)} collective-permute-done((bf16[1,8,28,8,128]{4,3,2,1,0:T(8,128)(2,1)S(1)}, bf16[1,8,28,8,128]{4,3,2,1,0:T(8,128)(2,1)S(1)}, u32[]{:S(2)}, u32[]{:S(2)}) %collective-permute-start.18) | collective-permute-done | bytes 458784 | tf_op jit(solution)/shard_map/ppermute | solution.py:23
  103.4 1.6 %collective-permute-start.21 = (bf16[1,8,28,8,128]{4,3,2,1,0:T(8,128)(2,1)S(1)}, bf16[1,8,28,8,128]{4,3,2,1,0:T(8,128)(2,1)S(1)}, u32[]{:S(2)}, u32[]{:S(2)}) collective-permute-start(bf16[1,8,28,8,128]{4,3,2,1,0:T(8,128)(2,1)S(1)} %get-tuple-element.70.refs_3_), channel_id=1, source_target_pairs={{0,1},{1,0},{2,3},{3,2},{4,5},{5,4},{6,7},{7,6},{8,9},{9,8},{10,11... | collective-permute-start | bytes 1376264 | tf_op jit(solution)/shard_map/ppermute | solution.py:23
  105.0 0.1 collective-permute-start.22
  105.1 0.4 collective-permute-start.23
  105.5 2.1 %shard_map.74.refs_3_ = bf16[32,8,28,8,128]{4,3,2,1,0:T(8,128)(2,1)} custom-call(bf16[1,8,28,8,128]{4,3,2,1,0:T(8,128)(2,1)S(1)} %get-tuple-element.69.refs_0_, bf16[1,8,28,8,128]{4,3,2,1,0:T(8,128)(2,1)S(1)} %get-tuple-element.73.refs_1_, bf16[1,8,28,8,128]{4,3,2,1,0:T(8,128)(2,1)S(1)} %collective-permute-done.24.refs_2_, ...), custom_call_target="tpu_custom_call", output_to_operand_aliasing={{}: (8, {})} | custom-call | flops 2000000000 | bytes 8257536 | tf_op jit(solution)/shard_map/pallas_call | solution.py:58
  107.5 0.2 collective-permute-done.23.refs_2_
  107.7 1.1 %shard_map.75 = bf16[32,8,28,8,128]{4,3,2,1,0:T(8,128)(2,1)} custom-call(bf16[1,8,28,8,128]{4,3,2,1,0:T(8,128)(2,1)S(1)} %collective-permute-done.21.refs_0_, bf16[1,8,28,8,128]{4,3,2,1,0:T(8,128)(2,1)S(1)} %collective-permute-done.22.refs_1_, bf16[1,8,28,8,128]{4,3,2,1,0:T(8,128)(2,1)S(1)} %collective-permute-done.23.refs_2_, ...), custom_call_target="tpu_custom_call", output_to_operand_aliasing={{}: (3, {})} | custom-call | flops 2000000000 | bytes 2752512 | tf_op jit(solution)/shard_map/pallas_call | solution.py:58
  (33 shorter events, 0.2 us)
Async XLA Ops:
  0.6 17.1 %all-to-all-start = ((bf16[8,28,8,128]{3,2,1,0:T(8,128)(2,1)}), bf16[8,28,8,128]{3,2,1,0:T(8,128)(2,1)S(1)}, u32[]{:S(2)}, u32[]{:S(2)}) async-start(bf16[8,28,8,128]{3,2,1,0:T(8,128)(2,1)} %bitcast.35), calls=%async_computation | async-start | bytes 917504 | tf_op jit(solution)/shard_map/all_to_all | solution.py:84
  37.0 9.0 %collective-permute-start = (bf16[1,8,28,8,128]{4,3,2,1,0:T(8,128)(2,1)S(1)}, bf16[1,8,28,8,128]{4,3,2,1,0:T(8,128)(2,1)S(1)}, u32[]{:S(2)}, u32[]{:S(2)}) collective-permute-start(bf16[1,8,28,8,128]{4,3,2,1,0:T(8,128)(2,1)S(1)} %fusion.refs_0_), channel_id=1, source_target_pairs={{0,1},{1,0},{2,3},{3,2},{4,5},{5,4},{6,7},{7,6},{8,9},{9,8},{10,11... | collective-permute-start | bytes 1376264 | tf_op jit(solution)/shard_map/ppermute | solution.py:23
  40.1 12.1 %collective-permute-start.1 = (bf16[1,8,28,8,128]{4,3,2,1,0:T(8,128)(2,1)S(1)}, bf16[1,8,28,8,128]{4,3,2,1,0:T(8,128)(2,1)S(1)}, u32[]{:S(2)}, u32[]{:S(2)}) collective-permute-start(bf16[1,8,28,8,128]{4,3,2,1,0:T(8,128)(2,1)S(1)} %fusion.refs_0_), channel_id=1, source_target_pairs={{0,16},{1,17},{2,18},{3,19},{4,20},{5,21},{6,22},{7,23},{8,24},{9,... | collective-permute-start | bytes 1376264 | tf_op jit(solution)/shard_map/ppermute | solution.py:23
  40.5 17.2 %collective-permute-start.2 = (bf16[1,8,28,8,128]{4,3,2,1,0:T(8,128)(2,1)S(1)}, bf16[1,8,28,8,128]{4,3,2,1,0:T(8,128)(2,1)S(1)}, u32[]{:S(2)}, u32[]{:S(2)}) collective-permute-start(bf16[1,8,28,8,128]{4,3,2,1,0:T(8,128)(2,1)S(1)} %fusion.refs_0_), channel_id=1, source_target_pairs={{0,2},{1,15},{2,4},{3,1},{4,6},{5,3},{6,8},{7,5},{8,10},{9,7},{10,... | collective-permute-start | bytes 1376264 | tf_op jit(solution)/shard_map/ppermute | solution.py:23
  46.1 11.7 %collective-permute-start.3 = (bf16[1,8,28,8,128]{4,3,2,1,0:T(8,128)(2,1)S(1)}, bf16[1,8,28,8,128]{4,3,2,1,0:T(8,128)(2,1)S(1)}, u32[]{:S(2)}, u32[]{:S(2)}) collective-permute-start(bf16[1,8,28,8,128]{4,3,2,1,0:T(8,128)(2,1)S(1)} %get-tuple-element.45.refs_1_), channel_id=1, source_target_pairs={{0,2},{1,15},{2,4},{3,1},{4,6},{5,3},{6,8},{7,5},{8,10},{9,7},{10,... | collective-permute-start | bytes 1376264 | tf_op jit(solution)/shard_map/ppermute | solution.py:23
  52.2 11.0 %collective-permute-start.4 = (bf16[1,8,28,8,128]{4,3,2,1,0:T(8,128)(2,1)S(1)}, bf16[1,8,28,8,128]{4,3,2,1,0:T(8,128)(2,1)S(1)}, u32[]{:S(2)}, u32[]{:S(2)}) collective-permute-start(bf16[1,8,28,8,128]{4,3,2,1,0:T(8,128)(2,1)S(1)} %get-tuple-element.47.refs_2_), channel_id=1, source_target_pairs={{0,2},{1,15},{2,4},{3,1},{4,6},{5,3},{6,8},{7,5},{8,10},{9,7},{10,... | collective-permute-start | bytes 1376264 | tf_op jit(solution)/shard_map/ppermute | solution.py:23
  57.9 15.1 %collective-permute-start.5 = (bf16[2,8,28,8,128]{4,3,2,1,0:T(8,128)(2,1)S(1)}, bf16[2,8,28,8,128]{4,3,2,1,0:T(8,128)(2,1)S(1)}, u32[]{:S(2)}, u32[]{:S(2)}) collective-permute-start(bf16[2,8,28,8,128]{4,3,2,1,0:T(8,128)(2,1)S(1)} %constant_dynamic-update-slice_fusion.refs_0_), channel_id=1, source_target_pairs={{0,2},{1,15},{2,4},{3,1},{4,6},{5,3},{6,8},{7,5},{8,10},{9,7},{10,... | collective-permute-start | bytes 2752520 | tf_op jit(solution)/shard_map/ppermute | solution.py:23
  59.7 13.3 %collective-permute-start.6 = (bf16[2,8,28,8,128]{4,3,2,1,0:T(8,128)(2,1)S(1)}, bf16[2,8,28,8,128]{4,3,2,1,0:T(8,128)(2,1)S(1)}, u32[]{:S(2)}, u32[]{:S(2)}) collective-permute-start(bf16[2,8,28,8,128]{4,3,2,1,0:T(8,128)(2,1)S(1)} %constant_dynamic-update-slice_fusion.refs_0_), channel_id=1, source_target_pairs={{0,1},{1,0},{2,3},{3,2},{4,5},{5,4},{6,7},{7,6},{8,9},{9,8},{10,11... | collective-permute-start | bytes 2752520 | tf_op jit(solution)/shard_map/ppermute | solution.py:23
  60.8 11.7 %collective-permute-start.7 = (bf16[1,8,28,8,128]{4,3,2,1,0:T(8,128)(2,1)S(1)}, bf16[1,8,28,8,128]{4,3,2,1,0:T(8,128)(2,1)S(1)}, u32[]{:S(2)}, u32[]{:S(2)}) collective-permute-start(bf16[1,8,28,8,128]{4,3,2,1,0:T(8,128)(2,1)S(1)} %get-tuple-element.50), channel_id=1, source_target_pairs={{0,16},{1,17},{2,18},{3,19},{4,20},{5,21},{6,22},{7,23},{8,24},{9,... | collective-permute-start | bytes 1376264 | tf_op jit(solution)/shard_map/ppermute | solution.py:23
  63.2 14.7 %collective-permute-start.8 = (bf16[1,8,28,8,128]{4,3,2,1,0:T(8,128)(2,1)S(1)}, bf16[1,8,28,8,128]{4,3,2,1,0:T(8,128)(2,1)S(1)}, u32[]{:S(2)}, u32[]{:S(2)}) collective-permute-start(bf16[1,8,28,8,128]{4,3,2,1,0:T(8,128)(2,1)S(1)} %get-tuple-element.53.refs_0_), channel_id=1, source_target_pairs={{0,2},{1,15},{2,4},{3,1},{4,6},{5,3},{6,8},{7,5},{8,10},{9,7},{10,... | collective-permute-start | bytes 1376264 | tf_op jit(solution)/shard_map/ppermute | solution.py:23
  66.4 13.7 %collective-permute-start.9 = (bf16[2,8,28,8,128]{4,3,2,1,0:T(8,128)(2,1)S(1)}, bf16[2,8,28,8,128]{4,3,2,1,0:T(8,128)(2,1)S(1)}, u32[]{:S(2)}, u32[]{:S(2)}) collective-permute-start(bf16[2,8,28,8,128]{4,3,2,1,0:T(8,128)(2,1)S(1)} %pad_maximum_fusion), channel_id=1, source_target_pairs={{0,1},{1,0},{2,3},{3,2},{4,5},{5,4},{6,7},{7,6},{8,9},{9,8},{10,11... | collective-permute-start | bytes 2752520 | tf_op jit(solution)/shard_map/ppermute | solution.py:23
  73.0 16.2 %collective-permute-start.10 = (bf16[2,8,28,8,128]{4,3,2,1,0:T(8,128)(2,1)S(1)}, bf16[2,8,28,8,128]{4,3,2,1,0:T(8,128)(2,1)S(1)}, u32[]{:S(2)}, u32[]{:S(2)}) collective-permute-start(bf16[2,8,28,8,128]{4,3,2,1,0:T(8,128)(2,1)S(1)} %get-tuple-element.56.refs_0_), channel_id=1, source_target_pairs={{0,2},{1,15},{2,4},{3,1},{4,6},{5,3},{6,8},{7,5},{8,10},{9,7},{10,... | collective-permute-start | bytes 2752520 | tf_op jit(solution)/shard_map/ppermute | solution.py:23
  76.1 13.1 %collective-permute-start.11 = (bf16[2,8,28,8,128]{4,3,2,1,0:T(8,128)(2,1)S(1)}, bf16[2,8,28,8,128]{4,3,2,1,0:T(8,128)(2,1)S(1)}, u32[]{:S(2)}, u32[]{:S(2)}) collective-permute-start(bf16[2,8,28,8,128]{4,3,2,1,0:T(8,128)(2,1)S(1)} %get-tuple-element.56.refs_0_), channel_id=1, source_target_pairs={{0,1},{1,0},{2,3},{3,2},{4,5},{5,4},{6,7},{7,6},{8,9},{9,8},{10,11... | collective-permute-start | bytes 2752520 | tf_op jit(solution)/shard_map/ppermute | solution.py:23
  76.2 11.7 %collective-permute-start.12 = (bf16[1,8,28,8,128]{4,3,2,1,0:T(8,128)(2,1)S(1)}, bf16[1,8,28,8,128]{4,3,2,1,0:T(8,128)(2,1)S(1)}, u32[]{:S(2)}, u32[]{:S(2)}) collective-permute-start(bf16[1,8,28,8,128]{4,3,2,1,0:T(8,128)(2,1)S(1)} %slice.9), channel_id=1, source_target_pairs={{0,16},{1,17},{2,18},{3,19},{4,20},{5,21},{6,22},{7,23},{8,24},{9,... | collective-permute-start | bytes 1376264 | tf_op jit(solution)/shard_map/ppermute | solution.py:23
  77.9 14.1 %collective-permute-start.13 = (bf16[1,8,28,8,128]{4,3,2,1,0:T(8,128)(2,1)S(1)}, bf16[1,8,28,8,128]{4,3,2,1,0:T(8,128)(2,1)S(1)}, u32[]{:S(2)}, u32[]{:S(2)}) collective-permute-start(bf16[1,8,28,8,128]{4,3,2,1,0:T(8,128)(2,1)S(1)} %get-tuple-element.58.refs_2_), channel_id=1, source_target_pairs={{0,1},{1,0},{2,3},{3,2},{4,5},{5,4},{6,7},{7,6},{8,9},{9,8},{10,11... | collective-permute-start | bytes 1376264 | tf_op jit(solution)/shard_map/ppermute | solution.py:23
  80.1 13.6 %collective-permute-start.14 = (bf16[1,8,28,8,128]{4,3,2,1,0:T(8,128)(2,1)S(1)}, bf16[1,8,28,8,128]{4,3,2,1,0:T(8,128)(2,1)S(1)}, u32[]{:S(2)}, u32[]{:S(2)}) collective-permute-start(bf16[1,8,28,8,128]{4,3,2,1,0:T(8,128)(2,1)S(1)} %get-tuple-element.61.refs_0_), channel_id=1, source_target_pairs={{0,2},{1,15},{2,4},{3,1},{4,6},{5,3},{6,8},{7,5},{8,10},{9,7},{10,... | collective-permute-start | bytes 1376264 | tf_op jit(solution)/shard_map/ppermute | solution.py:23
  87.8 5.9 %collective-permute-start.15 = (bf16[1,8,28,8,128]{4,3,2,1,0:T(8,128)(2,1)S(1)}, bf16[1,8,28,8,128]{4,3,2,1,0:T(8,128)(2,1)S(1)}, u32[]{:S(2)}, u32[]{:S(2)}) collective-permute-start(bf16[1,8,28,8,128]{4,3,2,1,0:T(8,128)(2,1)S(1)} %get-tuple-element.61.refs_0_), channel_id=1, source_target_pairs={{0,1},{1,0},{2,3},{3,2},{4,5},{5,4},{6,7},{7,6},{8,9},{9,8},{10,11... | collective-permute-start | bytes 1376264 | tf_op jit(solution)/shard_map/ppermute | solution.py:23
  89.2 14.2 %collective-permute-start.17 = (bf16[2,8,28,8,128]{4,3,2,1,0:T(8,128)(2,1)S(1)}, bf16[2,8,28,8,128]{4,3,2,1,0:T(8,128)(2,1)S(1)}, u32[]{:S(2)}, u32[]{:S(2)}) collective-permute-start(bf16[2,8,28,8,128]{4,3,2,1,0:T(8,128)(2,1)S(1)} %get-tuple-element.65.refs_0_), channel_id=1, source_target_pairs={{0,1},{1,0},{2,3},{3,2},{4,5},{5,4},{6,7},{7,6},{8,9},{9,8},{10,11... | collective-permute-start | bytes 2752520 | tf_op jit(solution)/shard_map/ppermute | solution.py:23
  90.0 7.9 %collective-permute-start.16 = (bf16[1,8,28,8,128]{4,3,2,1,0:T(8,128)(2,1)S(1)}, bf16[1,8,28,8,128]{4,3,2,1,0:T(8,128)(2,1)S(1)}, u32[]{:S(2)}, u32[]{:S(2)}) collective-permute-start(bf16[1,8,28,8,128]{4,3,2,1,0:T(8,128)(2,1)S(1)} %get-tuple-element.80), channel_id=1, source_target_pairs={{0,2},{1,15},{2,4},{3,1},{4,6},{5,3},{6,8},{7,5},{8,10},{9,7},{10,... | collective-permute-start | bytes 1376264 | tf_op jit(solution)/shard_map/ppermute | solution.py:23
  92.0 11.4 %collective-permute-start.18 = (bf16[1,8,28,8,128]{4,3,2,1,0:T(8,128)(2,1)S(1)}, bf16[1,8,28,8,128]{4,3,2,1,0:T(8,128)(2,1)S(1)}, u32[]{:S(2)}, u32[]{:S(2)}) collective-permute-start(bf16[1,8,28,8,128]{4,3,2,1,0:T(8,128)(2,1)S(1)} %get-tuple-element.79), channel_id=1, source_target_pairs={{0,16},{1,17},{2,18},{3,19},{4,20},{5,21},{6,22},{7,23},{8,24},{9,... | collective-permute-start | bytes 1376264 | tf_op jit(solution)/shard_map/ppermute | solution.py:23
  93.7 9.7 %collective-permute-start.19 = (bf16[1,8,28,8,128]{4,3,2,1,0:T(8,128)(2,1)S(1)}, bf16[1,8,28,8,128]{4,3,2,1,0:T(8,128)(2,1)S(1)}, u32[]{:S(2)}, u32[]{:S(2)}) collective-permute-start(bf16[1,8,28,8,128]{4,3,2,1,0:T(8,128)(2,1)S(1)} %get-tuple-element.69.refs_0_), channel_id=1, source_target_pairs={{0,2},{1,15},{2,4},{3,1},{4,6},{5,3},{6,8},{7,5},{8,10},{9,7},{10,... | collective-permute-start | bytes 1376264 | tf_op jit(solution)/shard_map/ppermute | solution.py:23
  95.8 7.6 %collective-permute-start.20 = (bf16[1,8,28,8,128]{4,3,2,1,0:T(8,128)(2,1)S(1)}, bf16[1,8,28,8,128]{4,3,2,1,0:T(8,128)(2,1)S(1)}, u32[]{:S(2)}, u32[]{:S(2)}) collective-permute-start(bf16[1,8,28,8,128]{4,3,2,1,0:T(8,128)(2,1)S(1)} %get-tuple-element.69.refs_0_), channel_id=1, source_target_pairs={{0,1},{1,0},{2,3},{3,2},{4,5},{5,4},{6,7},{7,6},{8,9},{9,8},{10,11... | collective-permute-start | bytes 1376264 | tf_op jit(solution)/shard_map/ppermute | solution.py:23
  97.9 7.6 %collective-permute-start.24 = (bf16[1,8,28,8,128]{4,3,2,1,0:T(8,128)(2,1)S(1)}, bf16[1,8,28,8,128]{4,3,2,1,0:T(8,128)(2,1)S(1)}, u32[]{:S(2)}, u32[]{:S(2)}) collective-permute-start(bf16[1,8,28,8,128]{4,3,2,1,0:T(8,128)(2,1)S(1)} %get-tuple-element.67.refs_2_), channel_id=1, source_target_pairs={{0,1},{1,0},{2,3},{3,2},{4,5},{5,4},{6,7},{7,6},{8,9},{9,8},{10,11... | collective-permute-start | bytes 1376264 | tf_op jit(solution)/shard_map/ppermute | solution.py:23
  103.4 4.1 %collective-permute-start.21 = (bf16[1,8,28,8,128]{4,3,2,1,0:T(8,128)(2,1)S(1)}, bf16[1,8,28,8,128]{4,3,2,1,0:T(8,128)(2,1)S(1)}, u32[]{:S(2)}, u32[]{:S(2)}) collective-permute-start(bf16[1,8,28,8,128]{4,3,2,1,0:T(8,128)(2,1)S(1)} %get-tuple-element.70.refs_3_), channel_id=1, source_target_pairs={{0,1},{1,0},{2,3},{3,2},{4,5},{5,4},{6,7},{7,6},{8,9},{9,8},{10,11... | collective-permute-start | bytes 1376264 | tf_op jit(solution)/shard_map/ppermute | solution.py:23
  105.0 2.6 %collective-permute-start.22 = (bf16[1,8,28,8,128]{4,3,2,1,0:T(8,128)(2,1)S(1)}, bf16[1,8,28,8,128]{4,3,2,1,0:T(8,128)(2,1)S(1)}, u32[]{:S(2)}, u32[]{:S(2)}) collective-permute-start(bf16[1,8,28,8,128]{4,3,2,1,0:T(8,128)(2,1)S(1)} %get-tuple-element.71.refs_5_), channel_id=1, source_target_pairs={{0,1},{1,0},{2,3},{3,2},{4,5},{5,4},{6,7},{7,6},{8,9},{9,8},{10,11... | collective-permute-start | bytes 1376264 | tf_op jit(solution)/shard_map/ppermute | solution.py:23
  105.1 2.7 %collective-permute-start.23 = (bf16[1,8,28,8,128]{4,3,2,1,0:T(8,128)(2,1)S(1)}, bf16[1,8,28,8,128]{4,3,2,1,0:T(8,128)(2,1)S(1)}, u32[]{:S(2)}, u32[]{:S(2)}) collective-permute-start(bf16[1,8,28,8,128]{4,3,2,1,0:T(8,128)(2,1)S(1)} %get-tuple-element.72.refs_7_), channel_id=1, source_target_pairs={{0,1},{1,0},{2,3},{3,2},{4,5},{5,4},{6,7},{7,6},{8,9},{9,8},{10,11... | collective-permute-start | bytes 1376264 | tf_op jit(solution)/shard_map/ppermute | solution.py:23

commit v5 on v4

--- a/solution.py
+++ b/solution.py
@@ -121,18 +121,18 @@
         return array, [(run, hops, kind, came) for kind in kinds]
 
     own = own[None]
-    a1, q0, other = along_slots(own), swap_run(own), swap_core(own)
-    token, other = gate(jnp.zeros(TILE, jnp.float32), other)
-    b1 = along_slots(other)
+    q0 = swap_run(own)
+    p0 = jnp.concatenate([own, swap_core(own)])
+    token, p0 = gate(jnp.zeros(TILE, jnp.float32), p0)
+    p1 = along_slots(p0)
     token, outer_all, momentum_new = write(token, outer_all, momentum_new)
 
     token, q0 = gate(token, q0)
     q1 = along_slots(q0)
 
-    token, a1, b1 = gate(token, a1, b1)
-    p1 = jnp.concatenate([a1, b1])
-    p2, y1, cp1 = along_slots(p1), swap_run(b1), swap_core(p1)
-    out = place(None, [rows(own, 0), rows(other, 0, (1,)), rows(q0, 0, run=1)], shape)
+    token, p1 = gate(token, p1)
+    p2, y1, cp1 = along_slots(p1), swap_run(p1[1:]), swap_core(p1)
+    out = place(None, [rows(p0, 0, (0, 1)), rows(q0, 0, run=1)], shape)
 
     token, out, q1 = gate(token, out, q1)
     q2, cq01 = along_slots(q1), swap_core(jnp.concatenate([q0, q1]))
@@ -154,8 +154,8 @@
     q4, cq3 = along_slots(q3), swap_core(q3)
     out = place(out, [rows(p3, 3, (0, 1)), rows(cp2, 2, (0, 1), 1), rows(y2, 2, (1,), run=1)], shape)
 
-    token, out, p4, cp3, y3, q4, cq3 = gate(token, out, p4, cp3, y3, q4, cq3)
-    cp4, cy3, cq4 = swap_core(p4), swap_core(y3), swap_core(q4)
+    token, out, p4, cp3, y3 = gate(token, out, p4, cp3, y3)
+    cp4, cy3 = swap_core(p4), swap_core(y3)
     out = place(
         out,
         [
@@ -165,13 +165,18 @@
             rows(p4, 4),
             rows(cp3, 3, (0, 1), 1),
             rows(y3, 3, (1,), run=1),
-            rows(cq3, 3, came=1, run=1),
-            rows(q4, 4, run=1),
         ],
         shape,
     )
-    out = place(out, [rows(cp4, 4, came=1), rows(cy3, 3, (1,), 1, 1), rows(cq4, 4, came=1, run=1)], shape)
-    return out, outer_all, momentum_new
+
+    token, out, q4, cq3 = gate(token, out, q4, cq3)
+    cq4 = swap_core(q4)
+    out = place(
+        out,
+        [rows(cq3, 3, came=1, run=1), rows(cp4, 4, came=1), rows(cy3, 3, (1,), 1, 1), rows(q4, 4, run=1)],
+        shape,
+    )
+    return place(out, [rows(cq4, 4, came=1, run=1)], shape), outer_all, momentum_new
 
 
 def body(inner, outer, momentum):

time: 109 us -> 109 us (level)
  starting transfers between devices: 47.6 us -> 45.7 us
    ppermute x25 -> x24, starting transfers between devices: 40.1 us -> 38.2 us  [move(): lax.ppermute(array, 'fsdp', [(i, fsdp_index(*target(*coords(i)))) for i i...]
    ppermute x25 -> x24, waiting for transfers between devices: 20.2 us -> 21 us  [move(): lax.ppermute(array, 'fsdp', [(i, fsdp_index(*target(*coords(i)))) for i i...]
    pallas_call x8 -> x9, Pallas kernels: 10.1 us -> 10.7 us  [place(): pl.pallas_call(kernel, out_shape=jax.ShapeDtypeStruct(shape, jnp.bfloat16...]
  transfers between devices with their start and end apart: 26 -> 25, of which waited for: 10 -> 9; matrix products, arithmetic and copies ran while one was open for 0% -> 0% of each run, Pallas kernels for 9% -> 10%
where the time goes in v5:
time: 109 us
  starting transfers between devices  45.7 us (42%)
  waiting for transfers between devices  30.6 us (28%)
  blocking collectives  17 us (16%)
  Pallas kernels  11.6 us (11%)
  other arithmetic  2.39 us (2%)
    ppermute x24, starting transfers between devices, move(): lax.ppermute(array, 'fsdp', [(i, fsdp_index(*target(*coords(i)))) for i i...  38.2 us
    ppermute x24, waiting for transfers between devices, move(): lax.ppermute(array, 'fsdp', [(i, fsdp_index(*target(*coords(i)))) for i i...  21 us
    all_to_all x1, blocking collectives, to_all(): lax.all_to_all(jnp.broadcast_to(array, (REPLICAS,) + array.shape), 'repli...  17 us
    pallas_call x9, Pallas kernels, place(): pl.pallas_call(kernel, out_shape=jax.ShapeDtypeStruct(shape, jnp.bfloat16...  10.7 us
    all_to_all x1, waiting for transfers between devices, step(): terms = lax.all_to_all(inner, 'replica', 0, 0).astype(jnp.float32)  9.63 us
    all_to_all x1, starting transfers between devices, step(): terms = lax.all_to_all(inner, 'replica', 0, 0).astype(jnp.float32)  7.49 us
  transfers between devices with their start and end apart: 25, of which 9 were waited for; matrix products, arithmetic and copies ran while one was open for 0% of the time, Pallas kernels for 10%

profile of v5, /device:TPU:1, one launch (start us, length us, event | category | flops | bytes accessed | tf_op | source)
XLA Modules:
  0.0 108.5 jit_solution(8875047130678897057)
XLA Ops:
  0.6 7.5 %all-to-all-start = ((bf16[8,28,8,128]{3,2,1,0:T(8,128)(2,1)}), bf16[8,28,8,128]{3,2,1,0:T(8,128)(2,1)S(1)}, u32[]{:S(2)}, u32[]{:S(2)}) async-start(bf16[8,28,8,128]{3,2,1,0:T(8,128)(2,1)} %bitcast.35), calls=%async_computation | async-start | bytes 917504 | tf_op jit(solution)/shard_map/all_to_all | solution.py:84
  8.1 9.6 %all-to-all-done = bf16[8,28,8,128]{3,2,1,0:T(8,128)(2,1)S(1)} async-done(((bf16[8,28,8,128]{3,2,1,0:T(8,128)(2,1)}), bf16[8,28,8,128]{3,2,1,0:T(8,128)(2,1)S(1)}, u32[]{:S(2)}, u32[]{:S(2)}) %all-to-all-start) | async-done | bytes 458784 | tf_op jit(solution)/shard_map/all_to_all | solution.py:84
  17.8 0.1 convert_reduce_fusion
  17.8 1.0 bitcast_subtract_fusion
  18.8 0.1 broadcast_in_dim.13
  18.9 17.0 %all_to_all.10.refs_1_ = f32[8,28,8,128]{3,2,1,0:T(8,128)S(1)} all-to-all(f32[8,28,8,128]{3,2,1,0:T(8,128)S(1)} %broadcast_in_dim.13), channel_id=1, replica_groups=mesh['replica'=8,'fsdp'=32] {'replica'}, dimensions={0} | all-to-all | bytes 1835008 | tf_op jit(solution)/shard_map/all_to_all | solution.py:91
  35.9 1.2 %fusion = bf16[1,8,28,8,128]{4,3,2,1,0:T(8,128)(2,1)S(1)} fusion(f32[8,28,8,128]{3,2,1,0:T(8,128)S(1)} %all_to_all.10.refs_1_, bf16[8,28,8,128]{3,2,1,0:T(8,128)(2,1)} %bitcast.36), kind=kLoop, calls=%fused_computation.4 | loop fusion | flops 917504 | bytes 1835008 | tf_op jit(solution)/shard_map/broadcast_in_dim | solution.py:123
  37.0 3.0 %collective-permute-start = (bf16[1,8,28,8,128]{4,3,2,1,0:T(8,128)(2,1)S(1)}, bf16[1,8,28,8,128]{4,3,2,1,0:T(8,128)(2,1)S(1)}, u32[]{:S(2)}, u32[]{:S(2)}) collective-permute-start(bf16[1,8,28,8,128]{4,3,2,1,0:T(8,128)(2,1)S(1)} %fusion), channel_id=1, source_target_pairs={{0,1},{1,0},{2,3},{3,2},{4,5},{5,4},{6,7},{7,6},{8,9},{9,8},{10,11... | collective-permute-start | bytes 1376264 | tf_op jit(solution)/shard_map/ppermute | solution.py:23
  40.1 0.4 collective-permute-start.1
  40.5 1.0 collective-permute-done
  41.5 0.1 pad_maximum_fusion.refs_1_
  41.6 5.7 %collective-permute-start.2 = (bf16[2,8,28,8,128]{4,3,2,1,0:T(8,128)(2,1)S(1)}, bf16[2,8,28,8,128]{4,3,2,1,0:T(8,128)(2,1)S(1)}, u32[]{:S(2)}, u32[]{:S(2)}) collective-permute-start(bf16[2,8,28,8,128]{4,3,2,1,0:T(8,128)(2,1)S(1)} %get-tuple-element.46.refs_0_), channel_id=1, source_target_pairs={{0,2},{1,15},{2,4},{3,1},{4,6},{5,3},{6,8},{7,5},{8,10},{9,7},{10,... | collective-permute-start | bytes 2752520 | tf_op jit(solution)/shard_map/ppermute | solution.py:23
  47.3 1.0 shard_map.59
  48.3 3.9 %collective-permute-done.1.refs_1_ = bf16[1,8,28,8,128]{4,3,2,1,0:T(8,128)(2,1)S(1)} collective-permute-done((bf16[1,8,28,8,128]{4,3,2,1,0:T(8,128)(2,1)S(1)}, bf16[1,8,28,8,128]{4,3,2,1,0:T(8,128)(2,1)S(1)}, u32[]{:S(2)}, u32[]{:S(2)}) %collective-permute-start.1) | collective-permute-done | bytes 458784 | tf_op jit(solution)/shard_map/ppermute | solution.py:23
  52.2 5.6 %collective-permute-start.3 = (bf16[1,8,28,8,128]{4,3,2,1,0:T(8,128)(2,1)S(1)}, bf16[1,8,28,8,128]{4,3,2,1,0:T(8,128)(2,1)S(1)}, u32[]{:S(2)}, u32[]{:S(2)}) collective-permute-start(bf16[1,8,28,8,128]{4,3,2,1,0:T(8,128)(2,1)S(1)} %get-tuple-element.48.refs_1_), channel_id=1, source_target_pairs={{0,2},{1,15},{2,4},{3,1},{4,6},{5,3},{6,8},{7,5},{8,10},{9,7},{10,... | collective-permute-start | bytes 1376264 | tf_op jit(solution)/shard_map/ppermute | solution.py:23
  57.7 3.0 %collective-permute-start.4 = (bf16[2,8,28,8,128]{4,3,2,1,0:T(8,128)(2,1)S(1)}, bf16[2,8,28,8,128]{4,3,2,1,0:T(8,128)(2,1)S(1)}, u32[]{:S(2)}, u32[]{:S(2)}) collective-permute-start(bf16[2,8,28,8,128]{4,3,2,1,0:T(8,128)(2,1)S(1)} %get-tuple-element.50.refs_0_), channel_id=1, source_target_pairs={{0,2},{1,15},{2,4},{3,1},{4,6},{5,3},{6,8},{7,5},{8,10},{9,7},{10,... | collective-permute-start | bytes 2752520 | tf_op jit(solution)/shard_map/ppermute | solution.py:23
  60.7 1.1 %shard_map.62.refs_1_ = bf16[32,8,28,8,128]{4,3,2,1,0:T(8,128)(2,1)} custom-call(bf16[2,8,28,8,128]{4,3,2,1,0:T(8,128)(2,1)S(1)} %get-tuple-element.46.refs_0_, bf16[1,8,28,8,128]{4,3,2,1,0:T(8,128)(2,1)S(1)} %get-tuple-element.48.refs_1_), custom_call_target="tpu_custom_call" | custom-call | flops 2000000000 | bytes 2752512 | tf_op jit(solution)/shard_map/pallas_call | solution.py:58
  61.9 0.5 collective-permute-start.6
  62.4 0.8 collective-permute-done.3.refs_2_
  63.2 3.1 %collective-permute-start.7 = (bf16[1,8,28,8,128]{4,3,2,1,0:T(8,128)(2,1)S(1)}, bf16[1,8,28,8,128]{4,3,2,1,0:T(8,128)(2,1)S(1)}, u32[]{:S(2)}, u32[]{:S(2)}) collective-permute-start(bf16[1,8,28,8,128]{4,3,2,1,0:T(8,128)(2,1)S(1)} %get-tuple-element.53.refs_0_), channel_id=1, source_target_pairs={{0,2},{1,15},{2,4},{3,1},{4,6},{5,3},{6,8},{7,5},{8,10},{9,7},{10,... | collective-permute-start | bytes 1376264 | tf_op jit(solution)/shard_map/ppermute | solution.py:23
  66.3 0.1 pad_maximum_fusion.1
  66.4 0.1 collective-permute-start.8
  66.5 1.0 shard_map.64.refs_1_
  67.4 6.1 %collective-permute-done.6.refs_4_ = bf16[1,8,28,8,128]{4,3,2,1,0:T(8,128)(2,1)S(1)} collective-permute-done((bf16[1,8,28,8,128]{4,3,2,1,0:T(8,128)(2,1)S(1)}, bf16[1,8,28,8,128]{4,3,2,1,0:T(8,128)(2,1)S(1)}, u32[]{:S(2)}, u32[]{:S(2)}) %collective-permute-start.6) | collective-permute-done | bytes 458784 | tf_op jit(solution)/shard_map/ppermute | solution.py:23
  73.6 2.6 %collective-permute-start.9 = (bf16[2,8,28,8,128]{4,3,2,1,0:T(8,128)(2,1)S(1)}, bf16[2,8,28,8,128]{4,3,2,1,0:T(8,128)(2,1)S(1)}, u32[]{:S(2)}, u32[]{:S(2)}) collective-permute-start(bf16[2,8,28,8,128]{4,3,2,1,0:T(8,128)(2,1)S(1)} %get-tuple-element.56.refs_0_), channel_id=1, source_target_pairs={{0,2},{1,15},{2,4},{3,1},{4,6},{5,3},{6,8},{7,5},{8,10},{9,7},{10,... | collective-permute-start | bytes 2752520 | tf_op jit(solution)/shard_map/ppermute | solution.py:23
  76.2 0.5 collective-permute-start.11
  76.6 0.8 shard_map.66.refs_1_
  77.4 0.5 collective-permute-done.7.refs_2_
  77.9 2.2 %collective-permute-start.12 = (bf16[1,8,28,8,128]{4,3,2,1,0:T(8,128)(2,1)S(1)}, bf16[1,8,28,8,128]{4,3,2,1,0:T(8,128)(2,1)S(1)}, u32[]{:S(2)}, u32[]{:S(2)}) collective-permute-start(bf16[1,8,28,8,128]{4,3,2,1,0:T(8,128)(2,1)S(1)} %get-tuple-element.58.refs_2_), channel_id=1, source_target_pairs={{0,1},{1,0},{2,3},{3,2},{4,5},{5,4},{6,7},{7,6},{8,9},{9,8},{10,11... | collective-permute-start | bytes 1376264 | tf_op jit(solution)/shard_map/ppermute | solution.py:23
  80.1 1.7 %collective-permute-start.13 = (bf16[1,8,28,8,128]{4,3,2,1,0:T(8,128)(2,1)S(1)}, bf16[1,8,28,8,128]{4,3,2,1,0:T(8,128)(2,1)S(1)}, u32[]{:S(2)}, u32[]{:S(2)}) collective-permute-start(bf16[1,8,28,8,128]{4,3,2,1,0:T(8,128)(2,1)S(1)} %get-tuple-element.61.refs_0_), channel_id=1, source_target_pairs={{0,2},{1,15},{2,4},{3,1},{4,6},{5,3},{6,8},{7,5},{8,10},{9,7},{10,... | collective-permute-start | bytes 1376264 | tf_op jit(solution)/shard_map/ppermute | solution.py:23
  81.8 1.4 %shard_map.68.refs_1_ = bf16[32,8,28,8,128]{4,3,2,1,0:T(8,128)(2,1)} custom-call(bf16[2,8,28,8,128]{4,3,2,1,0:T(8,128)(2,1)S(1)} %get-tuple-element.56.refs_0_, bf16[2,8,28,8,128]{4,3,2,1,0:T(8,128)(2,1)S(1)} %get-tuple-element.57.refs_1_, bf16[1,8,28,8,128]{4,3,2,1,0:T(8,128)(2,1)S(1)} %get-tuple-element.58.refs_2_, ...), custom_call_target="tpu_custom_call", output_to_operand_aliasing={{}: (3, {})} | custom-call | flops 2000000000 | bytes 4587520 | tf_op jit(solution)/shard_map/pallas_call | solution.py:58
  83.3 4.6 %collective-permute-done.11.refs_4_ = bf16[1,8,28,8,128]{4,3,2,1,0:T(8,128)(2,1)S(1)} collective-permute-done((bf16[1,8,28,8,128]{4,3,2,1,0:T(8,128)(2,1)S(1)}, bf16[1,8,28,8,128]{4,3,2,1,0:T(8,128)(2,1)S(1)}, u32[]{:S(2)}, u32[]{:S(2)}) %collective-permute-start.11) | collective-permute-done | bytes 458784 | tf_op jit(solution)/shard_map/ppermute | solution.py:23
  87.8 1.4 %collective-permute-start.14 = (bf16[1,8,28,8,128]{4,3,2,1,0:T(8,128)(2,1)S(1)}, bf16[1,8,28,8,128]{4,3,2,1,0:T(8,128)(2,1)S(1)}, u32[]{:S(2)}, u32[]{:S(2)}) collective-permute-start(bf16[1,8,28,8,128]{4,3,2,1,0:T(8,128)(2,1)S(1)} %get-tuple-element.61.refs_0_), channel_id=1, source_target_pairs={{0,1},{1,0},{2,3},{3,2},{4,5},{5,4},{6,7},{7,6},{8,9},{9,8},{10,11... | collective-permute-start | bytes 1376264 | tf_op jit(solution)/shard_map/ppermute | solution.py:23
  89.2 0.7 collective-permute-start.16
  90.0 1.8 %collective-permute-start.15 = (bf16[1,8,28,8,128]{4,3,2,1,0:T(8,128)(2,1)S(1)}, bf16[1,8,28,8,128]{4,3,2,1,0:T(8,128)(2,1)S(1)}, u32[]{:S(2)}, u32[]{:S(2)}) collective-permute-start(bf16[1,8,28,8,128]{4,3,2,1,0:T(8,128)(2,1)S(1)} %get-tuple-element.82), channel_id=1, source_target_pairs={{0,2},{1,15},{2,4},{3,1},{4,6},{5,3},{6,8},{7,5},{8,10},{9,7},{10,... | collective-permute-start | bytes 1376264 | tf_op jit(solution)/shard_map/ppermute | solution.py:23
  91.8 0.4 collective-permute-start.17
  92.2 1.3 %shard_map.70.refs_1_ = bf16[32,8,28,8,128]{4,3,2,1,0:T(8,128)(2,1)} custom-call(bf16[1,8,28,8,128]{4,3,2,1,0:T(8,128)(2,1)S(1)} %get-tuple-element.61.refs_0_, bf16[2,8,28,8,128]{4,3,2,1,0:T(8,128)(2,1)S(1)} %get-tuple-element.62.refs_1_, bf16[1,8,28,8,128]{4,3,2,1,0:T(8,128)(2,1)S(1)} %collective-permute-done.12.refs_2_, ...), custom_call_target="tpu_custom_call", output_to_operand_aliasing={{}: (3, {})} | custom-call | flops 2000000000 | bytes 3670016 | tf_op jit(solution)/shard_map/pallas_call | solution.py:58
  93.5 1.4 %collective-permute-start.18 = (bf16[1,8,28,8,128]{4,3,2,1,0:T(8,128)(2,1)S(1)}, bf16[1,8,28,8,128]{4,3,2,1,0:T(8,128)(2,1)S(1)}, u32[]{:S(2)}, u32[]{:S(2)}) collective-permute-start(bf16[1,8,28,8,128]{4,3,2,1,0:T(8,128)(2,1)S(1)} %get-tuple-element.67.refs_2_), channel_id=1, source_target_pairs={{0,1},{1,0},{2,3},{3,2},{4,5},{5,4},{6,7},{7,6},{8,9},{9,8},{10,11... | collective-permute-start | bytes 1376264 | tf_op jit(solution)/shard_map/ppermute | solution.py:23
  94.8 1.7 %collective-permute-start.19 = (bf16[1,8,28,8,128]{4,3,2,1,0:T(8,128)(2,1)S(1)}, bf16[1,8,28,8,128]{4,3,2,1,0:T(8,128)(2,1)S(1)}, u32[]{:S(2)}, u32[]{:S(2)}) collective-permute-start(bf16[1,8,28,8,128]{4,3,2,1,0:T(8,128)(2,1)S(1)} %get-tuple-element.70.refs_0_), channel_id=1, source_target_pairs={{0,2},{1,15},{2,4},{3,1},{4,6},{5,3},{6,8},{7,5},{8,10},{9,7},{10,... | collective-permute-start | bytes 1376264 | tf_op jit(solution)/shard_map/ppermute | solution.py:23
  96.6 1.4 %shard_map.72.refs_1_ = bf16[32,8,28,8,128]{4,3,2,1,0:T(8,128)(2,1)} custom-call(bf16[2,8,28,8,128]{4,3,2,1,0:T(8,128)(2,1)S(1)} %get-tuple-element.65.refs_0_, bf16[2,8,28,8,128]{4,3,2,1,0:T(8,128)(2,1)S(1)} %get-tuple-element.66.refs_1_, bf16[1,8,28,8,128]{4,3,2,1,0:T(8,128)(2,1)S(1)} %get-tuple-element.67.refs_2_, ...), custom_call_target="tpu_custom_call", output_to_operand_aliasing={{}: (3, {})} | custom-call | flops 2000000000 | bytes 4587520 | tf_op jit(solution)/shard_map/pallas_call | solution.py:58
  98.0 1.7 %collective-permute-start.20 = (bf16[1,8,28,8,128]{4,3,2,1,0:T(8,128)(2,1)S(1)}, bf16[1,8,28,8,128]{4,3,2,1,0:T(8,128)(2,1)S(1)}, u32[]{:S(2)}, u32[]{:S(2)}) collective-permute-start(bf16[1,8,28,8,128]{4,3,2,1,0:T(8,128)(2,1)S(1)} %get-tuple-element.70.refs_0_), channel_id=1, source_target_pairs={{0,1},{1,0},{2,3},{3,2},{4,5},{5,4},{6,7},{7,6},{8,9},{9,8},{10,11... | collective-permute-start | bytes 1376264 | tf_op jit(solution)/shard_map/ppermute | solution.py:23
  99.8 3.6 %collective-permute-done.17.refs_4_ = bf16[1,8,28,8,128]{4,3,2,1,0:T(8,128)(2,1)S(1)} collective-permute-done((bf16[1,8,28,8,128]{4,3,2,1,0:T(8,128)(2,1)S(1)}, bf16[1,8,28,8,128]{4,3,2,1,0:T(8,128)(2,1)S(1)}, u32[]{:S(2)}, u32[]{:S(2)}) %collective-permute-start.17) | collective-permute-done | bytes 458784 | tf_op jit(solution)/shard_map/ppermute | solution.py:23
  103.4 0.5 collective-permute-start.23
  103.9 1.7 %shard_map.74.refs_1_ = bf16[32,8,28,8,128]{4,3,2,1,0:T(8,128)(2,1)} custom-call(bf16[1,8,28,8,128]{4,3,2,1,0:T(8,128)(2,1)S(1)} %get-tuple-element.70.refs_0_, bf16[1,8,28,8,128]{4,3,2,1,0:T(8,128)(2,1)S(1)} %get-tuple-element.71.refs_1_, bf16[1,8,28,8,128]{4,3,2,1,0:T(8,128)(2,1)S(1)} %collective-permute-done.18.refs_2_, ...), custom_call_target="tpu_custom_call", output_to_operand_aliasing={{}: (6, {})} | custom-call | flops 2000000000 | bytes 6422528 | tf_op jit(solution)/shard_map/pallas_call | solution.py:58
  105.7 0.2 collective-permute-start.21
  105.8 1.3 %shard_map.76.refs_1_ = bf16[32,8,28,8,128]{4,3,2,1,0:T(8,128)(2,1)} custom-call(bf16[1,8,28,8,128]{4,3,2,1,0:T(8,128)(2,1)S(1)} %get-tuple-element.77.refs_0_, bf16[1,8,28,8,128]{4,3,2,1,0:T(8,128)(2,1)S(1)} %collective-permute-done.22.refs_1_, bf16[1,8,28,8,128]{4,3,2,1,0:T(8,128)(2,1)S(1)} %collective-permute-done.23.refs_2_, ...), custom_call_target="tpu_custom_call", output_to_operand_aliasing={{}: (4, {})} | custom-call | flops 2000000000 | bytes 3670016 | tf_op jit(solution)/shard_map/pallas_call | solution.py:58
  107.1 0.5 collective-permute-done.21.refs_0_
  107.6 0.8 shard_map.77
  (33 shorter events, 0.2 us)
Async XLA Ops:
  0.6 17.1 %all-to-all-start = ((bf16[8,28,8,128]{3,2,1,0:T(8,128)(2,1)}), bf16[8,28,8,128]{3,2,1,0:T(8,128)(2,1)S(1)}, u32[]{:S(2)}, u32[]{:S(2)}) async-start(bf16[8,28,8,128]{3,2,1,0:T(8,128)(2,1)} %bitcast.35), calls=%async_computation | async-start | bytes 917504 | tf_op jit(solution)/shard_map/all_to_all | solution.py:84
  37.0 4.5 %collective-permute-start = (bf16[1,8,28,8,128]{4,3,2,1,0:T(8,128)(2,1)S(1)}, bf16[1,8,28,8,128]{4,3,2,1,0:T(8,128)(2,1)S(1)}, u32[]{:S(2)}, u32[]{:S(2)}) collective-permute-start(bf16[1,8,28,8,128]{4,3,2,1,0:T(8,128)(2,1)S(1)} %fusion), channel_id=1, source_target_pairs={{0,1},{1,0},{2,3},{3,2},{4,5},{5,4},{6,7},{7,6},{8,9},{9,8},{10,11... | collective-permute-start | bytes 1376264 | tf_op jit(solution)/shard_map/ppermute | solution.py:23
  40.1 12.1 %collective-permute-start.1 = (bf16[1,8,28,8,128]{4,3,2,1,0:T(8,128)(2,1)S(1)}, bf16[1,8,28,8,128]{4,3,2,1,0:T(8,128)(2,1)S(1)}, u32[]{:S(2)}, u32[]{:S(2)}) collective-permute-start(bf16[1,8,28,8,128]{4,3,2,1,0:T(8,128)(2,1)S(1)} %fusion), channel_id=1, source_target_pairs={{0,16},{1,17},{2,18},{3,19},{4,20},{5,21},{6,22},{7,23},{8,24},{9,... | collective-permute-start | bytes 1376264 | tf_op jit(solution)/shard_map/ppermute | solution.py:23
  41.6 16.1 %collective-permute-start.2 = (bf16[2,8,28,8,128]{4,3,2,1,0:T(8,128)(2,1)S(1)}, bf16[2,8,28,8,128]{4,3,2,1,0:T(8,128)(2,1)S(1)}, u32[]{:S(2)}, u32[]{:S(2)}) collective-permute-start(bf16[2,8,28,8,128]{4,3,2,1,0:T(8,128)(2,1)S(1)} %get-tuple-element.46.refs_0_), channel_id=1, source_target_pairs={{0,2},{1,15},{2,4},{3,1},{4,6},{5,3},{6,8},{7,5},{8,10},{9,7},{10,... | collective-permute-start | bytes 2752520 | tf_op jit(solution)/shard_map/ppermute | solution.py:23
  52.2 11.0 %collective-permute-start.3 = (bf16[1,8,28,8,128]{4,3,2,1,0:T(8,128)(2,1)S(1)}, bf16[1,8,28,8,128]{4,3,2,1,0:T(8,128)(2,1)S(1)}, u32[]{:S(2)}, u32[]{:S(2)}) collective-permute-start(bf16[1,8,28,8,128]{4,3,2,1,0:T(8,128)(2,1)S(1)} %get-tuple-element.48.refs_1_), channel_id=1, source_target_pairs={{0,2},{1,15},{2,4},{3,1},{4,6},{5,3},{6,8},{7,5},{8,10},{9,7},{10,... | collective-permute-start | bytes 1376264 | tf_op jit(solution)/shard_map/ppermute | solution.py:23
  57.7 15.8 %collective-permute-start.4 = (bf16[2,8,28,8,128]{4,3,2,1,0:T(8,128)(2,1)S(1)}, bf16[2,8,28,8,128]{4,3,2,1,0:T(8,128)(2,1)S(1)}, u32[]{:S(2)}, u32[]{:S(2)}) collective-permute-start(bf16[2,8,28,8,128]{4,3,2,1,0:T(8,128)(2,1)S(1)} %get-tuple-element.50.refs_0_), channel_id=1, source_target_pairs={{0,2},{1,15},{2,4},{3,1},{4,6},{5,3},{6,8},{7,5},{8,10},{9,7},{10,... | collective-permute-start | bytes 2752520 | tf_op jit(solution)/shard_map/ppermute | solution.py:23
  60.7 12.8 %collective-permute-start.5 = (bf16[2,8,28,8,128]{4,3,2,1,0:T(8,128)(2,1)S(1)}, bf16[2,8,28,8,128]{4,3,2,1,0:T(8,128)(2,1)S(1)}, u32[]{:S(2)}, u32[]{:S(2)}) collective-permute-start(bf16[2,8,28,8,128]{4,3,2,1,0:T(8,128)(2,1)S(1)} %get-tuple-element.50.refs_0_), channel_id=1, source_target_pairs={{0,1},{1,0},{2,3},{3,2},{4,5},{5,4},{6,7},{7,6},{8,9},{9,8},{10,11... | collective-permute-start | bytes 2752520 | tf_op jit(solution)/shard_map/ppermute | solution.py:23
  61.9 11.7 %collective-permute-start.6 = (bf16[1,8,28,8,128]{4,3,2,1,0:T(8,128)(2,1)S(1)}, bf16[1,8,28,8,128]{4,3,2,1,0:T(8,128)(2,1)S(1)}, u32[]{:S(2)}, u32[]{:S(2)}) collective-permute-start(bf16[1,8,28,8,128]{4,3,2,1,0:T(8,128)(2,1)S(1)} %slice.12), channel_id=1, source_target_pairs={{0,16},{1,17},{2,18},{3,19},{4,20},{5,21},{6,22},{7,23},{8,24},{9,... | collective-permute-start | bytes 1376264 | tf_op jit(solution)/shard_map/ppermute | solution.py:23
  63.2 14.7 %collective-permute-start.7 = (bf16[1,8,28,8,128]{4,3,2,1,0:T(8,128)(2,1)S(1)}, bf16[1,8,28,8,128]{4,3,2,1,0:T(8,128)(2,1)S(1)}, u32[]{:S(2)}, u32[]{:S(2)}) collective-permute-start(bf16[1,8,28,8,128]{4,3,2,1,0:T(8,128)(2,1)S(1)} %get-tuple-element.53.refs_0_), channel_id=1, source_target_pairs={{0,2},{1,15},{2,4},{3,1},{4,6},{5,3},{6,8},{7,5},{8,10},{9,7},{10,... | collective-permute-start | bytes 1376264 | tf_op jit(solution)/shard_map/ppermute | solution.py:23
  66.4 13.7 %collective-permute-start.8 = (bf16[2,8,28,8,128]{4,3,2,1,0:T(8,128)(2,1)S(1)}, bf16[2,8,28,8,128]{4,3,2,1,0:T(8,128)(2,1)S(1)}, u32[]{:S(2)}, u32[]{:S(2)}) collective-permute-start(bf16[2,8,28,8,128]{4,3,2,1,0:T(8,128)(2,1)S(1)} %pad_maximum_fusion.1), channel_id=1, source_target_pairs={{0,1},{1,0},{2,3},{3,2},{4,5},{5,4},{6,7},{7,6},{8,9},{9,8},{10,11... | collective-permute-start | bytes 2752520 | tf_op jit(solution)/shard_map/ppermute | solution.py:23
  73.6 15.6 %collective-permute-start.9 = (bf16[2,8,28,8,128]{4,3,2,1,0:T(8,128)(2,1)S(1)}, bf16[2,8,28,8,128]{4,3,2,1,0:T(8,128)(2,1)S(1)}, u32[]{:S(2)}, u32[]{:S(2)}) collective-permute-start(bf16[2,8,28,8,128]{4,3,2,1,0:T(8,128)(2,1)S(1)} %get-tuple-element.56.refs_0_), channel_id=1, source_target_pairs={{0,2},{1,15},{2,4},{3,1},{4,6},{5,3},{6,8},{7,5},{8,10},{9,7},{10,... | collective-permute-start | bytes 2752520 | tf_op jit(solution)/shard_map/ppermute | solution.py:23
  76.1 13.1 %collective-permute-start.10 = (bf16[2,8,28,8,128]{4,3,2,1,0:T(8,128)(2,1)S(1)}, bf16[2,8,28,8,128]{4,3,2,1,0:T(8,128)(2,1)S(1)}, u32[]{:S(2)}, u32[]{:S(2)}) collective-permute-start(bf16[2,8,28,8,128]{4,3,2,1,0:T(8,128)(2,1)S(1)} %get-tuple-element.56.refs_0_), channel_id=1, source_target_pairs={{0,1},{1,0},{2,3},{3,2},{4,5},{5,4},{6,7},{7,6},{8,9},{9,8},{10,11... | collective-permute-start | bytes 2752520 | tf_op jit(solution)/shard_map/ppermute | solution.py:23
  76.2 11.7 %collective-permute-start.11 = (bf16[1,8,28,8,128]{4,3,2,1,0:T(8,128)(2,1)S(1)}, bf16[1,8,28,8,128]{4,3,2,1,0:T(8,128)(2,1)S(1)}, u32[]{:S(2)}, u32[]{:S(2)}) collective-permute-start(bf16[1,8,28,8,128]{4,3,2,1,0:T(8,128)(2,1)S(1)} %slice.13), channel_id=1, source_target_pairs={{0,16},{1,17},{2,18},{3,19},{4,20},{5,21},{6,22},{7,23},{8,24},{9,... | collective-permute-start | bytes 1376264 | tf_op jit(solution)/shard_map/ppermute | solution.py:23
  77.9 13.9 %collective-permute-start.12 = (bf16[1,8,28,8,128]{4,3,2,1,0:T(8,128)(2,1)S(1)}, bf16[1,8,28,8,128]{4,3,2,1,0:T(8,128)(2,1)S(1)}, u32[]{:S(2)}, u32[]{:S(2)}) collective-permute-start(bf16[1,8,28,8,128]{4,3,2,1,0:T(8,128)(2,1)S(1)} %get-tuple-element.58.refs_2_), channel_id=1, source_target_pairs={{0,1},{1,0},{2,3},{3,2},{4,5},{5,4},{6,7},{7,6},{8,9},{9,8},{10,11... | collective-permute-start | bytes 1376264 | tf_op jit(solution)/shard_map/ppermute | solution.py:23
  80.1 13.4 %collective-permute-start.13 = (bf16[1,8,28,8,128]{4,3,2,1,0:T(8,128)(2,1)S(1)}, bf16[1,8,28,8,128]{4,3,2,1,0:T(8,128)(2,1)S(1)}, u32[]{:S(2)}, u32[]{:S(2)}) collective-permute-start(bf16[1,8,28,8,128]{4,3,2,1,0:T(8,128)(2,1)S(1)} %get-tuple-element.61.refs_0_), channel_id=1, source_target_pairs={{0,2},{1,15},{2,4},{3,1},{4,6},{5,3},{6,8},{7,5},{8,10},{9,7},{10,... | collective-permute-start | bytes 1376264 | tf_op jit(solution)/shard_map/ppermute | solution.py:23
  87.8 7.0 %collective-permute-start.14 = (bf16[1,8,28,8,128]{4,3,2,1,0:T(8,128)(2,1)S(1)}, bf16[1,8,28,8,128]{4,3,2,1,0:T(8,128)(2,1)S(1)}, u32[]{:S(2)}, u32[]{:S(2)}) collective-permute-start(bf16[1,8,28,8,128]{4,3,2,1,0:T(8,128)(2,1)S(1)} %get-tuple-element.61.refs_0_), channel_id=1, source_target_pairs={{0,1},{1,0},{2,3},{3,2},{4,5},{5,4},{6,7},{7,6},{8,9},{9,8},{10,11... | collective-permute-start | bytes 1376264 | tf_op jit(solution)/shard_map/ppermute | solution.py:23
  89.2 14.2 %collective-permute-start.16 = (bf16[2,8,28,8,128]{4,3,2,1,0:T(8,128)(2,1)S(1)}, bf16[2,8,28,8,128]{4,3,2,1,0:T(8,128)(2,1)S(1)}, u32[]{:S(2)}, u32[]{:S(2)}) collective-permute-start(bf16[2,8,28,8,128]{4,3,2,1,0:T(8,128)(2,1)S(1)} %get-tuple-element.65.refs_0_), channel_id=1, source_target_pairs={{0,1},{1,0},{2,3},{3,2},{4,5},{5,4},{6,7},{7,6},{8,9},{9,8},{10,11... | collective-permute-start | bytes 2752520 | tf_op jit(solution)/shard_map/ppermute | solution.py:23
  90.0 8.0 %collective-permute-start.15 = (bf16[1,8,28,8,128]{4,3,2,1,0:T(8,128)(2,1)S(1)}, bf16[1,8,28,8,128]{4,3,2,1,0:T(8,128)(2,1)S(1)}, u32[]{:S(2)}, u32[]{:S(2)}) collective-permute-start(bf16[1,8,28,8,128]{4,3,2,1,0:T(8,128)(2,1)S(1)} %get-tuple-element.82), channel_id=1, source_target_pairs={{0,2},{1,15},{2,4},{3,1},{4,6},{5,3},{6,8},{7,5},{8,10},{9,7},{10,... | collective-permute-start | bytes 1376264 | tf_op jit(solution)/shard_map/ppermute | solution.py:23
  91.8 11.6 %collective-permute-start.17 = (bf16[1,8,28,8,128]{4,3,2,1,0:T(8,128)(2,1)S(1)}, bf16[1,8,28,8,128]{4,3,2,1,0:T(8,128)(2,1)S(1)}, u32[]{:S(2)}, u32[]{:S(2)}) collective-permute-start(bf16[1,8,28,8,128]{4,3,2,1,0:T(8,128)(2,1)S(1)} %get-tuple-element.81), channel_id=1, source_target_pairs={{0,16},{1,17},{2,18},{3,19},{4,20},{5,21},{6,22},{7,23},{8,24},{9,... | collective-permute-start | bytes 1376264 | tf_op jit(solution)/shard_map/ppermute | solution.py:23
  93.5 10.4 %collective-permute-start.18 = (bf16[1,8,28,8,128]{4,3,2,1,0:T(8,128)(2,1)S(1)}, bf16[1,8,28,8,128]{4,3,2,1,0:T(8,128)(2,1)S(1)}, u32[]{:S(2)}, u32[]{:S(2)}) collective-permute-start(bf16[1,8,28,8,128]{4,3,2,1,0:T(8,128)(2,1)S(1)} %get-tuple-element.67.refs_2_), channel_id=1, source_target_pairs={{0,1},{1,0},{2,3},{3,2},{4,5},{5,4},{6,7},{7,6},{8,9},{9,8},{10,11... | collective-permute-start | bytes 1376264 | tf_op jit(solution)/shard_map/ppermute | solution.py:23
  94.8 10.8 %collective-permute-start.19 = (bf16[1,8,28,8,128]{4,3,2,1,0:T(8,128)(2,1)S(1)}, bf16[1,8,28,8,128]{4,3,2,1,0:T(8,128)(2,1)S(1)}, u32[]{:S(2)}, u32[]{:S(2)}) collective-permute-start(bf16[1,8,28,8,128]{4,3,2,1,0:T(8,128)(2,1)S(1)} %get-tuple-element.70.refs_0_), channel_id=1, source_target_pairs={{0,2},{1,15},{2,4},{3,1},{4,6},{5,3},{6,8},{7,5},{8,10},{9,7},{10,... | collective-permute-start | bytes 1376264 | tf_op jit(solution)/shard_map/ppermute | solution.py:23
  98.0 7.6 %collective-permute-start.20 = (bf16[1,8,28,8,128]{4,3,2,1,0:T(8,128)(2,1)S(1)}, bf16[1,8,28,8,128]{4,3,2,1,0:T(8,128)(2,1)S(1)}, u32[]{:S(2)}, u32[]{:S(2)}) collective-permute-start(bf16[1,8,28,8,128]{4,3,2,1,0:T(8,128)(2,1)S(1)} %get-tuple-element.70.refs_0_), channel_id=1, source_target_pairs={{0,1},{1,0},{2,3},{3,2},{4,5},{5,4},{6,7},{7,6},{8,9},{9,8},{10,11... | collective-permute-start | bytes 1376264 | tf_op jit(solution)/shard_map/ppermute | solution.py:23
  103.4 2.5 %collective-permute-start.22 = (bf16[1,8,28,8,128]{4,3,2,1,0:T(8,128)(2,1)S(1)}, bf16[1,8,28,8,128]{4,3,2,1,0:T(8,128)(2,1)S(1)}, u32[]{:S(2)}, u32[]{:S(2)}) collective-permute-start(bf16[1,8,28,8,128]{4,3,2,1,0:T(8,128)(2,1)S(1)} %get-tuple-element.72.refs_3_), channel_id=1, source_target_pairs={{0,1},{1,0},{2,3},{3,2},{4,5},{5,4},{6,7},{7,6},{8,9},{9,8},{10,11... | collective-permute-start | bytes 1376264 | tf_op jit(solution)/shard_map/ppermute | solution.py:23
  103.4 2.5 %collective-permute-start.23 = (bf16[1,8,28,8,128]{4,3,2,1,0:T(8,128)(2,1)S(1)}, bf16[1,8,28,8,128]{4,3,2,1,0:T(8,128)(2,1)S(1)}, u32[]{:S(2)}, u32[]{:S(2)}) collective-permute-start(bf16[1,8,28,8,128]{4,3,2,1,0:T(8,128)(2,1)S(1)} %get-tuple-element.74.refs_5_), channel_id=1, source_target_pairs={{0,1},{1,0},{2,3},{3,2},{4,5},{5,4},{6,7},{7,6},{8,9},{9,8},{10,11... | collective-permute-start | bytes 1376264 | tf_op jit(solution)/shard_map/ppermute | solution.py:23
  105.7 1.9 %collective-permute-start.21 = (bf16[1,8,28,8,128]{4,3,2,1,0:T(8,128)(2,1)S(1)}, bf16[1,8,28,8,128]{4,3,2,1,0:T(8,128)(2,1)S(1)}, u32[]{:S(2)}, u32[]{:S(2)}) collective-permute-start(bf16[1,8,28,8,128]{4,3,2,1,0:T(8,128)(2,1)S(1)} %get-tuple-element.76.refs_3_), channel_id=1, source_target_pairs={{0,1},{1,0},{2,3},{3,2},{4,5},{5,4},{6,7},{7,6},{8,9},{9,8},{10,11... | collective-permute-start | bytes 1376264 | tf_op jit(solution)/shard_map/ppermute | solution.py:23
